TPU v7x, 32 devices: a whole 2x2x4 slice. The times are simulated.
32 devices in a mesh: seq: 4 (over y, x), chan: 8 (over z, core).
Axes of the slice: x: 2, y: 2, z: 4, core: 2. Of those that a mesh axis runs over, the one named last changes fastest.
Arguments:
- residual: bfloat16 [16384, 2048], P(('seq', 'chan')), may hold values from -6 to 6
- cotangent: bfloat16 [16384, 2048], P(('seq', 'chan')), may hold values from -6 to 6
- resets: int32 [16384], P('seq'), may hold values 0 or 1
- branch_weights: bfloat16 [2048, 2, 2560], P(None, None, 'chan'), may hold values from -0.125 to 0.125
- gate_blocks: bfloat16 [2, 16, 160, 160], P(None, 'chan'), may hold values from -0.5 to 0.5
- mixer_weights: bfloat16 [2560, 2048], P('chan'), may hold values from -0.3125 to 0.3125
- expand_weights: bfloat16 [2048, 2, 6144], P(None, None, 'chan'), may hold values from -0.125 to 0.125
- shrink_weights: bfloat16 [6144, 2048], P('chan'), may hold values from -0.109375 to 0.109375
- branch_state: float32 [4, 2048, 2, 2560], P(None, 'seq', None, 'chan'), as said below
- gate_state: float32 [4, 2, 16, 160, 160], P(None, None, 'chan', 'seq'), as said below
- mixer_state: float32 [4, 2560, 2048], P(None, 'chan', 'seq'), as said below
- expand_state: float32 [4, 2048, 2, 6144], P(None, 'seq', None, 'chan'), as said below
- shrink_state: float32 [4, 6144, 2048], P(None, 'chan', 'seq'), as said below
- channel_state: float32 [4, 8, 2560], P(None, None, 'chan'), as said below
- gains_state: float32 [4, 2, 2048], replicated, as said below
Outputs:
- output: bfloat16 [16384, 2048], P(('seq', 'chan'))
- residual_grad: float32 [16384, 2048], P(('seq', 'chan'))
- branch_grad: float32 [2048, 2, 2560], P('seq', None, 'chan')
- gate_grad: float32 [2, 16, 160, 160], P(None, 'chan', 'seq')
- mixer_grad: float32 [2560, 2048], P('chan', 'seq')
- expand_grad: float32 [2048, 2, 6144], P('seq', None, 'chan')
- shrink_grad: float32 [6144, 2048], P('chan', 'seq')
- channel_grad: float32 [8, 2560], P(None, 'chan')
- gains_grad: float32 [2, 2048], replicated
- grad_norm: float32 [], replicated
- branch_new: float32 [4, 2048, 2, 2560], P(None, 'seq', None, 'chan')
- gate_new: float32 [4, 2, 16, 160, 160], P(None, None, 'chan', 'seq')
- mixer_new: float32 [4, 2560, 2048], P(None, 'chan', 'seq')
- expand_new: float32 [4, 2048, 2, 6144], P(None, 'seq', None, 'chan')
- shrink_new: float32 [4, 6144, 2048], P(None, 'chan', 'seq')
- channel_new: float32 [2, 8, 2560], P(None, None, 'chan')
- channel_moments: float32 [2, 8, 2560], P(None, None, 'chan')
- gains_new: float32 [4, 2, 2048], replicated
- branch_copy: bfloat16 [2048, 2, 2560], P('seq', None, 'chan')
- gate_copy: bfloat16 [2, 16, 160, 160], P(None, 'chan', 'seq')
- mixer_copy: bfloat16 [2560, 2048], P('chan', 'seq')
- expand_copy: bfloat16 [2048, 2, 6144], P('seq', None, 'chan')
- shrink_copy: bfloat16 [6144, 2048], P('chan', 'seq')
Inputs may be any that keep to these rules, and one draw needn't show every extreme that they name: `branch_state`: index 0 holds master weights, 1 first moments, 2 second moments (positive), 3 the weight average. `gate_state`: index 0 holds master weights, 1 first moments, 2 second moments (positive), 3 the weight average. `mixer_state`: index 0 holds master weights, 1 first moments, 2 second moments (positive), 3 the weight average. `expand_state`: index 0 holds master weights, 1 first moments, 2 second moments (positive), 3 the weight average. `shrink_state`: index 0 holds master weights, 1 first moments, 2 second moments (positive), 3 the weight average. `channel_state`: index 0 holds master values, 1 first moments, 2 second moments (positive), 3 the average; the decay parameter row is negative. `gains_state`: index 0 holds the gains' offsets from 1, 1 first moments, 2 second moments (positive), 3 the average.
All inputs are finite; a program needn't handle non-finite values. No bound on the sum of `resets` on one device may be relied on, other than what follows from the above.
Results may differ from a plain program's by a relative error of at most 0.02.
Values may be sent and summed in bfloat16 or wider, within the bound.
No kernel may reach another device: no remote copies, remote signals or barrier semaphores. Data moves between devices by JAX's collectives and lax.ppermute only.
A program may use at most 384 MiB of HBM per device.

v0:
```python
import math

import jax
import jax.numpy as jnp
from jax import lax
from jax.sharding import PartitionSpec as P

CONV = 4
SEQ_LEN = 2048
SEQS = 2
STEP = 10
PARAMS = 54321152


norm_eps = 1e-06
lru_scale = 8.0
clip_rms = 0.4
beta_one = 0.9
beta_two = 0.95
adam_eps = 1e-08
weight_decay = 0.1
ema_keep = 0.99
rate_matrix = 0.02
rate_gate = 0.1
rate_channel = 1.0
rate_gains = 0.5


def combine(earlier, latter):
    return (earlier[0] * latter[0], latter[0] * earlier[1] + latter[1])


def shifted(values, offset):
    if offset == 0:
        return values
    length = values.shape[1]
    return jnp.pad(values, ((0, 0), (offset, 0), (0, 0)))[:, :length, :]


def shifted_back(values, offset):
    if offset == 0:
        return values
    length = values.shape[1]
    return jnp.pad(values, ((0, 0), (0, offset), (0, 0)))[:, offset : offset + length, :]


def contract_rows(left_mat, right_mat):
    return lax.dot_general(
        left_mat, right_mat, (((0,), (0,)), ((), ())), preferred_element_type=jnp.float32
    )


def contract_cols(left_mat, right_mat):
    return lax.dot_general(
        left_mat, right_mat, (((1,), (1,)), ((), ())), preferred_element_type=jnp.float32
    )


def norm_back(values, scale, gain, upstream):
    scaled = gain * upstream
    return scale * scaled - values * scale * scale * scale * jnp.mean(
        scaled * values, axis=-1, keepdims=True
    )


def adam(old_state, gradient, factor, step_rate, decay_use):
    clipped = gradient * factor
    moment_one = beta_one * old_state[1] + (1.0 - beta_one) * clipped
    moment_two = beta_two * old_state[2] + (1.0 - beta_two) * clipped * clipped
    first_hat = moment_one / (1.0 - beta_one**STEP)
    second_hat = moment_two / (1.0 - beta_two**STEP)
    master = old_state[0] - step_rate * (
        first_hat / (jnp.sqrt(second_hat) + adam_eps) + decay_use * old_state[0]
    )
    average = ema_keep * old_state[3] + (1.0 - ema_keep) * master
    return (jnp.stack([master, moment_one, moment_two, average]), master)


def local(
    residual,
    cotangent,
    resets,
    branch_weights,
    gate_blocks,
    mixer_weights,
    expand_weights,
    shrink_weights,
    branch_state,
    gate_state,
    mixer_state,
    expand_state,
    shrink_state,
    channel_state,
    gains_state,
):
    width = residual.shape[1]
    chan_width = branch_weights.shape[2]
    hidden_width = expand_weights.shape[2]
    block_count = gate_blocks.shape[1]
    block_size = gate_blocks.shape[2]
    group_rows = SEQS * SEQ_LEN
    gains = gains_state[0]
    gain_first = 1.0 + gains[0]
    gain_second = 1.0 + gains[1]
    channel = channel_state[0]
    branch_flat = branch_weights.reshape(width, 2 * chan_width)
    expand_flat = expand_weights.reshape(width, 2 * hidden_width)
    rows_float = residual.astype(jnp.float32)
    scale_one = lax.rsqrt(jnp.mean(rows_float * rows_float, axis=-1, keepdims=True) + norm_eps)
    normed_one = (rows_float * scale_one * gain_first).astype(jnp.bfloat16)
    normed_all = lax.all_gather(normed_one, "chan", axis=0, tiled=True)
    projected = jnp.dot(normed_all, branch_flat, preferred_element_type=jnp.float32)
    flag_block = resets.reshape(SEQS, SEQ_LEN)
    step_index = lax.broadcasted_iota(jnp.int32, flag_block.shape, 1)
    starting = jnp.logical_or(flag_block == 1, step_index == 0)
    latest = lax.cummax(jnp.where(starting, step_index, 0), axis=1)
    inside = step_index - latest
    retain_mask = (1.0 - starting.astype(jnp.float32))[:, :, None]
    valid_masks = [(inside >= offset).astype(jnp.float32)[:, :, None] for offset in range(CONV)]
    gate_branch = projected[:, :chan_width]
    recur_input = projected[:, chan_width:].reshape(SEQS, SEQ_LEN, chan_width)
    tap_inputs = [shifted(recur_input, offset) * valid_masks[offset] for offset in range(CONV)]
    convolved = channel[CONV] + sum(
        (channel[offset] * tap_inputs[offset] for offset in range(CONV))
    )
    conv_low = convolved.astype(jnp.bfloat16)
    conv_float = conv_low.astype(jnp.float32)
    blocked = conv_low.reshape(group_rows, block_count, block_size)
    gate_pre = (
        jnp.einsum(
            "rhi,hij->rhj", blocked, gate_blocks[0], preferred_element_type=jnp.float32
        ).reshape(SEQS, SEQ_LEN, chan_width)
        + channel[CONV + 1]
    )
    input_pre = (
        jnp.einsum(
            "rhi,hij->rhj", blocked, gate_blocks[1], preferred_element_type=jnp.float32
        ).reshape(SEQS, SEQ_LEN, chan_width)
        + channel[CONV + 2]
    )
    recur_gate = jax.nn.sigmoid(gate_pre)
    input_gate = jax.nn.sigmoid(input_pre)
    softened = jax.nn.softplus(channel[CONV + 3])
    log_decay = -lru_scale * softened * recur_gate
    decay_rate = jnp.exp(log_decay)
    norm_term = jnp.sqrt(-jnp.expm1(2.0 * log_decay))
    coeff_term = decay_rate * retain_mask
    drive_term = norm_term * input_gate * conv_float
    hidden = lax.associative_scan(combine, (coeff_term, drive_term), axis=1)[1]
    gate_act, gate_pull = jax.vjp(jax.nn.gelu, gate_branch)
    gate_shaped = gate_act.reshape(SEQS, SEQ_LEN, chan_width)
    mixed = (gate_shaped * hidden).reshape(group_rows, chan_width).astype(jnp.bfloat16)
    middle = rows_float + lax.psum_scatter(
        jnp.dot(mixed, mixer_weights, preferred_element_type=jnp.float32),
        "chan",
        scatter_dimension=0,
        tiled=True,
    )
    scale_two = lax.rsqrt(jnp.mean(middle * middle, axis=-1, keepdims=True) + norm_eps)
    normed_two = (middle * scale_two * gain_second).astype(jnp.bfloat16)
    normed_mlp = lax.all_gather(normed_two, "chan", axis=0, tiled=True)
    expanded = jnp.dot(normed_mlp, expand_flat, preferred_element_type=jnp.float32)
    gate_part = expanded[:, :hidden_width]
    up_part = expanded[:, hidden_width:]
    act_part, act_pull = jax.vjp(jax.nn.gelu, gate_part)
    product_low = (act_part * up_part).astype(jnp.bfloat16)
    output = (
        middle
        + lax.psum_scatter(
            jnp.dot(product_low, shrink_weights, preferred_element_type=jnp.float32).astype(
                jnp.bfloat16
            ),
            "chan",
            scatter_dimension=0,
            tiled=True,
        ).astype(jnp.float32)
    ).astype(jnp.bfloat16)
    back_float = cotangent.astype(jnp.float32)
    back_all = lax.all_gather(cotangent, "chan", axis=0, tiled=True)
    product_grad = contract_cols(back_all, shrink_weights)
    shrink_local = contract_rows(product_low, back_all)
    gate_grad_low = act_pull(product_grad * up_part)[0].astype(jnp.bfloat16)
    up_grad_low = (product_grad * act_part).astype(jnp.bfloat16)
    expand_back = jnp.concatenate([gate_grad_low, up_grad_low], axis=1)
    normed_two_grad = lax.psum_scatter(
        contract_cols(expand_back, expand_flat).astype(jnp.bfloat16),
        "chan",
        scatter_dimension=0,
        tiled=True,
    ).astype(jnp.float32)
    expand_local = contract_rows(normed_mlp, expand_back)
    gain_two = jnp.sum(normed_two_grad * middle * scale_two, axis=0)
    middle_grad = back_float + norm_back(middle, scale_two, gain_second, normed_two_grad)
    branch_back = lax.all_gather(middle_grad.astype(jnp.bfloat16), "chan", axis=0, tiled=True)
    mixer_local = contract_rows(mixed, branch_back)
    mixed_grad = contract_cols(branch_back, mixer_weights).reshape(SEQS, SEQ_LEN, chan_width)
    hidden_grad = mixed_grad * gate_shaped
    gate_branch_low = gate_pull((mixed_grad * hidden).reshape(group_rows, chan_width))[0].astype(
        jnp.bfloat16
    )
    coeff_next = shifted_back(coeff_term, 1)
    carried = lax.associative_scan(combine, (coeff_next, hidden_grad), reverse=True, axis=1)[1]
    hidden_prev = shifted(hidden, 1)
    log_grad = (
        carried * hidden_prev * coeff_term
        - carried * input_gate * conv_float * decay_rate * decay_rate / norm_term
    )
    recur_pre_low = (log_grad * (-lru_scale * softened) * recur_gate * (1.0 - recur_gate)).astype(
        jnp.bfloat16
    )
    input_pre_low = (carried * norm_term * conv_float * input_gate * (1.0 - input_gate)).astype(
        jnp.bfloat16
    )
    recur_flat = recur_pre_low.reshape(group_rows, block_count, block_size)
    input_flat = input_pre_low.reshape(group_rows, block_count, block_size)
    block_back = jnp.einsum(
        "rhj,hij->rhi", recur_flat, gate_blocks[0], preferred_element_type=jnp.float32
    ) + jnp.einsum("rhj,hij->rhi", input_flat, gate_blocks[1], preferred_element_type=jnp.float32)
    conv_grad = carried * norm_term * input_gate + block_back.reshape(SEQS, SEQ_LEN, chan_width)
    gate_local = jnp.stack(
        [
            jnp.einsum("rhi,rhj->hij", blocked, recur_flat, preferred_element_type=jnp.float32),
            jnp.einsum("rhi,rhj->hij", blocked, input_flat, preferred_element_type=jnp.float32),
        ]
    )
    tap_grads = [jnp.sum(conv_grad * tap_inputs[offset], axis=(0, 1)) for offset in range(CONV)]
    recur_grad = sum(
        (
            shifted_back(channel[offset] * conv_grad * valid_masks[offset], offset)
            for offset in range(CONV)
        )
    )
    lru_grad = (
        jnp.sum(log_grad * recur_gate, axis=(0, 1)) * -lru_scale * jax.nn.sigmoid(channel[CONV + 3])
    )
    channel_local = jnp.stack(
        tap_grads
        + [
            jnp.sum(conv_grad, axis=(0, 1)),
            jnp.sum(recur_pre_low, axis=(0, 1), dtype=jnp.float32),
            jnp.sum(input_pre_low, axis=(0, 1), dtype=jnp.float32),
            lru_grad,
        ]
    )
    branch_back_low = jnp.concatenate(
        [gate_branch_low, recur_grad.reshape(group_rows, chan_width).astype(jnp.bfloat16)], axis=1
    )
    normed_one_grad = lax.psum_scatter(
        contract_cols(branch_back_low, branch_flat).astype(jnp.bfloat16),
        "chan",
        scatter_dimension=0,
        tiled=True,
    ).astype(jnp.float32)
    branch_local = contract_rows(normed_all, branch_back_low)
    gain_one = jnp.sum(normed_one_grad * rows_float * scale_one, axis=0)
    residual_grad = middle_grad + norm_back(rows_float, scale_one, gain_first, normed_one_grad)
    gains_local = jnp.stack([gain_one, gain_two])
    gains_grad = lax.psum(gains_local, ("seq", "chan"))
    channel_grad = lax.psum(channel_local, "seq")
    grad_shards = (
        lax.psum_scatter(
            branch_local.reshape(width, 2, chan_width).astype(jnp.bfloat16),
            "seq",
            scatter_dimension=0,
            tiled=True,
        ).astype(jnp.float32),
        lax.psum_scatter(
            gate_local.astype(jnp.bfloat16), "seq", scatter_dimension=2, tiled=True
        ).astype(jnp.float32),
        lax.psum_scatter(
            mixer_local.astype(jnp.bfloat16), "seq", scatter_dimension=1, tiled=True
        ).astype(jnp.float32),
        lax.psum_scatter(
            expand_local.reshape(width, 2, hidden_width).astype(jnp.bfloat16),
            "seq",
            scatter_dimension=0,
            tiled=True,
        ).astype(jnp.float32),
        lax.psum_scatter(
            shrink_local.astype(jnp.bfloat16), "seq", scatter_dimension=1, tiled=True
        ).astype(jnp.float32),
    )
    branch_grad, gate_grad, mixer_grad, expand_grad, shrink_grad = grad_shards
    own_squares = sum((jnp.sum(shard_grad * shard_grad) for shard_grad in grad_shards))
    own_squares = own_squares + jnp.where(
        lax.axis_index("seq") == 0, jnp.sum(channel_grad * channel_grad), 0.0
    )
    total_squares = lax.psum(own_squares, ("seq", "chan"))
    grad_norm = jnp.sqrt(total_squares + jnp.sum(gains_grad * gains_grad))
    clip_limit = clip_rms * math.sqrt(PARAMS)
    factor = jnp.minimum(1.0, clip_limit / (grad_norm + 1e-06))
    branch_new, branch_master = adam(branch_state, branch_grad, factor, rate_matrix, weight_decay)
    gate_new, gate_master = adam(gate_state, gate_grad, factor, rate_gate, weight_decay)
    mixer_new, mixer_master = adam(mixer_state, mixer_grad, factor, rate_matrix, weight_decay)
    expand_new, expand_master = adam(expand_state, expand_grad, factor, rate_matrix, weight_decay)
    shrink_new, shrink_master = adam(shrink_state, shrink_grad, factor, rate_matrix, weight_decay)
    channel_full, channel_master = adam(channel_state, channel_grad, factor, rate_channel, 0.0)
    gains_new, gains_master = adam(gains_state, gains_grad, factor, rate_gains, 0.0)
    channel_new = jnp.stack([channel_full[0], channel_full[3]])
    channel_moments = channel_full[1:3]
    return (
        output,
        residual_grad,
        branch_grad,
        gate_grad,
        mixer_grad,
        expand_grad,
        shrink_grad,
        channel_grad,
        gains_grad,
        grad_norm,
        branch_new,
        gate_new,
        mixer_new,
        expand_new,
        shrink_new,
        channel_new,
        channel_moments,
        gains_new,
        branch_master.astype(jnp.bfloat16),
        gate_master.astype(jnp.bfloat16),
        mixer_master.astype(jnp.bfloat16),
        expand_master.astype(jnp.bfloat16),
        shrink_master.astype(jnp.bfloat16),
    )


def solution(mesh):
    in_specs = (
        P(("seq", "chan"), None),
        P(("seq", "chan"), None),
        P("seq"),
        P(None, None, "chan"),
        P(None, "chan", None, None),
        P("chan", None),
        P(None, None, "chan"),
        P("chan", None),
        P(None, "seq", None, "chan"),
        P(None, None, "chan", "seq", None),
        P(None, "chan", "seq"),
        P(None, "seq", None, "chan"),
        P(None, "chan", "seq"),
        P(None, None, "chan"),
        P(),
    )
    out_specs = (
        P(("seq", "chan"), None),
        P(("seq", "chan"), None),
        P("seq", None, "chan"),
        P(None, "chan", "seq", None),
        P("chan", "seq"),
        P("seq", None, "chan"),
        P("chan", "seq"),
        P(None, "chan"),
        P(),
        P(),
        P(None, "seq", None, "chan"),
        P(None, None, "chan", "seq", None),
        P(None, "chan", "seq"),
        P(None, "seq", None, "chan"),
        P(None, "chan", "seq"),
        P(None, None, "chan"),
        P(None, None, "chan"),
        P(),
        P("seq", None, "chan"),
        P(None, "chan", "seq", None),
        P("chan", "seq"),
        P("seq", None, "chan"),
        P("chan", "seq"),
    )
    return jax.shard_map(local, mesh=mesh, in_specs=in_specs, out_specs=out_specs, check_vma=False)
```

profile of v0, /device:TPU:0, one launch (start us, length us, event | category | flops | bytes accessed | tf_op | source)
XLA Modules:
  0.0 2919.9 jit_solution(8702632678125096071)
XLA Ops:
  17.8 151.0 %all-gather.5.cloned.1.call-done = bf16[4096,2048]{1,0:T(8,128)(2,1)} async-done(((bf16[512,2048]{1,0:T(8,128)(2,1)}), bf16[4096,2048]{1,0:T(8,128)(2,1)}) %all-gather.5.cloned.1.call-update) | async-done | bytes 16777232 | tf_op jit(solution)/shard_map/all_gather | solution.py:111
  271.7 24.2 exponential_multiply_fusion
  691.9 323.9 %reduce-scatter.9.cloned.1.call-done = f32[512,2048]{1,0:T(8,128)} async-done(((f32[4096,2048]{1,0:T(8,128)}), f32[512,2048]{1,0:T(8,128)}) %reduce-scatter.9.cloned.1.call-update) | async-done | bytes 4194320 | tf_op jit(solution)/shard_map/reduce_scatter | solution.py:153
  1030.9 141.8 %all-gather.7.cloned.1.call-done = bf16[4096,2048]{1,0:T(8,128)(2,1)} async-done(((bf16[512,2048]{1,0:T(8,128)(2,1)}), bf16[4096,2048]{1,0:T(8,128)(2,1)}) %all-gather.7.cloned.1.call-update) | async-done | bytes 16777232 | tf_op jit(solution)/shard_map/all_gather | solution.py:161
  1172.7 33.8 %fusion.167 = f32[4096,1536]{0,1:T(8,128)} fusion(bf16[4096,2048]{1,0:T(8,128)(2,1)} %all-gather.7.cloned.1.call-done, bf16[2048,1536]{1,0:T(8,128)(2,1)} %bitcast.372), kind=kOutput, calls=%fused_computation.380 | convolution fusion | flops 25769803776 | bytes 48234496 | tf_op jit(solution)/shard_map/dot_general | solution.py:162
  1206.5 117.1 %all-gather.9.cloned.1.call-done = bf16[4096,2048]{1,0:T(8,128)(2,1)} async-done(((bf16[512,2048]{1,0:T(8,128)(2,1)}), bf16[4096,2048]{1,0:T(8,128)(2,1)}) %all-gather.9.cloned.1.call-update) | async-done | bytes 16777232 | tf_op jit(solution)/shard_map/all_gather | solution.py:179
  1323.6 33.5 %fusion.6 = (bf16[4096,768]{0,1:T(8,128)(2,1)}, bf16[4096,768]{0,1:T(8,128)(2,1)}, bf16[4096,768]{0,1:T(8,128)(2,1)}) fusion(f32[4096,1536]{0,1:T(8,128)} %fusion.167, bf16[4096,2048]{1,0:T(8,128)(2,1)} %all-gather.9.cloned.1.call-done, bf16[768,2048]{1,0:T(8,128)(2,1)S(1)} %copy-done), kind=kOutput, calls=%fused_computation.11 | convolution fusion | flops 12966690816 | bytes 63963136 | tf_op jit(solution)/shard_map/dot_general | solution.py:54
  1357.1 32.9 %convolution_convert_fusion.1 = bf16[4096,2048]{1,0:T(8,128)(2,1)} fusion(bf16[2048,1536]{1,0:T(8,128)(2,1)} %bitcast.373, bf16[4096,768]{0,1:T(8,128)(2,1)} %get-tuple-element.80, bf16[4096,768]{0,1:T(8,128)(2,1)} %get-tuple-element.79), kind=kOutput, calls=%fused_computation.3 | convolution fusion | flops 25803358208 | bytes 35651584 | tf_op jit(solution)/shard_map/dot_general | solution.py:54
  1390.1 166.6 %reduce-scatter.13.cloned.1.call-done = bf16[512,2048]{1,0:T(8,128)(2,1)} async-done(((bf16[4096,2048]{1,0:T(8,128)(2,1)}), bf16[512,2048]{1,0:T(8,128)(2,1)}) %reduce-scatter.13.cloned.1.call-update) | async-done | bytes 2097168 | tf_op jit(solution)/shard_map/reduce_scatter | solution.py:185
  1572.9 26.7 slice.835
  1630.2 24.7 slice.836
  1654.9 24.7 slice.843
  1679.6 25.5 slice.834
  1777.1 24.6 slice.838
  1801.7 24.7 slice.840
  2092.9 25.6 slice.920
  2145.6 48.4 %rev.2 = f32[2,2048,320]{2,1,0:T(8,128)} reverse(f32[2,2048,320]{2,1,0:T(8,128)} %add.704), dimensions={1} | reverse | bytes 10485760 | tf_op jit(solution)/shard_map/rev | solution.py:202
  2194.2 28.6 convert_reduce_fusion
  2280.9 22.9 multiply_reduce_fusion.1
  2359.5 34.9 %fusion.8 = bf16[2048,1536]{0,1:T(8,128)(2,1)} fusion(bf16[4096,2048]{1,0:T(8,128)(2,1)} %all-gather.7.cloned.1.call-done, bf16[4096,768]{0,1:T(8,128)(2,1)} %get-tuple-element.80, bf16[4096,768]{0,1:T(8,128)(2,1)} %get-tuple-element.79), kind=kOutput, calls=%fused_computation.27 | convolution fusion | flops 25798115328 | bytes 35651584 | tf_op jit(solution)/shard_map/dot_general | solution.py:48
  2484.3 78.0 %all-reduce.58.cloned.1.call-done = (bf16[2,2,160,160]{3,2,1,0:T(8,128)(2,1)}, bf16[2048,2,768]{2,1,0:T(2,128)(2,1)}) async-done(((bf16[2,2,160,160]{3,2,1,0:T(8,128)(2,1)}, bf16[2048,2,768]{2,1,0:T(2,128)(2,1)}), (bf16[2,2,160,160]{3,2,1,0:T(8,128)(2,1)}, bf16[2048,2,768]{2,1,0:T(2,128)(2,1)})) %all-reduce.58.cloned.1.call-update) | async-done | bytes 6496272
  2574.0 159.1 %reduce-scatter.15.cloned.1.call-done = bf16[512,2048]{1,0:T(8,128)(2,1)} async-done(((bf16[4096,2048]{1,0:T(8,128)(2,1)}), bf16[512,2048]{1,0:T(8,128)(2,1)}) %reduce-scatter.15.cloned.1.call-update) | async-done | bytes 2097168 | tf_op jit(solution)/shard_map/reduce_scatter | solution.py:248
  2736.9 40.0 %all-reduce.54 = (f32[2,2048]{1,0:T(2,128)S(1)}, f32[]{:T(128)}) all-reduce(f32[2,2048]{1,0:T(2,128)S(1)} %pad_maximum_fusion.35, f32[]{:T(128)S(6)} %add.717), channel_id=1, replica_groups=mesh['seq'=4,'chan'=8] {'seq','chan'}, use_global_device_ids=true, to_apply=%region_26.27 | all-reduce | flops 4097 | bytes 32776 | tf_op jit(solution)/shard_map/psum | solution.py:258
  2831.6 71.5 %reduce-scatter.11.cloned.1.call-done = bf16[512,2048]{1,0:T(8,128)(2,1)} async-done(((bf16[4096,2048]{1,0:T(8,128)(2,1)}), bf16[512,2048]{1,0:T(8,128)(2,1)}) %reduce-scatter.11.cloned.1.call-update) | async-done | bytes 2097168 | tf_op jit(solution)/shard_map/reduce_scatter | solution.py:169
  (627 shorter events, 1211.4 us)
Async XLA Ops:
  7.2 1316.4 %copy-start = (bf16[768,2048]{1,0:T(8,128)(2,1)S(1)}, bf16[768,2048]{1,0:T(8,128)(2,1)}, u32[]{:S(2)}) copy-start(bf16[768,2048]{1,0:T(8,128)(2,1)} %param.22) | copy-start | bytes 9437188
  7.2 161.6 %all-gather.5.cloned.1.call-start = ((), (), s32[]{:S(2)}) async-start(), calls=%async_computation.7 | async-start | bytes 18874368 | tf_op jit(solution)/shard_map/all_gather | solution.py:111
  14.9 1000.9 %reduce-scatter.9.cloned.1.call-start = ((), (), s32[]{:S(2)}) async-start(), calls=%async_computation.8 | async-start | bytes 37748736 | tf_op jit(solution)/shard_map/reduce_scatter | solution.py:153
  17.7 253.9 %copy-start.42 = (f32[2,2048]{1,0:T(2,128)}, f32[2,2048]{1,0:T(2,128)S(1)}, u32[]{:S(2)}) copy-start(f32[2,2048]{1,0:T(2,128)S(1)} %fusion.109) | copy-start | bytes 49156
  17.8 253.8 %copy-start.27 = (f32[2,2048]{1,0:T(2,128)}, f32[2,2048]{1,0:T(2,128)S(1)}, u32[]{:S(2)}) copy-start(f32[2,2048]{1,0:T(2,128)S(1)} %get-tuple-element.156) | copy-start | bytes 49156
  17.8 253.8 %copy-start.29 = (f32[2,2048]{1,0:T(2,128)}, f32[2,2048]{1,0:T(2,128)S(1)}, u32[]{:S(2)}) copy-start(f32[2,2048]{1,0:T(2,128)S(1)} %get-tuple-element.157) | copy-start | bytes 49156
  17.8 253.8 %copy-start.31 = (f32[2,2048]{1,0:T(2,128)}, f32[2,2048]{1,0:T(2,128)S(1)}, u32[]{:S(2)}) copy-start(f32[2,2048]{1,0:T(2,128)S(1)} %get-tuple-element.158) | copy-start | bytes 49156
  17.8 253.8 %copy-start.33 = (f32[2,2048]{1,0:T(2,128)}, f32[2,2048]{1,0:T(2,128)S(1)}, u32[]{:S(2)}) copy-start(f32[2,2048]{1,0:T(2,128)S(1)} %get-tuple-element.159) | copy-start | bytes 49156
  691.9 329.5 %copy-start.39 = (f32[1,1,2048]{2,1,0:T(1,128)S(1)}, f32[1,1,2048]{2,1,0:T(1,128)}, u32[]{:S(2)}) copy-start(f32[1,1,2048]{2,1,0:T(1,128)} %get-tuple-element.142) | copy-start | bytes 24580
  691.9 480.8 %all-gather.7.cloned.1.call-start = ((), (), s32[]{:S(2)}) async-start(), calls=%async_computation.9 | async-start | bytes 18874368 | tf_op jit(solution)/shard_map/all_gather | solution.py:161
  1023.1 300.5 %all-gather.9.cloned.1.call-start = ((), (), s32[]{:S(2)}) async-start(), calls=%async_computation.11 | async-start | bytes 18874368 | tf_op jit(solution)/shard_map/all_gather | solution.py:179
  1023.7 533.1 %reduce-scatter.13.cloned.1.call-start = ((), (), s32[]{:S(2)}) async-start(), calls=%async_computation.12 | async-start | bytes 18874368 | tf_op jit(solution)/shard_map/reduce_scatter | solution.py:185
  1390.1 334.9 %all-gather.11.cloned.1.call-start = ((), (), s32[]{:S(2)}) async-start(), calls=%async_computation.13 | async-start | bytes 18874368 | tf_op jit(solution)/shard_map/all_gather | solution.py:194
  1566.8 891.1 %reduce-scatter.21.cloned.1.call-start = ((), (), s32[]{:S(2)}) async-start(), calls=%async_computation.17 | async-start | bytes 3932160 | tf_op jit(solution)/shard_map/reduce_scatter | solution.py:279
  1724.9 753.9 %reduce-scatter.19.cloned.1.call-start = ((), (), s32[]{:S(2)}) async-start(), calls=%async_computation.16 | async-start | bytes 1638400 | tf_op jit(solution)/shard_map/reduce_scatter | solution.py:270
  2342.1 139.2 %reduce-scatter.17.cloned.1.call-start = ((), (), s32[]{:S(2)}) async-start(), calls=%async_computation.15 | async-start | bytes 3276800 | tf_op jit(solution)/shard_map/reduce_scatter | solution.py:261
  2359.5 202.9 %all-reduce.58.cloned.1.call-start = ((), (), s32[]{:S(2)}) async-start(), calls=%async_computation.18 | async-start | bytes 13238272
  2416.6 316.5 %reduce-scatter.15.cloned.1.call-start = ((), (), s32[]{:S(2)}) async-start(), calls=%async_computation.14 | async-start | bytes 18874368 | tf_op jit(solution)/shard_map/reduce_scatter | solution.py:248
  2436.4 466.8 %reduce-scatter.11.cloned.1.call-start = ((), (), s32[]{:S(2)}) async-start(), calls=%async_computation.10 | async-start | bytes 18874368 | tf_op jit(solution)/shard_map/reduce_scatter | solution.py:169
  2455.4 277.7 %copy-start.45 = (f32[1,1,2048]{2,1,0:T(1,128)S(1)}, f32[1,1,2048]{2,1,0:T(1,128)}, u32[]{:S(2)}) copy-start(f32[1,1,2048]{2,1,0:T(1,128)} %copy-done.44) | copy-start | bytes 24580
  2455.4 277.7 %copy-start.78 = (f32[512]{0:T(512)S(1)}, f32[512]{0:T(512)}, u32[]{:S(2)}) copy-start(f32[512]{0:T(512)} %copy-done.77) | copy-start | bytes 6148
  2477.5 301.5 %copy-start.46 = (f32[8,320]{1,0:T(8,128)}, f32[8,320]{1,0:T(8,128)S(1)}, u32[]{:S(2)}) copy-start(f32[8,320]{1,0:T(8,128)S(1)} %psum.21) | copy-start | bytes 30724
  2481.3 255.6 %copy-start.85 = (f32[2048]{0:T(1024)S(1)}, f32[2048]{0:T(1024)}, u32[]{:S(2)}) copy-start(f32[2048]{0:T(1024)} %get-tuple-element.26) | copy-start | bytes 24580
  2563.9 217.6 %copy-start.26 = (f32[2,2,40,160]{3,2,1,0:T(8,128)}, f32[2,2,40,160]{3,2,1,0:T(8,128)S(1)}, u32[]{:S(2)}) copy-start(f32[2,2,40,160]{3,2,1,0:T(8,128)S(1)} %get-tuple-element.65) | copy-start | bytes 307204
  (105 other events, 3046.4 us)
Sparse Core Ops, SparseCore 0:
  15.0 153.7 all-gather.4
  692.0 323.7 reduce-scatter.8
  1023.2 149.4 all-gather.6
  1174.2 149.3 all-gather.8
  1390.2 166.4 reduce-scatter.12
  1567.0 149.4 all-gather.10
  1725.0 42.1 reduce-scatter.20
  2342.2 27.5 reduce-scatter.18
  2373.6 39.5 reduce-scatter.16
  2418.1 144.2 all-reduce.57
  2564.8 168.2 reduce-scatter.14
  2735.4 167.6 reduce-scatter.10
where the time goes:
time: 2960 us; the launch traced here: 2920 us
  waiting for transfers between devices  1210 us (41%)
  local copies, waits for them, and re-layouts  965 us (33%)
  other arithmetic  380 us (13%)
  matrix products  284 us (10%)
  blocking collectives  56.1 us (2%)
    slice x73, local copies, waits for them, and re-layouts, local(): lax.associative_scan(combine, (coeff_next, hidden_grad), reverse=True, ax...  404 us
    reduce_scatter x1, waiting for transfers between devices, local(): lax.psum_scatter(jnp.dot(mixed, mixer_weights, preferred_element_type=jnp...  324 us
    slice x67, local copies, waits for them, and re-layouts, local(): hidden = lax.associative_scan(combine, (coeff_term, drive_term), axis=1)[1]  242 us
    reduce_scatter x1, waiting for transfers between devices, local(): lax.psum_scatter(contract_cols(expand_back, expand_flat).astype(jnp.bfloa...  167 us
    reduce_scatter x1, waiting for transfers between devices, local(): lax.psum_scatter(contract_cols(branch_back_low, branch_flat).astype(jnp.b...  159 us
    all_gather x1, waiting for transfers between devices, local(): normed_all = lax.all_gather(normed_one, 'chan', axis=0, tiled=True)  151 us
    all_gather x1, waiting for transfers between devices, local(): normed_mlp = lax.all_gather(normed_two, 'chan', axis=0, tiled=True)  142 us
    all_gather x1, waiting for transfers between devices, local(): back_all = lax.all_gather(cotangent, 'chan', axis=0, tiled=True)  117 us
  transfers between devices with their start and end apart: 12, of which 8 were waited for; matrix products, arithmetic and copies ran while one was open for 34% of the time, Pallas kernels for 0%

commit v1 on v0

v1 whole, which is shorter than its diff:
```python
import math

import jax
import jax.numpy as jnp
from jax import lax
from jax.experimental import pallas as pl
from jax.experimental.pallas import tpu as pltpu
from jax.sharding import PartitionSpec as P

CONV = 4
SEQ_LEN = 2048
SEQS = 2
STEP = 10
PARAMS = 54321152


norm_eps = 1e-06
lru_scale = 8.0
clip_rms = 0.4
beta_one = 0.9
beta_two = 0.95
adam_eps = 1e-08
weight_decay = 0.1
ema_keep = 0.99
rate_matrix = 0.02
rate_gate = 0.1
rate_channel = 1.0
rate_gains = 0.5
SUB = 8
TILE = 16
GELU_SCALE = math.sqrt(2.0 / math.pi)
GELU_CUBE = 0.044715


def contract_rows(left_mat, right_mat):
    return lax.dot_general(
        left_mat, right_mat, (((0,), (0,)), ((), ())), preferred_element_type=jnp.float32
    )


def contract_cols(left_mat, right_mat):
    return lax.dot_general(
        left_mat, right_mat, (((1,), (1,)), ((), ())), preferred_element_type=jnp.float32
    )


def contract(left_mat, right_mat):
    return jnp.dot(left_mat, right_mat, preferred_element_type=jnp.float32)


def norm_back(values, scale, gain, upstream):
    scaled = gain * upstream
    return scale * scaled - values * scale * scale * scale * jnp.mean(
        scaled * values, axis=-1, keepdims=True
    )


def adam(old_state, gradient, factor, step_rate, decay_use):
    clipped = gradient * factor
    moment_one = beta_one * old_state[1] + (1.0 - beta_one) * clipped
    moment_two = beta_two * old_state[2] + (1.0 - beta_two) * clipped * clipped
    first_hat = moment_one / (1.0 - beta_one**STEP)
    second_hat = moment_two / (1.0 - beta_two**STEP)
    master = old_state[0] - step_rate * (
        first_hat / (jnp.sqrt(second_hat) + adam_eps) + decay_use * old_state[0]
    )
    average = ema_keep * old_state[3] + (1.0 - ema_keep) * master
    return (jnp.stack([master, moment_one, moment_two, average]), master)


def gelu_parts(values):
    square = values * values
    turn = jnp.tanh(GELU_SCALE * values * (1.0 + GELU_CUBE * square))
    half = 0.5 * (1.0 + turn)
    slope = half + 0.5 * values * (1.0 - turn * turn) * (
        GELU_SCALE * (1.0 + 3.0 * GELU_CUBE * square)
    )
    return values * half, slope


def decay_parts(log_decay):
    decay = jnp.exp(log_decay)
    z = 2.0 * log_decay
    series = 1.0 + z * (1.0 / 7.0)
    for order in (6.0, 5.0, 4.0, 3.0, 2.0):
        series = 1.0 + z * (1.0 / order) * series
    return decay, jnp.where(z > -0.35, -z * series, 1.0 - decay * decay)


def roll_down(values, offset):
    return pltpu.roll(values, offset, 0)


def roll_up(values, offset):
    return pltpu.roll(values, SUB - offset, 0)


def lru_forward_kernel(
    place_ref,
    gate_ref,
    recur_ref,
    mask_ref,
    rate_w_ref,
    input_w_ref,
    par_ref,
    mixed_ref,
    hidden_ref,
    conv_ref,
    rate_ref,
    admit_ref,
    rate_pre,
    input_pre,
    tail,
    state,
):
    block, width = gate_ref.shape

    @pl.when(pl.program_id(0) == 0)
    def _():
        tail[...] = jnp.zeros_like(tail)
        state[...] = jnp.zeros_like(state)

    row = lax.broadcasted_iota(jnp.int32, (SUB, width), 0)

    def convolve(step, before):
        base = pl.multiple_of(step * TILE, TILE)
        halves = []
        for half in range(2):
            rows = pl.ds(base + half * SUB, SUB)
            now = recur_ref[rows, :]
            masks = mask_ref[rows, :]
            total = par_ref[CONV : CONV + 1, :] + par_ref[0:1, :] * now
            for offset in range(1, CONV):
                moved = jnp.where(
                    row < offset, roll_down(before, offset), roll_down(now, offset)
                )
                total = total + par_ref[offset : offset + 1, :] * (
                    moved * masks[:, offset - 1 : offset]
                )
            halves.append(total)
            before = now
        conv_ref[pl.ds(base, TILE), :] = jnp.concatenate(halves, axis=0).astype(jnp.bfloat16)
        return before

    tail[...] = lax.fori_loop(0, block // TILE, convolve, tail[...])
    low = conv_ref[...]
    rate_pre[...] = contract(low, rate_w_ref[...])
    input_pre[...] = contract(low, input_w_ref[...])

    def advance(step, carry):
        base = pl.multiple_of(step * TILE, TILE)
        conv = conv_ref[pl.ds(base, TILE), :].astype(jnp.float32)
        halves = []
        for half in range(2):
            rows = pl.ds(base + half * SUB, SUB)
            rate = jax.nn.sigmoid(rate_pre[rows, :] + par_ref[CONV + 1 : CONV + 2, :])
            admit = jax.nn.sigmoid(input_pre[rows, :] + par_ref[CONV + 2 : CONV + 3, :])
            decay, rest = decay_parts(par_ref[CONV + 3 : CONV + 4, :] * rate)
            coeff = decay * mask_ref[rows, 0:1]
            drive = jnp.sqrt(rest) * admit * conv[half * SUB : (half + 1) * SUB, :]
            for offset in (1, 2, 4):
                inner = row >= offset
                drive = drive + coeff * jnp.where(inner, roll_down(drive, offset), 0.0)
                coeff = coeff * jnp.where(inner, roll_down(coeff, offset), 1.0)
            hidden = drive + coeff * carry
            carry = jnp.broadcast_to(hidden[SUB - 1 : SUB, :], hidden.shape)
            hidden_ref[rows, :] = hidden
            rate_ref[rows, :] = rate
            admit_ref[rows, :] = admit
            branch = gate_ref[rows, :]
            turn = jnp.tanh(GELU_SCALE * branch * (1.0 + GELU_CUBE * branch * branch))
            halves.append(0.5 * branch * (1.0 + turn) * hidden)
        mixed_ref[pl.ds(base, TILE), :] = jnp.concatenate(halves, axis=0).astype(jnp.bfloat16)
        return carry

    state[...] = lax.fori_loop(0, block // TILE, advance, state[...])


def lru_backward_kernel(
    place_ref,
    upstream_ref,
    gate_ref,
    recur_ref,
    hidden_ref,
    before_ref,
    conv_ref,
    rate_ref,
    admit_ref,
    mask_ref,
    rate_w_ref,
    input_w_ref,
    par_ref,
    gate_back_ref,
    recur_back_ref,
    rate_grad_ref,
    input_grad_ref,
    sums_ref,
    rate_low,
    input_low,
    conv_back,
    state,
    ahead,
):
    block, width = gate_ref.shape
    steps = block // TILE

    @pl.when(pl.program_id(0) == 0)
    def _():
        state[...] = jnp.zeros_like(state)
        ahead[...] = jnp.zeros_like(ahead)
        sums_ref[...] = jnp.zeros_like(sums_ref)
        rate_grad_ref[...] = jnp.zeros_like(rate_grad_ref)
        input_grad_ref[...] = jnp.zeros_like(input_grad_ref)

    row = lax.broadcasted_iota(jnp.int32, (SUB, width), 0)

    def retreat(step, carry):
        carried_next, coeff_next = carry
        index = steps - 1 - step
        base = pl.multiple_of(index * TILE, TILE)
        conv_tile = conv_ref[pl.ds(base, TILE), :].astype(jnp.float32)
        halves = [None, None, None]
        lows = [[None, None] for _ in range(3)]
        edge = pl.multiple_of(jnp.maximum(base - SUB, 0), SUB)
        earlier = jnp.where(index == 0, before_ref[...], hidden_ref[pl.ds(edge, SUB), :])
        for half in (1, 0):
            rows = pl.ds(base + half * SUB, SUB)
            conv = conv_tile[half * SUB : (half + 1) * SUB, :]
            rate = rate_ref[rows, :]
            admit = admit_ref[rows, :]
            speed = par_ref[CONV + 3 : CONV + 4, :]
            decay, rest = decay_parts(speed * rate)
            inverse = lax.rsqrt(rest)
            norm = rest * inverse
            coeff = decay * mask_ref[rows, 0:1]
            act, slope = gelu_parts(gate_ref[rows, :])
            upstream = upstream_ref[rows, :]
            hidden = hidden_ref[rows, :]
            carried = upstream * act
            chain = jnp.where(row == SUB - 1, coeff_next, roll_up(coeff, 1))
            for offset in (1, 2, 4):
                inner = row < SUB - offset
                carried = carried + chain * jnp.where(inner, roll_up(carried, offset), 0.0)
                chain = chain * jnp.where(inner, roll_up(chain, offset), 1.0)
            carried = carried + chain * carried_next
            carried_next = jnp.broadcast_to(carried[0:1, :], carried.shape)
            coeff_next = jnp.broadcast_to(coeff[0:1, :], coeff.shape)
            if half == 1:
                last = hidden_ref[pl.ds(base, SUB), :]
            else:
                last = earlier
            previous = jnp.where(row == 0, roll_down(last, 1), roll_down(hidden, 1))
            log_grad = carried * (
                previous * coeff - admit * conv * (decay * decay) * inverse
            )
            rate_back = log_grad * speed * rate * (1.0 - rate)
            drive = carried * norm
            direct = drive * admit
            input_back = drive * conv * admit * (1.0 - admit)
            conv_back[rows, :] = direct
            lows[0][half] = upstream * hidden * slope
            lows[1][half] = rate_back
            lows[2][half] = input_back
            sums_ref[5] += rate_back
            sums_ref[6] += input_back
            sums_ref[7] += log_grad * rate
        tile = pl.ds(base, TILE)
        gate_back_ref[tile, :] = jnp.concatenate(lows[0], axis=0).astype(jnp.bfloat16)
        rate_low[tile, :] = jnp.concatenate(lows[1], axis=0).astype(jnp.bfloat16)
        input_low[tile, :] = jnp.concatenate(lows[2], axis=0).astype(jnp.bfloat16)
        return carried_next, coeff_next

    carried_next, coeff_next = lax.fori_loop(0, steps, retreat, (state[0], state[1]))
    state[0] = carried_next
    state[1] = coeff_next
    low = conv_ref[...]
    rate_back_low = rate_low[...]
    input_back_low = input_low[...]
    rate_grad_ref[...] += contract_rows(low, rate_back_low)
    input_grad_ref[...] += contract_rows(low, input_back_low)
    conv_back[...] += contract_cols(rate_back_low, rate_w_ref[...]) + contract_cols(
        input_back_low, input_w_ref[...]
    )

    def unconvolve(step, carry):
        base = pl.multiple_of((steps - 1 - step) * TILE, TILE)
        halves = [None, None]
        nexts = list(carry)
        for half in (1, 0):
            rows = pl.ds(base + half * SUB, SUB)
            grad = conv_back[rows, :]
            now = recur_ref[rows, :]
            masks = mask_ref[rows, :]
            sums_ref[0] += grad * now
            sums_ref[CONV] += grad
            total = par_ref[0:1, :] * grad
            for offset in range(1, CONV):
                kept = grad * masks[:, offset - 1 : offset]
                moved = jnp.where(
                    row < SUB - offset, roll_up(kept, offset), roll_up(nexts[offset - 1], offset)
                )
                nexts[offset - 1] = kept
                sums_ref[offset] += moved * now
                total = total + par_ref[offset : offset + 1, :] * moved
            halves[half] = total
        recur_back_ref[pl.ds(base, TILE), :] = jnp.concatenate(halves, axis=0).astype(jnp.bfloat16)
        return tuple(nexts)

    nexts = lax.fori_loop(0, steps, unconvolve, tuple(ahead[k] for k in range(CONV - 1)))
    for k in range(CONV - 1):
        ahead[k] = nexts[k]


def lru_sizes(rows, width, piece):
    block = min(256, piece)
    return block, rows // block, piece // block


def lru_forward(place, gate_branch, recur_input, masks, rate_w, input_w, params, piece):
    rows, width = gate_branch.shape
    block, count, per = lru_sizes(rows, width, piece)

    def there(i, place_ref):
        return (((i // per) ^ place_ref[0]) * per + i % per, 0)

    def here(i, place_ref):
        return (i, 0)

    def fixed(i, place_ref):
        return (0, 0)

    tall = lambda where: pl.BlockSpec((block, width), where)
    square = pl.BlockSpec((width, width), fixed)
    return pl.pallas_call(
        lru_forward_kernel,
        grid_spec=pltpu.PrefetchScalarGridSpec(
            num_scalar_prefetch=1,
            grid=(count,),
            in_specs=[
                tall(there),
                tall(there),
                pl.BlockSpec((block, SUB), here),
                square,
                square,
                pl.BlockSpec((2 * CONV, width), fixed),
            ],
            out_specs=[tall(there), tall(here), tall(here), tall(here), tall(here)],
            scratch_shapes=[
                pltpu.VMEM((block, width), jnp.float32),
                pltpu.VMEM((block, width), jnp.float32),
                pltpu.VMEM((SUB, width), jnp.float32),
                pltpu.VMEM((SUB, width), jnp.float32),
            ],
        ),
        out_shape=[
            jax.ShapeDtypeStruct((rows, width), jnp.bfloat16),
            jax.ShapeDtypeStruct((rows, width), jnp.float32),
            jax.ShapeDtypeStruct((rows, width), jnp.bfloat16),
            jax.ShapeDtypeStruct((rows, width), jnp.float32),
            jax.ShapeDtypeStruct((rows, width), jnp.float32),
        ],
        compiler_params=pltpu.CompilerParams(
            dimension_semantics=("arbitrary",), vmem_limit_bytes=48 * 2**20
        ),
        cost_estimate=pl.CostEstimate(
            flops=4 * rows * width * width,
            bytes_accessed=26 * rows * width,
            transcendentals=6 * rows * width,
        ),
        name="lru_forward",
    )(place, gate_branch, recur_input, masks, rate_w, input_w, params)


def lru_backward(
    place, upstream, gate_branch, recur_input, hidden, conv, rate, admit, masks, rate_w, input_w,
    params, piece,
):
    rows, width = gate_branch.shape
    block, count, per = lru_sizes(rows, width, piece)

    def there(i, place_ref):
        t = count - 1 - i
        return (((t // per) ^ place_ref[0]) * per + t % per, 0)

    def here(i, place_ref):
        return (count - 1 - i, 0)

    def before(i, place_ref):
        return (jnp.maximum((count - 1 - i) * (block // SUB) - 1, 0), 0)

    def fixed(i, place_ref):
        return (0, 0)

    tall = lambda where: pl.BlockSpec((block, width), where)
    square = pl.BlockSpec((width, width), fixed)
    return pl.pallas_call(
        lru_backward_kernel,
        grid_spec=pltpu.PrefetchScalarGridSpec(
            num_scalar_prefetch=1,
            grid=(count,),
            in_specs=[
                tall(there),
                tall(there),
                tall(there),
                tall(here),
                pl.BlockSpec((SUB, width), before),
                tall(here),
                tall(here),
                tall(here),
                pl.BlockSpec((block, SUB), here),
                square,
                square,
                pl.BlockSpec((2 * CONV, width), fixed),
            ],
            out_specs=[
                tall(there),
                tall(there),
                square,
                square,
                pl.BlockSpec((2 * CONV, SUB, width), lambda i, place_ref: (0, 0, 0)),
            ],
            scratch_shapes=[
                pltpu.VMEM((block, width), jnp.bfloat16),
                pltpu.VMEM((block, width), jnp.bfloat16),
                pltpu.VMEM((block, width), jnp.float32),
                pltpu.VMEM((2, SUB, width), jnp.float32),
                pltpu.VMEM((CONV - 1, SUB, width), jnp.float32),
            ],
        ),
        out_shape=[
            jax.ShapeDtypeStruct((rows, width), jnp.bfloat16),
            jax.ShapeDtypeStruct((rows, width), jnp.bfloat16),
            jax.ShapeDtypeStruct((width, width), jnp.float32),
            jax.ShapeDtypeStruct((width, width), jnp.float32),
            jax.ShapeDtypeStruct((2 * CONV, SUB, width), jnp.float32),
        ],
        compiler_params=pltpu.CompilerParams(
            dimension_semantics=("arbitrary",), vmem_limit_bytes=48 * 2**20
        ),
        cost_estimate=pl.CostEstimate(
            flops=8 * rows * width * width,
            bytes_accessed=30 * rows * width,
            transcendentals=6 * rows * width,
        ),
        name="lru_backward",
    )(
        place, upstream, gate_branch, recur_input, hidden, hidden, conv, rate, admit, masks,
        rate_w, input_w, params,
    )


def swap(values, axis, bit):
    return lax.ppermute(
        values, axis, [(i, i ^ bit) for i in range(lax.axis_size(axis))]
    )


def bits_of(size):
    return [1 << k for k in reversed(range(size.bit_length() - 1))]


def gather_rows(own, size):
    blocks = {0: own}
    for bit in bits_of(size):
        blocks.update({m | bit: swap(block, "chan", bit) for m, block in list(blocks.items())})
    return jnp.concatenate([blocks[m] for m in range(size)], axis=0)


def scatter_rows(partial, size):
    rows = partial.shape[0] // size
    blocks = {m: partial[m * rows : (m + 1) * rows] for m in range(size)}
    for bit in reversed(bits_of(size)):
        blocks = {
            m: block.astype(jnp.float32)
            + swap(blocks[m | bit].astype(jnp.bfloat16), "chan", bit).astype(jnp.float32)
            for m, block in blocks.items()
            if not m & bit
        }
    return blocks[0]


def block_diagonal(blocks):
    count, size, _ = blocks.shape
    return jnp.concatenate(
        [jnp.pad(blocks[k], ((0, 0), (k * size, (count - 1 - k) * size))) for k in range(count)],
        axis=0,
    )


def diagonal_blocks(matrix, count):
    size = matrix.shape[0] // count
    return jnp.stack(
        [matrix[k * size : (k + 1) * size, k * size : (k + 1) * size] for k in range(count)]
    )


def local(
    residual,
    cotangent,
    resets,
    branch_weights,
    gate_blocks,
    mixer_weights,
    expand_weights,
    shrink_weights,
    branch_state,
    gate_state,
    mixer_state,
    expand_state,
    shrink_state,
    channel_state,
    gains_state,
):
    seq_count = lax.axis_size("seq")
    group = lax.axis_size("chan") // SEQS
    seq_place = lax.axis_index("seq")
    chan_place = lax.axis_index("chan")
    place = (chan_place % group).astype(jnp.int32).reshape(1)
    width = residual.shape[1]
    piece = residual.shape[0]
    chan_width = branch_weights.shape[2]
    hidden_width = expand_weights.shape[2]
    block_count = gate_blocks.shape[1]

    def partner(values):
        return swap(values, "chan", group)

    def fetch(matrix):
        rows = matrix.shape[0] // seq_count
        part = lax.dynamic_slice_in_dim(matrix, seq_place * rows, rows, axis=0)
        return lax.all_gather(partner(part), "seq", axis=0, tiled=True)

    gains = gains_state[0]
    gain_first = 1.0 + gains[0]
    gain_second = 1.0 + gains[1]
    rows_float = residual.astype(jnp.float32)
    scale_one = lax.rsqrt(jnp.mean(rows_float * rows_float, axis=-1, keepdims=True) + norm_eps)
    normed_one = (rows_float * scale_one * gain_first).astype(jnp.bfloat16)
    normed_all = gather_rows(normed_one, group)

    own_branch = branch_weights.transpose(1, 2, 0)
    other_branch = fetch(own_branch.reshape(2 * chan_width, width)).reshape(own_branch.shape)
    branch_full = jnp.concatenate([own_branch, other_branch], axis=1)
    gate_full = jnp.concatenate([gate_blocks, partner(gate_blocks)], axis=1)
    rate_w = block_diagonal(gate_full[0])
    input_w = block_diagonal(gate_full[1])
    channel = channel_state[0]
    channel_full = jnp.concatenate([channel, partner(channel)], axis=1)
    speed = -lru_scale * jax.nn.softplus(channel_full[CONV + 3 :])
    params = jnp.concatenate([channel_full[: CONV + 3], speed], axis=0)
    mixer_full = jnp.concatenate([mixer_weights, fetch(mixer_weights)], axis=0)
    own_expand = expand_weights.reshape(width, 2 * hidden_width)
    other_expand = fetch(own_expand)
    expand_full = jnp.concatenate(
        [
            own_expand[:, :hidden_width],
            other_expand[:, :hidden_width],
            own_expand[:, hidden_width:],
            other_expand[:, hidden_width:],
        ],
        axis=1,
    )
    shrink_full = jnp.concatenate([shrink_weights, fetch(shrink_weights)], axis=0)
    pair_width = 2 * hidden_width

    flags = lax.dynamic_index_in_dim(
        resets.reshape(SEQS, SEQ_LEN), chan_place // group, axis=0, keepdims=False
    )
    stays = jnp.where(jnp.arange(SEQ_LEN) == 0, 0.0, 1.0 - (flags == 1).astype(jnp.float32))
    within = [stays]
    for offset in range(1, CONV - 1):
        within.append(within[-1] * jnp.pad(stays, (offset, 0))[:SEQ_LEN])
    masks = jnp.stack(within + [stays] * (SUB - len(within)), axis=1)

    gate_branch = contract_cols(normed_all, branch_full[0])
    recur_input = contract_cols(normed_all, branch_full[1])
    mixed, hidden, conv_low, rate, admit = lru_forward(
        place, gate_branch, recur_input, masks, rate_w, input_w, params, piece
    )
    middle = rows_float + scatter_rows(contract(mixed, mixer_full).astype(jnp.bfloat16), group)
    scale_two = lax.rsqrt(jnp.mean(middle * middle, axis=-1, keepdims=True) + norm_eps)
    normed_two = (middle * scale_two * gain_second).astype(jnp.bfloat16)
    normed_mlp = gather_rows(normed_two, group)
    back_all = gather_rows(cotangent, group)
    expanded = contract(normed_mlp, expand_full)
    up_part = expanded[:, pair_width:]
    act_part, slope_part = gelu_parts(expanded[:, :pair_width])
    product_low = (act_part * up_part).astype(jnp.bfloat16)
    product_grad = contract_cols(back_all, shrink_full)
    gate_grad_low = (product_grad * up_part * slope_part).astype(jnp.bfloat16)
    up_grad_low = (product_grad * act_part).astype(jnp.bfloat16)
    expand_back = jnp.concatenate([gate_grad_low, up_grad_low], axis=1)
    normed_two_grad = scatter_rows(
        contract_cols(expand_back, expand_full).astype(jnp.bfloat16), group
    )
    output = (
        middle + scatter_rows(contract(product_low, shrink_full).astype(jnp.bfloat16), group)
    ).astype(jnp.bfloat16)
    gain_two = jnp.sum(normed_two_grad * middle * scale_two, axis=0)
    back_float = cotangent.astype(jnp.float32)
    middle_grad = back_float + norm_back(middle, scale_two, gain_second, normed_two_grad)
    branch_back = gather_rows(middle_grad.astype(jnp.bfloat16), group)

    def reduce_seq(matrix):
        return lax.psum_scatter(
            matrix.astype(jnp.bfloat16), "seq", scatter_dimension=0, tiled=True
        )

    shrink_part = reduce_seq(contract_rows(back_all, product_low))
    expand_part = reduce_seq(contract_rows(normed_mlp, expand_back))

    mixed_grad = contract_cols(branch_back, mixer_full)
    gate_back, recur_back, rate_w_grad, input_w_grad, sums = lru_backward(
        place, mixed_grad, gate_branch, recur_input, hidden, conv_low, rate, admit, masks,
        rate_w, input_w, params, piece,
    )
    branch_back_low = jnp.concatenate([gate_back, recur_back], axis=1)
    branch_part = reduce_seq(contract_rows(normed_all, branch_back_low))
    mixer_part = reduce_seq(contract_rows(branch_back, mixed))
    normed_one_grad = scatter_rows(
        contract(branch_back_low, branch_full.reshape(4 * chan_width, width)).astype(jnp.bfloat16),
        group,
    )
    gain_one = jnp.sum(normed_one_grad * rows_float * scale_one, axis=0)
    residual_grad = middle_grad + norm_back(rows_float, scale_one, gain_first, normed_one_grad)
    gains_grad = lax.psum(jnp.stack([gain_one, gain_two]), ("seq", "chan"))

    channel_pair = jnp.sum(sums, axis=1)
    channel_pair = jnp.concatenate(
        [
            channel_pair[: CONV + 3],
            channel_pair[CONV + 3 :] * -lru_scale * jax.nn.sigmoid(channel_full[CONV + 3 :]),
        ],
        axis=0,
    )
    channel_grad = lax.psum(
        channel_pair[:, :chan_width] + partner(channel_pair[:, chan_width:]), "seq"
    )
    block_size = gate_blocks.shape[2]
    gate_pair = jnp.stack(
        [
            diagonal_blocks(rate_w_grad, 2 * block_count),
            diagonal_blocks(input_w_grad, 2 * block_count),
        ]
    )
    gate_part = lax.psum_scatter(
        gate_pair.astype(jnp.bfloat16), "seq", scatter_dimension=2, tiled=True
    )

    def settle(part, pieces, each):
        mine = [part[:, 2 * k * each : (2 * k + 1) * each] for k in range(pieces)]
        theirs = [part[:, (2 * k + 1) * each : (2 * k + 2) * each] for k in range(pieces)]
        mine = jnp.concatenate(mine, axis=1).astype(jnp.float32)
        return mine + partner(jnp.concatenate(theirs, axis=1)).astype(jnp.float32)

    shrink_grad = settle(shrink_part, 1, hidden_width).T
    expand_grad = settle(expand_part, 2, hidden_width).reshape(-1, 2, hidden_width)
    mixer_grad = settle(mixer_part, 1, chan_width).T
    branch_grad = settle(branch_part, 2, chan_width).reshape(-1, 2, chan_width)
    gate_grad = gate_part[:, :block_count].astype(jnp.float32) + partner(
        gate_part[:, block_count:]
    ).astype(jnp.float32)
    grad_shards = (branch_grad, gate_grad, mixer_grad, expand_grad, shrink_grad)
    own_squares = sum((jnp.sum(shard_grad * shard_grad) for shard_grad in grad_shards))
    own_squares = own_squares + jnp.where(
        seq_place == 0, jnp.sum(channel_grad * channel_grad), 0.0
    )
    total_squares = lax.psum(own_squares, ("seq", "chan"))
    grad_norm = jnp.sqrt(total_squares + jnp.sum(gains_grad * gains_grad))
    clip_limit = clip_rms * math.sqrt(PARAMS)
    factor = jnp.minimum(1.0, clip_limit / (grad_norm + 1e-06))
    branch_new, branch_master = adam(branch_state, branch_grad, factor, rate_matrix, weight_decay)
    gate_new, gate_master = adam(gate_state, gate_grad, factor, rate_gate, weight_decay)
    mixer_new, mixer_master = adam(mixer_state, mixer_grad, factor, rate_matrix, weight_decay)
    expand_new, expand_master = adam(expand_state, expand_grad, factor, rate_matrix, weight_decay)
    shrink_new, shrink_master = adam(shrink_state, shrink_grad, factor, rate_matrix, weight_decay)
    channel_all, _ = adam(channel_state, channel_grad, factor, rate_channel, 0.0)
    gains_new, _ = adam(gains_state, gains_grad, factor, rate_gains, 0.0)
    channel_new = jnp.stack([channel_all[0], channel_all[3]])
    channel_moments = channel_all[1:3]
    return (
        output,
        residual_grad,
        branch_grad,
        gate_grad,
        mixer_grad,
        expand_grad,
        shrink_grad,
        channel_grad,
        gains_grad,
        grad_norm,
        branch_new,
        gate_new,
        mixer_new,
        expand_new,
        shrink_new,
        channel_new,
        channel_moments,
        gains_new,
        branch_master.astype(jnp.bfloat16),
        gate_master.astype(jnp.bfloat16),
        mixer_master.astype(jnp.bfloat16),
        expand_master.astype(jnp.bfloat16),
        shrink_master.astype(jnp.bfloat16),
    )


def solution(mesh):
    in_specs = (
        P(("seq", "chan"), None),
        P(("seq", "chan"), None),
        P("seq"),
        P(None, None, "chan"),
        P(None, "chan", None, None),
        P("chan", None),
        P(None, None, "chan"),
        P("chan", None),
        P(None, "seq", None, "chan"),
        P(None, None, "chan", "seq", None),
        P(None, "chan", "seq"),
        P(None, "seq", None, "chan"),
        P(None, "chan", "seq"),
        P(None, None, "chan"),
        P(),
    )
    out_specs = (
        P(("seq", "chan"), None),
        P(("seq", "chan"), None),
        P("seq", None, "chan"),
        P(None, "chan", "seq", None),
        P("chan", "seq"),
        P("seq", None, "chan"),
        P("chan", "seq"),
        P(None, "chan"),
        P(),
        P(),
        P(None, "seq", None, "chan"),
        P(None, None, "chan", "seq", None),
        P(None, "chan", "seq"),
        P(None, "seq", None, "chan"),
        P(None, "chan", "seq"),
        P(None, None, "chan"),
        P(None, None, "chan"),
        P(),
        P("seq", None, "chan"),
        P(None, "chan", "seq", None),
        P("chan", "seq"),
        P("seq", None, "chan"),
        P("chan", "seq"),
    )
    return jax.shard_map(local, mesh=mesh, in_specs=in_specs, out_specs=out_specs, check_vma=False)
```

time: 2960 us -> 1330 us (0.45); the launches traced: 2920 us -> 1330 us
  local copies, waits for them, and re-layouts: 965 us -> 168 us
  waiting for transfers between devices: 1210 us -> 591 us
  other arithmetic: 380 us -> 110 us
  Pallas kernels: 0 us -> 87.2 us
    slice x142 -> x14, local copies, waits for them, and re-layouts: 652 us -> 48.8 us  [the longest x2 11.9 us: adam(): average = ema_keep * old_state[3] + (1.0 - ema_keep) * master]
    reduce_scatter x7 -> x4, waiting for transfers between devices: 721 us -> 138 us  [reduce_seq(): lax.psum_scatter(matrix.astype(jnp.bfloat16), 'seq', scatter_dimension=0,...]
    ppermute x0 -> x36, waiting for transfers between devices: none -> 453 us  [swap(): lax.ppermute(values, axis, [(i, i ^ bit) for i in range(lax.axis_size(axi...]
    all_gather x4, waiting for transfers between devices: 410 us -> 0.03 us  [fetch(): return lax.all_gather(partner(part), 'seq', axis=0, tiled=True)]
    pad x40 -> x0, local copies, waits for them, and re-layouts: 107 us -> none  [the longest x20 53.7 us: local(): lax.associative_scan(combine, (coeff_next, hidden_grad), reverse=True, ax...]
    reshape x12 -> x2, local copies, waits for them, and re-layouts: 89.8 us -> 2.37 us  [the longest x1 2.35 us: local(): settle(expand_part, 2, hidden_width).reshape(-1, 2, hidden_width)]
    pallas_call x0 -> x2, Pallas kernels: none -> 87.2 us  [the longest x1 50.3 us: lru_backward(): pl.pallas_call(lru_backward_kernel, grid_spec=pltpu.PrefetchScalarGridSpe...]
    mul x23 -> x5, other arithmetic: 86.6 us -> 6.84 us  [the longest x2 6.1 us: adam(): clipped = gradient * factor]
  transfers between devices with their start and end apart: 12 -> 45, of which waited for: 8 -> 19; matrix products, arithmetic and copies ran while one was open for 34% -> 22% of each run, Pallas kernels for 0% -> 3%
where the time goes in v1:
time: 1330 us
  waiting for transfers between devices  591 us (44%)
  matrix products  267 us (20%)
  local copies, waits for them, and re-layouts  168 us (13%)
  other arithmetic  110 us (8%)
  Pallas kernels  87.2 us (7%)
  blocking collectives  54.9 us (4%)
  starting transfers between devices  28.7 us (2%)
  between operations  22.2 us (2%)
    ppermute x36, waiting for transfers between devices, swap(): lax.ppermute(values, axis, [(i, i ^ bit) for i in range(lax.axis_size(axi...  453 us
    reduce_scatter x4, waiting for transfers between devices, reduce_seq(): lax.psum_scatter(matrix.astype(jnp.bfloat16), 'seq', scatter_dimension=0,...  138 us
    dot_general x5, matrix products, contract_cols(): lax.dot_general(left_mat, right_mat, (((1,), (1,)), ((), ())), preferred_...  113 us
    unnamed x193, local copies, waits for them, and re-layouts  85.4 us
    dot_general x4, matrix products, contract_rows(): lax.dot_general(left_mat, right_mat, (((0,), (0,)), ((), ())), preferred_...  79.4 us
    dot_general x4, matrix products, contract(): return jnp.dot(left_mat, right_mat, preferred_element_type=jnp.float32)  74 us
    pallas_call x1, Pallas kernels, lru_backward(): pl.pallas_call(lru_backward_kernel, grid_spec=pltpu.PrefetchScalarGridSpe...  50.3 us
    psum x1, blocking collectives, local(): gains_grad = lax.psum(jnp.stack([gain_one, gain_two]), ('seq', 'chan'))  39.2 us
  transfers between devices with their start and end apart: 45, of which 19 were waited for; matrix products, arithmetic and copies ran while one was open for 22% of the time, Pallas kernels for 3%

profile of v1, /device:TPU:0, one launch (start us, length us, event | category | flops | bytes accessed | tf_op | source)
XLA Modules:
  0.0 1328.6 jit_solution(16310041848107958412)
XLA Ops:
  36.5 23.7 %collective-permute-done.3 = bf16[160,2048]{1,0:T(8,128)(2,1)S(1)} collective-permute-done((bf16[160,2048]{1,0:T(8,128)(2,1)S(1)}, bf16[160,2048]{1,0:T(8,128)(2,1)S(1)}, u32[]{:S(2)}, u32[]{:S(2)}) %collective-permute-start.3) | collective-permute-done | bytes 655392 | tf_op jit(solution)/shard_map/ppermute | solution.py:453
  76.5 40.0 %collective-permute-done.1 = bf16[512,2048]{1,0:T(8,128)(2,1)} collective-permute-done((bf16[512,2048]{1,0:T(8,128)(2,1)}, bf16[512,2048]{1,0:T(8,128)(2,1)}, u32[]{:S(2)}, u32[]{:S(2)}) %collective-permute-start.1) | collective-permute-done | bytes 2097184 | tf_op jit(solution)/shard_map/ppermute | solution.py:453
  122.5 64.1 %collective-permute-done.14 = bf16[192,2048]{1,0:T(8,128)(2,1)S(1)} collective-permute-done((bf16[192,2048]{1,0:T(8,128)(2,1)}, bf16[192,2048]{1,0:T(8,128)(2,1)S(1)}, u32[]{:S(2)}, u32[]{:S(2)}) %collective-permute-start.14) | collective-permute-done | bytes 786464 | tf_op jit(solution)/shard_map/ppermute | solution.py:453
  219.6 37.0 %lru_forward.1 = (bf16[2048,640]{1,0:T(8,128)(2,1)S(1)}, f32[2048,640]{1,0:T(8,128)}, bf16[2048,640]{1,0:T(8,128)(2,1)}, f32[2048,640]{1,0:T(8,128)}, f32[2048,640]{1,0:T(8,128)}) custom-call(s32[1]{0:T(128)} %bitcast.place_ref, f32[2048,640]{1,0:T(8,128)} %fusion.26.gate_ref, f32[2048,640]{1,0:T(8,128)} %fusion.30.recur_ref, f32[2048,8]{1,0:T(8,128)S(1)} %copy.127.mask_ref, ...), custom_call_target="tpu_custom_call" | custom-call | flops 3355443200 | bytes 34078720 | tf_op jit(solution)/shard_map/lru_forward/pallas_call | solution.py:334
  282.8 46.4 %collective-permute-done.9 = bf16[512,2048]{1,0:T(8,128)(2,1)S(1)} collective-permute-done((bf16[512,2048]{1,0:T(8,128)(2,1)S(1)}, bf16[512,2048]{1,0:T(8,128)(2,1)S(1)}, u32[]{:S(2)}, u32[]{:S(2)}) %collective-permute-start.9) | collective-permute-done | bytes 2097184 | tf_op jit(solution)/shard_map/ppermute | solution.py:453
  335.6 38.6 %collective-permute-done.19 = bf16[512,2048]{1,0:T(8,128)(2,1)S(1)} collective-permute-done((bf16[512,2048]{1,0:T(8,128)(2,1)S(1)}, bf16[512,2048]{1,0:T(8,128)(2,1)S(1)}, u32[]{:S(2)}, u32[]{:S(2)}) %collective-permute-start.19) | collective-permute-done | bytes 2097184 | tf_op jit(solution)/shard_map/ppermute | solution.py:453
  379.7 38.8 %collective-permute-done.11 = bf16[512,2048]{1,0:T(8,128)(2,1)} collective-permute-done((bf16[512,2048]{1,0:T(8,128)(2,1)}, bf16[512,2048]{1,0:T(8,128)(2,1)}, u32[]{:S(2)}, u32[]{:S(2)}) %collective-permute-start.11) | collective-permute-done | bytes 2097184 | tf_op jit(solution)/shard_map/ppermute | solution.py:453
  441.3 35.3 %fusion.32 = f32[2048,3072]{1,0:T(8,128)} fusion(bf16[2048,768]{1,0:T(8,128)(2,1)} %get-tuple-element.218, bf16[2048,768]{1,0:T(8,128)(2,1)} %get-tuple-element.216, bf16[2048,768]{1,0:T(8,128)(2,1)} %get-tuple-element.217, bf16[2048,768]{1,0:T(8,128)(2,1)} %get-tuple-element.215, bf16[2048,2048]{1,0:T(8,128)(2,1)} %pad_maximum_fusion.41), kind=kOutput, calls=%fused_computation.90 | convolution fusion | flops 25820135424 | bytes 46137344 | tf_op jit(solution)/shard_map/dot_general | solution.py:48
  476.6 33.2 %multiply_convert_fusion.1 = (bf16[2048,1536]{1,0:T(8,128)(2,1)}, bf16[2048,1536]{1,0:T(8,128)(2,1)}, bf16[2048,1536]{1,0:T(8,128)(2,1)}) fusion(f32[2048,3072]{1,0:T(8,128)} %fusion.32, bf16[2048,2048]{1,0:T(8,128)(2,1)} %constant_dynamic-update-slice_fusion.4, bf16[1536,2048]{1,0:T(8,128)(2,1)} %constant_dynamic-update-slice_fusion.2), kind=kOutput, calls=%fused_computation.4 | convolution fusion | flops 12960399360 | bytes 58720256 | tf_op jit(solution)/shard_map/dot_general | solution.py:42
  509.7 34.2 %fusion.2 = bf16[2048,2048]{1,0:T(8,128)(2,1)} fusion(bf16[2048,1536]{1,0:T(8,128)(2,1)} %get-tuple-element.197, bf16[2048,1536]{1,0:T(8,128)(2,1)} %get-tuple-element.196, bf16[2048,768]{1,0:T(8,128)(2,1)} %get-tuple-element.218, bf16[2048,768]{1,0:T(8,128)(2,1)} %get-tuple-element.216, bf16[2048,768]{1,0:T(8,128)(2,1)} %get-tuple-element.217, ...), kind=kOutput, calls=%fused_computation.24 | convolution fusion | flops 25849495552 | bytes 33554432 | tf_op jit(solution)/shard_map/dot_general | solution.py:42
  549.4 17.2 %convolution_convert_fusion.2 = bf16[2048,2048]{1,0:T(8,128)(2,1)S(1)} fusion(bf16[2048,1536]{1,0:T(8,128)(2,1)} %get-tuple-element.198, bf16[1536,2048]{1,0:T(8,128)(2,1)} %constant_dynamic-update-slice_fusion.2), kind=kOutput, calls=%fused_computation.20 | convolution fusion | flops 12889096192 | bytes 20971520 | tf_op jit(solution)/shard_map/dot_general | solution.py:48
  578.4 39.7 %collective-permute-done.23 = bf16[512,2048]{1,0:T(8,128)(2,1)S(1)} collective-permute-done((bf16[512,2048]{1,0:T(8,128)(2,1)S(1)}, bf16[512,2048]{1,0:T(8,128)(2,1)S(1)}, u32[]{:S(2)}, u32[]{:S(2)}) %collective-permute-start.23) | collective-permute-done | bytes 2097184 | tf_op jit(solution)/shard_map/ppermute | solution.py:453
  621.3 41.3 %collective-permute-done.17 = bf16[512,2048]{1,0:T(8,128)(2,1)} collective-permute-done((bf16[512,2048]{1,0:T(8,128)(2,1)S(1)}, bf16[512,2048]{1,0:T(8,128)(2,1)}, u32[]{:S(2)}, u32[]{:S(2)}) %collective-permute-start.17) | collective-permute-done | bytes 2097184 | tf_op jit(solution)/shard_map/ppermute | solution.py:453
  670.7 47.0 %collective-permute-done.25 = bf16[512,2048]{1,0:T(8,128)(2,1)S(1)} collective-permute-done((bf16[512,2048]{1,0:T(8,128)(2,1)}, bf16[512,2048]{1,0:T(8,128)(2,1)S(1)}, u32[]{:S(2)}, u32[]{:S(2)}) %collective-permute-start.25) | collective-permute-done | bytes 2097184 | tf_op jit(solution)/shard_map/ppermute | solution.py:453
  721.9 16.9 %fusion.43.upstream_ref = f32[2048,640]{1,0:T(8,128)} fusion(bf16[640,2048]{1,0:T(8,128)(2,1)} %constant_dynamic-update-slice_fusion, bf16[512,2048]{1,0:T(8,128)(2,1)S(1)} %collective-permute-done.26, bf16[512,2048]{1,0:T(8,128)(2,1)S(1)} %collective-permute-done.25, bf16[512,2048]{1,0:T(8,128)(2,1)S(1)} %collective-permute-done.24, ...), kind=kOutput, calls=%fused_computation.113 | convolution fusion | flops 5402263552 | bytes 16252928 | tf_op jit(solution)/shard_map/dot_general | solution.py:42
  738.8 50.3 %lru_backward.1 = (bf16[2048,640]{1,0:T(8,128)(2,1)}, bf16[2048,640]{1,0:T(8,128)(2,1)}, f32[640,640]{1,0:T(8,128)S(1)}, f32[640,640]{1,0:T(8,128)S(1)}, f32[8,8,640]{2,1,0:T(8,128)S(1)}) custom-call(s32[1]{0:T(128)} %bitcast.place_ref, f32[2048,640]{1,0:T(8,128)} %fusion.43.upstream_ref, f32[2048,640]{1,0:T(8,128)} %fusion.26.gate_ref, ...), custom_call_target="tpu_custom_call" | custom-call | flops 6710886400 | bytes 39321600 | tf_op jit(solution)/shard_map/lru_backward/pallas_call | solution.py:396
  790.7 19.6 %convolution_convert_fusion.4 = bf16[2048,1536]{1,0:T(8,128)(2,1)} fusion(bf16[2048,2048]{1,0:T(8,128)(2,1)} %constant_dynamic-update-slice_fusion.4, bf16[2048,1536]{1,0:T(8,128)(2,1)} %get-tuple-element.198), kind=kOutput, calls=%fused_computation.22 | convolution fusion | flops 12888047616 | bytes 20971520 | tf_op jit(solution)/shard_map/dot_general | solution.py:36
  822.4 34.1 %convolution_convert_fusion = bf16[2048,3072]{1,0:T(8,128)(2,1)} fusion(bf16[2048,1536]{1,0:T(8,128)(2,1)} %get-tuple-element.197, bf16[2048,1536]{1,0:T(8,128)(2,1)} %get-tuple-element.196, bf16[512,2048]{1,0:T(8,128)(2,1)} %collective-permute-done.12, bf16[512,2048]{1,0:T(8,128)(2,1)} %collective-permute-done.11, ...), kind=kOutput, calls=%fused_computation.9 | convolution fusion | flops 25834815488 | bytes 33554432 | tf_op jit(solution)/shard_map/dot_general | solution.py:36
  935.7 17.7 %collective-permute-done.35 = f32[8,320]{1,0:T(8,128)S(1)} collective-permute-done((f32[8,320]{1,0:T(8,128)S(1)}, f32[8,320]{1,0:T(8,128)S(1)}, u32[]{:S(2)}, u32[]{:S(2)}) %collective-permute-start.35) | collective-permute-done | bytes 10272 | tf_op jit(solution)/shard_map/ppermute | solution.py:453
  953.4 15.7 %psum.21 = f32[8,320]{1,0:T(8,128)S(1)} all-reduce(f32[8,320]{1,0:T(8,128)S(1)} %fusion.83), channel_id=1, replica_groups=mesh['seq'=4,'chan'=8] {'seq'}, use_global_device_ids=true, to_apply=%region_10.11 | all-reduce | flops 2560 | bytes 20480 | tf_op jit(solution)/shard_map/psum | solution.py:636
  997.2 78.9 %reduce-scatter.10.cloned.1.call-done = bf16[512,3072]{1,0:T(8,128)(2,1)} async-done(((bf16[2048,3072]{1,0:T(8,128)(2,1)}), bf16[512,3072]{1,0:T(8,128)(2,1)}) %reduce-scatter.10.cloned.1.call-update) | async-done | bytes 3145744 | tf_op jit(solution)/shard_map/reduce_scatter | solution.py:605
  1081.9 59.3 %reduce-scatter.6.cloned.1.call-done = bf16[512,1280]{1,0:T(8,128)(2,1)} async-done(((bf16[2048,1280]{1,0:T(8,128)(2,1)}), bf16[512,1280]{1,0:T(8,128)(2,1)}) %reduce-scatter.6.cloned.1.call-update) | async-done | bytes 1310736 | tf_op jit(solution)/shard_map/reduce_scatter | solution.py:605
  1156.0 22.6 %collective-permute-done.30 = bf16[512,640]{1,0:T(8,128)(2,1)} collective-permute-done((bf16[512,640]{1,0:T(8,128)(2,1)}, bf16[512,640]{1,0:T(8,128)(2,1)}, u32[]{:S(2)}, u32[]{:S(2)}) %collective-permute-start.30) | collective-permute-done | bytes 655392 | tf_op jit(solution)/shard_map/ppermute | solution.py:453
  1188.4 39.2 %all-reduce.11 = (f32[2,2048]{1,0:T(2,128)S(1)}, f32[]{:T(128)}) all-reduce(f32[2,2048]{1,0:T(2,128)S(1)} %copy-done.57, f32[]{:T(128)S(6)} %add.411), channel_id=1, replica_groups=mesh['seq'=4,'chan'=8] {'seq','chan'}, use_global_device_ids=true, to_apply=%region_13.14 | all-reduce | flops 4097 | bytes 32776 | tf_op jit(solution)/shard_map/psum | solution.py:626
  (393 shorter events, 415.8 us)
Async XLA Ops:
  7.2 180.6 %all-gather.7.cloned.1.call-start = ((), (), s32[]{:S(2)}) async-start(), calls=%async_computation.5 | async-start | bytes 1638400 | tf_op jit(solution)/shard_map/all_gather | solution.py:531
  28.0 162.4 %all-gather.5.cloned.1.call-start = ((), (), s32[]{:S(2)}) async-start(), calls=%async_computation.4 | async-start | bytes 3276800 | tf_op jit(solution)/shard_map/all_gather | solution.py:531
  32.5 84.1 %collective-permute-start.1 = (bf16[512,2048]{1,0:T(8,128)(2,1)}, bf16[512,2048]{1,0:T(8,128)(2,1)}, u32[]{:S(2)}, u32[]{:S(2)}) collective-permute-start(bf16[512,2048]{1,0:T(8,128)(2,1)} %fusion.5), channel_id=1, source_target_pairs={{0,2},{1,3},{2,0},{3,1},{4,6},{5,7},{6,4},{7,5},{8,10},{9,11},{10,... | collective-permute-start | bytes 6291464 | tf_op jit(solution)/shard_map/ppermute | solution.py:453
  61.1 363.3 %all-gather.11.cloned.1.call-start = ((), (), s32[]{:S(2)}) async-start(), calls=%async_computation.7 | async-start | bytes 3932160 | tf_op jit(solution)/shard_map/all_gather | solution.py:531
  61.1 129.3 %collective-permute-start = (bf16[512,2048]{1,0:T(8,128)(2,1)}, bf16[512,2048]{1,0:T(8,128)(2,1)}, u32[]{:S(2)}, u32[]{:S(2)}) collective-permute-start(bf16[512,2048]{1,0:T(8,128)(2,1)} %fusion.5), channel_id=1, source_target_pairs={{0,1},{1,0},{2,3},{3,2},{4,5},{5,4},{6,7},{7,6},{8,9},{9,8},{10,11... | collective-permute-start | bytes 6291464 | tf_op jit(solution)/shard_map/ppermute | solution.py:453
  61.2 60.0 %collective-permute-start.4 = (bf16[2,2,160,160]{3,2,1,0:T(8,128)(2,1)}, bf16[2,2,160,160]{3,2,1,0:T(8,128)(2,1)S(1)}, u32[]{:S(2)}, u32[]{:S(2)}) collective-permute-start(bf16[2,2,160,160]{3,2,1,0:T(8,128)(2,1)} %param.19), channel_id=1, source_target_pairs={{0,4},{1,5},{2,6},{3,7},{4,0},{5,1},{6,2},{7,3},{8,12},{9,13},{10,... | collective-permute-start | bytes 614408 | tf_op jit(solution)/shard_map/ppermute | solution.py:453
  74.7 196.6 %collective-permute-start.13 = (bf16[512,1536]{1,0:T(8,128)(2,1)}, bf16[512,1536]{1,0:T(8,128)(2,1)}, u32[]{:S(2)}, u32[]{:S(2)}) collective-permute-start(bf16[512,1536]{1,0:T(8,128)(2,1)} %constant_dynamic-slice_fusion.1), channel_id=1, source_target_pairs={{0,4},{1,5},{2,6},{3,7},{4,0},{5,1},{6,2},{7,3},{8,12},{9,13},{10,... | collective-permute-start | bytes 4718600 | tf_op jit(solution)/shard_map/ppermute | solution.py:453
  116.5 73.8 %collective-permute-start.2 = (bf16[512,2048]{1,0:T(8,128)(2,1)}, bf16[512,2048]{1,0:T(8,128)(2,1)}, u32[]{:S(2)}, u32[]{:S(2)}) collective-permute-start(bf16[512,2048]{1,0:T(8,128)(2,1)} %collective-permute-done.1), channel_id=1, source_target_pairs={{0,1},{1,0},{2,3},{3,2},{4,5},{5,4},{6,7},{7,6},{8,9},{9,8},{10,11... | collective-permute-start | bytes 6291464 | tf_op jit(solution)/shard_map/ppermute | solution.py:453
  120.3 66.3 %collective-permute-start.14 = (bf16[192,2048]{1,0:T(8,128)(2,1)}, bf16[192,2048]{1,0:T(8,128)(2,1)S(1)}, u32[]{:S(2)}, u32[]{:S(2)}) collective-permute-start(bf16[192,2048]{1,0:T(8,128)(2,1)} %constant_dynamic-slice_fusion), channel_id=1, source_target_pairs={{0,4},{1,5},{2,6},{3,7},{4,0},{5,1},{6,2},{7,3},{8,12},{9,13},{10,... | collective-permute-start | bytes 2359304 | tf_op jit(solution)/shard_map/ppermute | solution.py:453
  187.5 240.8 %all-gather.9.cloned.1.call-start = ((), (), s32[]{:S(2)}) async-start(), calls=%async_computation.6 | async-start | bytes 7864320 | tf_op jit(solution)/shard_map/all_gather | solution.py:531
  271.3 697.7 %all-reduce.14.cloned.1.call-start = ((), (), s32[]{:S(2)}) async-start(), calls=%async_computation.12 | async-start | bytes 1310720
  280.8 93.4 %collective-permute-start.19 = (bf16[512,2048]{1,0:T(8,128)(2,1)S(1)}, bf16[512,2048]{1,0:T(8,128)(2,1)S(1)}, u32[]{:S(2)}, u32[]{:S(2)}) collective-permute-start(bf16[512,2048]{1,0:T(8,128)(2,1)S(1)} %copy-done.14), channel_id=1, source_target_pairs={{0,2},{1,3},{2,0},{3,1},{4,6},{5,7},{6,4},{7,5},{8,10},{9,11},{10,... | collective-permute-start | bytes 6291464 | tf_op jit(solution)/shard_map/ppermute | solution.py:453
  335.6 82.9 %collective-permute-start.11 = (bf16[512,2048]{1,0:T(8,128)(2,1)}, bf16[512,2048]{1,0:T(8,128)(2,1)}, u32[]{:S(2)}, u32[]{:S(2)}) collective-permute-start(bf16[512,2048]{1,0:T(8,128)(2,1)} %multiply_convert_fusion.3), channel_id=1, source_target_pairs={{0,2},{1,3},{2,0},{3,1},{4,6},{5,7},{6,4},{7,5},{8,10},{9,11},{10,... | collective-permute-start | bytes 6291464 | tf_op jit(solution)/shard_map/ppermute | solution.py:453
  335.6 84.4 %collective-permute-start.18 = (bf16[512,2048]{1,0:T(8,128)(2,1)S(1)}, bf16[512,2048]{1,0:T(8,128)(2,1)S(1)}, u32[]{:S(2)}, u32[]{:S(2)}) collective-permute-start(bf16[512,2048]{1,0:T(8,128)(2,1)S(1)} %copy-done.14), channel_id=1, source_target_pairs={{0,1},{1,0},{2,3},{3,2},{4,5},{5,4},{6,7},{7,6},{8,9},{9,8},{10,11... | collective-permute-start | bytes 6291464 | tf_op jit(solution)/shard_map/ppermute | solution.py:453
  573.4 89.2 %collective-permute-start.17 = (bf16[512,2048]{1,0:T(8,128)(2,1)S(1)}, bf16[512,2048]{1,0:T(8,128)(2,1)}, u32[]{:S(2)}, u32[]{:S(2)}) collective-permute-start(bf16[512,2048]{1,0:T(8,128)(2,1)S(1)} %add_convert_fusion.3), channel_id=1, source_target_pairs={{0,2},{1,3},{2,0},{3,1},{4,6},{5,7},{6,4},{7,5},{8,10},{9,11},{10,... | collective-permute-start | bytes 6291464 | tf_op jit(solution)/shard_map/ppermute | solution.py:453
  790.6 199.6 %reduce-scatter.12.cloned.1.call-start = ((), (), s32[]{:S(2)}) async-start(), calls=%async_computation.11 | async-start | bytes 7864320 | tf_op jit(solution)/shard_map/reduce_scatter | solution.py:605
  810.3 184.1 %reduce-scatter.8.cloned.1.call-start = ((), (), s32[]{:S(2)}) async-start(), calls=%async_computation.9 | async-start | bytes 3276800 | tf_op jit(solution)/shard_map/reduce_scatter | solution.py:605
  822.3 253.8 %reduce-scatter.10.cloned.1.call-start = ((), (), s32[]{:S(2)}) async-start(), calls=%async_computation.10 | async-start | bytes 15728640 | tf_op jit(solution)/shard_map/reduce_scatter | solution.py:605
  856.5 284.7 %reduce-scatter.6.cloned.1.call-start = ((), (), s32[]{:S(2)}) async-start(), calls=%async_computation.8 | async-start | bytes 6553600 | tf_op jit(solution)/shard_map/reduce_scatter | solution.py:605
  904.8 74.0 %collective-permute-start.27 = (bf16[512,2048]{1,0:T(8,128)(2,1)}, bf16[512,2048]{1,0:T(8,128)(2,1)}, u32[]{:S(2)}, u32[]{:S(2)}) collective-permute-start(bf16[512,2048]{1,0:T(8,128)(2,1)} %get-tuple-element.203), channel_id=1, source_target_pairs={{0,1},{1,0},{2,3},{3,2},{4,5},{5,4},{6,7},{7,6},{8,9},{9,8},{10,11... | collective-permute-start | bytes 6291464 | tf_op jit(solution)/shard_map/ppermute | solution.py:453
  907.1 71.7 %collective-permute-start.29 = (bf16[512,2048]{1,0:T(8,128)(2,1)}, bf16[512,2048]{1,0:T(8,128)(2,1)}, u32[]{:S(2)}, u32[]{:S(2)}) collective-permute-start(bf16[512,2048]{1,0:T(8,128)(2,1)} %add_convert_fusion), channel_id=1, source_target_pairs={{0,2},{1,3},{2,0},{3,1},{4,6},{5,7},{6,4},{7,5},{8,10},{9,11},{10,... | collective-permute-start | bytes 6291464 | tf_op jit(solution)/shard_map/ppermute | solution.py:453
  992.4 155.0 %collective-permute-start.34 = (bf16[512,768]{1,0:T(8,128)(2,1)}, bf16[512,768]{1,0:T(8,128)(2,1)S(1)}, u32[]{:S(2)}, u32[]{:S(2)}) collective-permute-start(bf16[512,768]{1,0:T(8,128)(2,1)} %slice.467), channel_id=1, source_target_pairs={{0,4},{1,5},{2,6},{3,7},{4,0},{5,1},{6,2},{7,3},{8,12},{9,13},{10,... | collective-permute-start | bytes 2359304 | tf_op jit(solution)/shard_map/ppermute | solution.py:453
  996.3 157.7 %collective-permute-start.32 = (bf16[512,320]{1,0:T(8,128)(2,1)}, bf16[512,320]{1,0:T(8,128)(2,1)S(1)}, u32[]{:S(2)}, u32[]{:S(2)}) collective-permute-start(bf16[512,320]{1,0:T(8,128)(2,1)} %slice.461), channel_id=1, source_target_pairs={{0,4},{1,5},{2,6},{3,7},{4,0},{5,1},{6,2},{7,3},{8,12},{9,13},{10,... | collective-permute-start | bytes 983048 | tf_op jit(solution)/shard_map/ppermute | solution.py:453
  1079.5 104.8 %collective-permute-start.33 = (bf16[512,1536]{1,0:T(8,128)(2,1)}, bf16[512,1536]{1,0:T(8,128)(2,1)}, u32[]{:S(2)}, u32[]{:S(2)}) collective-permute-start(bf16[512,1536]{1,0:T(8,128)(2,1)} %pad_maximum_fusion.16), channel_id=1, source_target_pairs={{0,4},{1,5},{2,6},{3,7},{4,0},{5,1},{6,2},{7,3},{8,12},{9,13},{10,... | collective-permute-start | bytes 4718600 | tf_op jit(solution)/shard_map/ppermute | solution.py:453
  (105 other events, 2562.0 us)
Sparse Core Ops, SparseCore 0:
  28.1 29.9 all-gather.6
  61.2 38.9 all-gather.4
  187.7 42.5 all-gather.10
  271.4 68.5 all-gather.8
  790.8 44.6 all-reduce.13
  838.3 70.2 reduce-scatter.11
  912.1 39.5 reduce-scatter.7
  955.3 120.7 reduce-scatter.9
  1079.7 61.4 reduce-scatter.5

commit v2 on v1

--- a/solution.py
+++ b/solution.py
@@ -97,13 +97,16 @@
 
 def lru_forward_kernel(
     place_ref,
-    gate_ref,
-    recur_ref,
+    normed_ref,
+    gate_w_ref,
+    recur_w_ref,
     mask_ref,
     rate_w_ref,
     input_w_ref,
     par_ref,
     mixed_ref,
+    gate_ref,
+    recur_ref,
     hidden_ref,
     conv_ref,
     rate_ref,
@@ -120,6 +123,9 @@
         tail[...] = jnp.zeros_like(tail)
         state[...] = jnp.zeros_like(state)
 
+    normed = normed_ref[...]
+    recur_ref[...] = contract_cols(normed, recur_w_ref[...])
+    gate_ref[...] = contract_cols(normed, gate_w_ref[...])
     row = lax.broadcasted_iota(jnp.int32, (SUB, width), 0)
 
     def convolve(step, before):
@@ -178,7 +184,8 @@
 
 def lru_backward_kernel(
     place_ref,
-    upstream_ref,
+    back_ref,
+    mixer_ref,
     gate_ref,
     recur_ref,
     hidden_ref,
@@ -195,6 +202,7 @@
     rate_grad_ref,
     input_grad_ref,
     sums_ref,
+    upstream_ref,
     rate_low,
     input_low,
     conv_back,
@@ -212,6 +220,7 @@
         rate_grad_ref[...] = jnp.zeros_like(rate_grad_ref)
         input_grad_ref[...] = jnp.zeros_like(input_grad_ref)
 
+    upstream_ref[...] = contract_cols(back_ref[...], mixer_ref[...])
     row = lax.broadcasted_iota(jnp.int32, (SUB, width), 0)
 
     def retreat(step, carry):
@@ -316,8 +325,9 @@
     return block, rows // block, piece // block
 
 
-def lru_forward(place, gate_branch, recur_input, masks, rate_w, input_w, params, piece):
-    rows, width = gate_branch.shape
+def lru_forward(place, normed, gate_w, recur_w, masks, rate_w, input_w, params, piece):
+    rows, depth = normed.shape
+    width = gate_w.shape[0]
     block, count, per = lru_sizes(rows, width, piece)
 
     def there(i, place_ref):
@@ -331,20 +341,24 @@
 
     tall = lambda where: pl.BlockSpec((block, width), where)
     square = pl.BlockSpec((width, width), fixed)
+    flat = pl.BlockSpec((width, depth), fixed)
+    floats = jax.ShapeDtypeStruct((rows, width), jnp.float32)
+    lows = jax.ShapeDtypeStruct((rows, width), jnp.bfloat16)
     return pl.pallas_call(
         lru_forward_kernel,
         grid_spec=pltpu.PrefetchScalarGridSpec(
             num_scalar_prefetch=1,
             grid=(count,),
             in_specs=[
-                tall(there),
-                tall(there),
+                pl.BlockSpec((block, depth), there),
+                flat,
+                flat,
                 pl.BlockSpec((block, SUB), here),
                 square,
                 square,
                 pl.BlockSpec((2 * CONV, width), fixed),
             ],
-            out_specs=[tall(there), tall(here), tall(here), tall(here), tall(here)],
+            out_specs=[tall(there)] + [tall(here)] * 6,
             scratch_shapes=[
                 pltpu.VMEM((block, width), jnp.float32),
                 pltpu.VMEM((block, width), jnp.float32),
@@ -352,30 +366,25 @@
                 pltpu.VMEM((SUB, width), jnp.float32),
             ],
         ),
-        out_shape=[
-            jax.ShapeDtypeStruct((rows, width), jnp.bfloat16),
-            jax.ShapeDtypeStruct((rows, width), jnp.float32),
-            jax.ShapeDtypeStruct((rows, width), jnp.bfloat16),
-            jax.ShapeDtypeStruct((rows, width), jnp.float32),
-            jax.ShapeDtypeStruct((rows, width), jnp.float32),
-        ],
+        out_shape=[lows, floats, floats, floats, lows, floats, floats],
         compiler_params=pltpu.CompilerParams(
             dimension_semantics=("arbitrary",), vmem_limit_bytes=48 * 2**20
         ),
         cost_estimate=pl.CostEstimate(
-            flops=4 * rows * width * width,
-            bytes_accessed=26 * rows * width,
+            flops=4 * rows * width * (width + depth),
+            bytes_accessed=26 * rows * width + 2 * rows * depth,
             transcendentals=6 * rows * width,
         ),
         name="lru_forward",
-    )(place, gate_branch, recur_input, masks, rate_w, input_w, params)
+    )(place, normed, gate_w, recur_w, masks, rate_w, input_w, params)
 
 
 def lru_backward(
-    place, upstream, gate_branch, recur_input, hidden, conv, rate, admit, masks, rate_w, input_w,
-    params, piece,
+    place, back, mixer, gate_branch, recur_input, hidden, conv, rate, admit, masks, rate_w,
+    input_w, params, piece,
 ):
-    rows, width = gate_branch.shape
+    rows, depth = back.shape
+    width = gate_branch.shape[1]
     block, count, per = lru_sizes(rows, width, piece)
 
     def there(i, place_ref):
@@ -399,9 +408,10 @@
             num_scalar_prefetch=1,
             grid=(count,),
             in_specs=[
-                tall(there),
-                tall(there),
-                tall(there),
+                pl.BlockSpec((block, depth), there),
+                pl.BlockSpec((width, depth), fixed),
+                tall(here),
+                tall(here),
                 tall(here),
                 pl.BlockSpec((SUB, width), before),
                 tall(here),
@@ -420,6 +430,7 @@
                 pl.BlockSpec((2 * CONV, SUB, width), lambda i, place_ref: (0, 0, 0)),
             ],
             scratch_shapes=[
+                pltpu.VMEM((block, width), jnp.float32),
                 pltpu.VMEM((block, width), jnp.bfloat16),
                 pltpu.VMEM((block, width), jnp.bfloat16),
                 pltpu.VMEM((block, width), jnp.float32),
@@ -438,15 +449,59 @@
             dimension_semantics=("arbitrary",), vmem_limit_bytes=48 * 2**20
         ),
         cost_estimate=pl.CostEstimate(
-            flops=8 * rows * width * width,
-            bytes_accessed=30 * rows * width,
+            flops=8 * rows * width * width + 2 * rows * width * depth,
+            bytes_accessed=30 * rows * width + 2 * rows * depth,
             transcendentals=6 * rows * width,
         ),
         name="lru_backward",
     )(
-        place, upstream, gate_branch, recur_input, hidden, hidden, conv, rate, admit, masks,
+        place, back, mixer, gate_branch, recur_input, hidden, hidden, conv, rate, admit, masks,
         rate_w, input_w, params,
     )
+
+
+def adam_kernel(step_rate, decay_use, factor_ref, state_ref, grad_ref, new_ref, copy_ref):
+    clipped = grad_ref[...] * factor_ref[0, 0]
+    master = state_ref[0]
+    moment_one = beta_one * state_ref[1] + (1.0 - beta_one) * clipped
+    moment_two = beta_two * state_ref[2] + (1.0 - beta_two) * clipped * clipped
+    first_hat = moment_one * (1.0 / (1.0 - beta_one**STEP))
+    second_hat = moment_two * (1.0 / (1.0 - beta_two**STEP))
+    master = master - step_rate * (
+        first_hat / (jnp.sqrt(second_hat) + adam_eps) + decay_use * master
+    )
+    new_ref[0] = master
+    new_ref[1] = moment_one
+    new_ref[2] = moment_two
+    new_ref[3] = ema_keep * state_ref[3] + (1.0 - ema_keep) * master
+    copy_ref[...] = master.astype(jnp.bfloat16)
+
+
+def adam_matrix(state, gradient, factor, step_rate, decay_use):
+    rows, rest = gradient.shape[0], gradient.shape[1:]
+    goal = max(16, 2**16 // math.prod(rest))
+    fits = [b for b in range(16, rows + 1, 16) if rows % b == 0 and (b <= goal or b == 16)]
+    block = max(fits, default=rows)
+    zeros = (0,) * len(rest)
+    wide = pl.BlockSpec((4, block) + rest, lambda i: (0, i) + zeros)
+    narrow = pl.BlockSpec((block,) + rest, lambda i: (i,) + zeros)
+    return pl.pallas_call(
+        lambda *refs: adam_kernel(step_rate, decay_use, *refs),
+        grid=(rows // block,),
+        in_specs=[pl.BlockSpec(memory_space=pltpu.SMEM), wide, narrow],
+        out_specs=[wide, narrow],
+        out_shape=[
+            jax.ShapeDtypeStruct(state.shape, jnp.float32),
+            jax.ShapeDtypeStruct(gradient.shape, jnp.bfloat16),
+        ],
+        compiler_params=pltpu.CompilerParams(
+            dimension_semantics=("arbitrary",), vmem_limit_bytes=48 * 2**20
+        ),
+        cost_estimate=pl.CostEstimate(
+            flops=20 * gradient.size, bytes_accessed=38 * gradient.size, transcendentals=0
+        ),
+        name="adam",
+    )(factor.reshape(1, 1), state, gradient)
 
 
 def swap(values, axis, bit):
@@ -459,24 +514,90 @@
     return [1 << k for k in reversed(range(size.bit_length() - 1))]
 
 
-def gather_rows(own, size):
+def later(values, *others):
+    return lax.optimization_barrier((values,) + others)[0]
+
+
+def tree_sum(terms):
+    while len(terms) > 1:
+        terms = [left + right for left, right in zip(terms[::2], terms[1::2])]
+    return terms[0]
+
+
+def sum_over_all(values):
+    values = values + swap(values, "chan", 1)
+    for axis, step in (("chan", 2), ("seq", 1)):
+        others = range(step, lax.axis_size(axis), step)
+        values = tree_sum([values] + [swap(values, axis, other) for other in others])
+    return values
+
+
+def sum_by_steps(values, axes):
+    for axis in axes:
+        for bit in bits_of(lax.axis_size(axis)):
+            values = values + swap(values, axis, bit)
+    return values
+
+
+def both(*values):
+    return lax.optimization_barrier(values)
+
+
+def gather_blocks(own, size):
     blocks = {0: own}
     for bit in bits_of(size):
         blocks.update({m | bit: swap(block, "chan", bit) for m, block in list(blocks.items())})
-    return jnp.concatenate([blocks[m] for m in range(size)], axis=0)
-
-
-def scatter_rows(partial, size):
-    rows = partial.shape[0] // size
-    blocks = {m: partial[m * rows : (m + 1) * rows] for m in range(size)}
-    for bit in reversed(bits_of(size)):
+    return [blocks[m] for m in range(size)]
+
+
+def lay_rows(blocks, room=1):
+    rows = room * sum(block.shape[0] for block in blocks)
+    return lay_more(jnp.zeros((rows,) + blocks[0].shape[1:], blocks[0].dtype), blocks, 0)
+
+
+def lay_more(whole, blocks, start=None):
+    if start is None:
+        start = whole.shape[0] - sum(block.shape[0] for block in blocks)
+    for block in blocks:
+        whole = lax.dynamic_update_slice_in_dim(whole, block, start, axis=0)
+        start += block.shape[0]
+    return whole
+
+
+def split_rows(mat, piece):
+    return [mat[k * piece : (k + 1) * piece] for k in range(mat.shape[0] // piece)]
+
+
+def scatter_near(partial, piece):
+    blocks = dict(enumerate(split_rows(partial, piece)))
+    came = []
+    for bit in reversed(bits_of(len(blocks))):
+        inward = {m: swap(blocks[m | bit], "chan", bit) for m in blocks if not m & bit}
+        came += inward.values()
         blocks = {
-            m: block.astype(jnp.float32)
-            + swap(blocks[m | bit].astype(jnp.bfloat16), "chan", bit).astype(jnp.float32)
-            for m, block in blocks.items()
-            if not m & bit
+            m: (blocks[m].astype(jnp.float32) + block.astype(jnp.float32)).astype(jnp.bfloat16)
+            for m, block in inward.items()
         }
-    return blocks[0]
+    return blocks[0], came
+
+
+def rows_far(parts):
+    return [part[part.shape[0] // 2 :] for part in parts]
+
+
+def rows_near(parts):
+    return [part[: part.shape[0] // 2] for part in parts]
+
+
+def scatter_start(product, parts, size, piece):
+    far = product(*rows_far(parts)).astype(jnp.bfloat16)
+    total, came = scatter_near(far, piece)
+    return swap(total, "chan", size // 2), came, far
+
+
+def scatter_end(arrived, near, piece):
+    total, _ = scatter_near(near, piece)
+    return total.astype(jnp.float32) + arrived.astype(jnp.float32)
 
 
 def block_diagonal(blocks):
@@ -525,10 +646,12 @@
     def partner(values):
         return swap(values, "chan", group)
 
-    def fetch(matrix):
+    def fetch_part(matrix):
         rows = matrix.shape[0] // seq_count
-        part = lax.dynamic_slice_in_dim(matrix, seq_place * rows, rows, axis=0)
-        return lax.all_gather(partner(part), "seq", axis=0, tiled=True)
+        return partner(lax.dynamic_slice_in_dim(matrix, seq_place * rows, rows, axis=0))
+
+    def share(part):
+        return lax.all_gather(part, "seq", axis=0, tiled=True)
 
     gains = gains_state[0]
     gain_first = 1.0 + gains[0]
@@ -536,11 +659,29 @@
     rows_float = residual.astype(jnp.float32)
     scale_one = lax.rsqrt(jnp.mean(rows_float * rows_float, axis=-1, keepdims=True) + norm_eps)
     normed_one = (rows_float * scale_one * gain_first).astype(jnp.bfloat16)
-    normed_all = gather_rows(normed_one, group)
-
+    side = group // 2
     own_branch = branch_weights.transpose(1, 2, 0)
-    other_branch = fetch(own_branch.reshape(2 * chan_width, width)).reshape(own_branch.shape)
+    first_part = fetch_part(
+        later(
+            jnp.concatenate([own_branch.reshape(2 * chan_width, width), mixer_weights], axis=0),
+            normed_one,
+        )
+    )
+    half = piece // 2
+    normed_top, first_part = both(swap(normed_one[:half], "chan", side), first_part)
+    others = share(first_part)
+    other_branch = others[: 2 * chan_width].reshape(own_branch.shape)
+    other_mixer = others[2 * chan_width :]
     branch_full = jnp.concatenate([own_branch, other_branch], axis=1)
+    normed_end = swap(later(normed_one, normed_top)[half:], "chan", side)
+    normed_far = gather_blocks(jnp.concatenate([normed_top, normed_end], axis=0), side)
+    normed_all = lay_rows(gather_blocks(normed_one, side) + normed_far)
+    back_far = swap(later(cotangent, normed_end), "chan", side)
+    own_expand = expand_weights.reshape(width, 2 * hidden_width)
+    expand_part = fetch_part(later(own_expand, normed_end))
+    shrink_part = fetch_part(later(shrink_weights, normed_end))
+    pair_width = 2 * hidden_width
+
     gate_full = jnp.concatenate([gate_blocks, partner(gate_blocks)], axis=1)
     rate_w = block_diagonal(gate_full[0])
     input_w = block_diagonal(gate_full[1])
@@ -548,9 +689,23 @@
     channel_full = jnp.concatenate([channel, partner(channel)], axis=1)
     speed = -lru_scale * jax.nn.softplus(channel_full[CONV + 3 :])
     params = jnp.concatenate([channel_full[: CONV + 3], speed], axis=0)
-    mixer_full = jnp.concatenate([mixer_weights, fetch(mixer_weights)], axis=0)
-    own_expand = expand_weights.reshape(width, 2 * hidden_width)
-    other_expand = fetch(own_expand)
+
+    flags = lax.dynamic_index_in_dim(
+        resets.reshape(SEQS, SEQ_LEN), chan_place // group, axis=0, keepdims=False
+    )
+    stays = jnp.where(jnp.arange(SEQ_LEN) == 0, 0.0, 1.0 - (flags == 1).astype(jnp.float32))
+    within = [stays]
+    for offset in range(1, CONV - 1):
+        within.append(within[-1] * jnp.pad(stays, (offset, 0))[:SEQ_LEN])
+    masks = jnp.stack(within + [stays] * (SUB - len(within)), axis=1)
+
+    mixed, gate_branch, recur_input, hidden, conv_low, rate, admit = lru_forward(
+        place, normed_all, branch_full[0], branch_full[1], masks, rate_w, input_w, params, piece
+    )
+    mixed, back_far, expand_part = both(mixed, back_far, expand_part)
+    mixer_full = jnp.concatenate([mixer_weights, other_mixer], axis=0)
+    back_all = lay_rows(gather_blocks(cotangent, side) + gather_blocks(back_far, side))
+    other_expand = share(expand_part)
     expand_full = jnp.concatenate(
         [
             own_expand[:, :hidden_width],
@@ -560,70 +715,121 @@
         ],
         axis=1,
     )
-    shrink_full = jnp.concatenate([shrink_weights, fetch(shrink_weights)], axis=0)
-    pair_width = 2 * hidden_width
-
-    flags = lax.dynamic_index_in_dim(
-        resets.reshape(SEQS, SEQ_LEN), chan_place // group, axis=0, keepdims=False
-    )
-    stays = jnp.where(jnp.arange(SEQ_LEN) == 0, 0.0, 1.0 - (flags == 1).astype(jnp.float32))
-    within = [stays]
-    for offset in range(1, CONV - 1):
-        within.append(within[-1] * jnp.pad(stays, (offset, 0))[:SEQ_LEN])
-    masks = jnp.stack(within + [stays] * (SUB - len(within)), axis=1)
-
-    gate_branch = contract_cols(normed_all, branch_full[0])
-    recur_input = contract_cols(normed_all, branch_full[1])
-    mixed, hidden, conv_low, rate, admit = lru_forward(
-        place, gate_branch, recur_input, masks, rate_w, input_w, params, piece
-    )
-    middle = rows_float + scatter_rows(contract(mixed, mixer_full).astype(jnp.bfloat16), group)
+    through_mixer = lambda left: contract(left, mixer_full)
+    arrived, came, _ = scatter_start(through_mixer, [mixed], group, piece)
+    near = through_mixer(*rows_near([later(mixed, *came)])).astype(jnp.bfloat16)
+    arrived, shrink_part = both(arrived, shrink_part)
+    middle = rows_float + scatter_end(arrived, near, piece)
     scale_two = lax.rsqrt(jnp.mean(middle * middle, axis=-1, keepdims=True) + norm_eps)
     normed_two = (middle * scale_two * gain_second).astype(jnp.bfloat16)
-    normed_mlp = gather_rows(normed_two, group)
-    back_all = gather_rows(cotangent, group)
+    shrink_full = lay_rows([shrink_weights, share(later(shrink_part, other_expand))])
+    mlp_near = lay_rows(gather_blocks(normed_two, side), 2)
+    mlp_far, mlp_near, back_all, expand_full = both(
+        swap(normed_two, "chan", side), mlp_near, back_all, expand_full
+    )
+    normed_mlp = lay_more(mlp_near, gather_blocks(mlp_far, side))
     expanded = contract(normed_mlp, expand_full)
+    product_grad = contract_cols(back_all, shrink_full)
     up_part = expanded[:, pair_width:]
     act_part, slope_part = gelu_parts(expanded[:, :pair_width])
     product_low = (act_part * up_part).astype(jnp.bfloat16)
-    product_grad = contract_cols(back_all, shrink_full)
     gate_grad_low = (product_grad * up_part * slope_part).astype(jnp.bfloat16)
     up_grad_low = (product_grad * act_part).astype(jnp.bfloat16)
-    expand_back = jnp.concatenate([gate_grad_low, up_grad_low], axis=1)
-    normed_two_grad = scatter_rows(
-        contract_cols(expand_back, expand_full).astype(jnp.bfloat16), group
-    )
-    output = (
-        middle + scatter_rows(contract(product_low, shrink_full).astype(jnp.bfloat16), group)
-    ).astype(jnp.bfloat16)
-    gain_two = jnp.sum(normed_two_grad * middle * scale_two, axis=0)
-    back_float = cotangent.astype(jnp.float32)
-    middle_grad = back_float + norm_back(middle, scale_two, gain_second, normed_two_grad)
-    branch_back = gather_rows(middle_grad.astype(jnp.bfloat16), group)
-
     def reduce_seq(matrix):
         return lax.psum_scatter(
             matrix.astype(jnp.bfloat16), "seq", scatter_dimension=0, tiled=True
         )
 
-    shrink_part = reduce_seq(contract_rows(back_all, product_low))
-    expand_part = reduce_seq(contract_rows(normed_mlp, expand_back))
-
-    mixed_grad = contract_cols(branch_back, mixer_full)
+    def through_expand(*grads):
+        return contract_cols(jnp.concatenate(grads, axis=1), expand_full)
+
+    def through_shrink(left):
+        return contract(left, shrink_full)
+
+    arrived, came, _ = scatter_start(through_expand, [gate_grad_low, up_grad_low], group, piece)
+    gate_grad_low, up_grad_low, product_low, *_ = both(
+        gate_grad_low, up_grad_low, product_low, *came
+    )
+    expand_local = contract_rows(
+        normed_mlp, jnp.concatenate([gate_grad_low, up_grad_low], axis=1)
+    ).astype(jnp.bfloat16)
+    arrived, expand_local, gate_grad_low = both(arrived, expand_local, gate_grad_low)
+    near = through_expand(*rows_near([gate_grad_low, up_grad_low])).astype(jnp.bfloat16)
+    expand_sum = reduce_seq(expand_local)
+    normed_two_grad = scatter_end(arrived, near, piece)
+    back_float = cotangent.astype(jnp.float32)
+    middle_grad = back_float + norm_back(middle, scale_two, gain_second, normed_two_grad)
+    middle_low = middle_grad.astype(jnp.bfloat16)
+    product_low = later(product_low, middle_low)
+    shrink_local = contract_rows(back_all, product_low).astype(jnp.bfloat16)
+    middle_near = lay_rows(gather_blocks(middle_low, side), 2)
+    product_low = later(product_low, shrink_local)
+    out_arrived, _, out_far = scatter_start(through_shrink, [product_low], group, piece)
+    out_near = through_shrink(*rows_near([later(product_low, out_far)])).astype(jnp.bfloat16)
+    middle_far, shrink_local, middle_near, out_near = both(
+        swap(middle_low, "chan", side), shrink_local, middle_near, out_near
+    )
+    shrink_sum = reduce_seq(shrink_local)
+    branch_back = lay_more(middle_near, gather_blocks(middle_far, side))
+    gain_two = jnp.sum(normed_two_grad * middle * scale_two, axis=0)
+
+    def settle(part, pieces, each):
+        mine = [part[:, 2 * k * each : (2 * k + 1) * each] for k in range(pieces)]
+        theirs = [part[:, (2 * k + 1) * each : (2 * k + 2) * each] for k in range(pieces)]
+        return jnp.concatenate(mine, axis=1), partner(jnp.concatenate(theirs, axis=1))
+
+    def total(pair):
+        return pair[0].astype(jnp.float32) + pair[1].astype(jnp.float32)
+
+    mixer_local = contract_rows(branch_back, mixed).astype(jnp.bfloat16)
+    mixer_sum = reduce_seq(mixer_local)
+    expand_pair = settle(expand_sum, 2, hidden_width)
     gate_back, recur_back, rate_w_grad, input_w_grad, sums = lru_backward(
-        place, mixed_grad, gate_branch, recur_input, hidden, conv_low, rate, admit, masks,
-        rate_w, input_w, params, piece,
-    )
+        place, later(branch_back, mixer_local), mixer_full, gate_branch, recur_input, hidden,
+        conv_low, rate, admit, masks, rate_w, input_w, params, piece,
+    )
+    gate_back, out_arrived, expand_theirs = both(gate_back, out_arrived, expand_pair[1])
+    expand_pair = (expand_pair[0], expand_theirs)
     branch_back_low = jnp.concatenate([gate_back, recur_back], axis=1)
-    branch_part = reduce_seq(contract_rows(normed_all, branch_back_low))
-    mixer_part = reduce_seq(contract_rows(branch_back, mixed))
-    normed_one_grad = scatter_rows(
-        contract(branch_back_low, branch_full.reshape(4 * chan_width, width)).astype(jnp.bfloat16),
-        group,
-    )
+    branch_local = contract_rows(normed_all, branch_back_low).astype(jnp.bfloat16)
+    branch_sum = reduce_seq(branch_local)
+    through_branch = lambda left: contract(left, branch_full.reshape(4 * chan_width, width))
+    branch_back_low = later(branch_back_low, branch_local)
+    arrived, came, far = scatter_start(through_branch, [branch_back_low], group, piece)
+    branch_back_low, *_ = both(branch_back_low, *came)
+    shrink_pair = settle(later(shrink_sum, far), 1, hidden_width)
+    near = through_branch(*rows_near([branch_back_low])).astype(jnp.bfloat16)
+    mixer_pair = settle(later(mixer_sum, near), 1, chan_width)
+    rate_w_grad, input_w_grad, sums = (
+        later(rate_w_grad, far), later(input_w_grad, far), later(sums, far)
+    )
+    block_size = gate_blocks.shape[2]
+    gate_pair = jnp.stack(
+        [
+            diagonal_blocks(rate_w_grad, 2 * block_count),
+            diagonal_blocks(input_w_grad, 2 * block_count),
+        ]
+    )
+    gate_pair = gate_pair.reshape(
+        2, 2 * block_count, seq_count, block_size // seq_count, block_size
+    )
+
+    def gate_rows(other):
+        rows = lax.dynamic_index_in_dim(gate_pair, seq_place ^ other, axis=2, keepdims=False)
+        return swap(rows.astype(jnp.bfloat16), "seq", other).astype(jnp.float32) if other else rows
+
+    gate_part = sum(gate_rows(other) for other in range(seq_count))
+    gate_theirs = partner(gate_part[:, block_count:].astype(jnp.bfloat16))
+    branch_sum, near, arrived, gate_theirs, shrink_theirs, mixer_theirs = both(
+        branch_sum, near, arrived, gate_theirs, shrink_pair[1], mixer_pair[1]
+    )
+    mixer_pair = (mixer_pair[0], mixer_theirs)
+    shrink_pair = (shrink_pair[0], shrink_theirs)
+    output = (middle + scatter_end(out_arrived, out_near, piece)).astype(jnp.bfloat16)
+    normed_one_grad = scatter_end(arrived, near, piece)
     gain_one = jnp.sum(normed_one_grad * rows_float * scale_one, axis=0)
     residual_grad = middle_grad + norm_back(rows_float, scale_one, gain_first, normed_one_grad)
-    gains_grad = lax.psum(jnp.stack([gain_one, gain_two]), ("seq", "chan"))
+    gains_grad = sum_by_steps(jnp.stack([gain_one, gain_two]), ("seq", "chan"))
 
     channel_pair = jnp.sum(sums, axis=1)
     channel_pair = jnp.concatenate(
@@ -633,47 +839,52 @@
         ],
         axis=0,
     )
-    channel_grad = lax.psum(
-        channel_pair[:, :chan_width] + partner(channel_pair[:, chan_width:]), "seq"
-    )
-    block_size = gate_blocks.shape[2]
-    gate_pair = jnp.stack(
-        [
-            diagonal_blocks(rate_w_grad, 2 * block_count),
-            diagonal_blocks(input_w_grad, 2 * block_count),
-        ]
-    )
-    gate_part = lax.psum_scatter(
-        gate_pair.astype(jnp.bfloat16), "seq", scatter_dimension=2, tiled=True
-    )
-
-    def settle(part, pieces, each):
-        mine = [part[:, 2 * k * each : (2 * k + 1) * each] for k in range(pieces)]
-        theirs = [part[:, (2 * k + 1) * each : (2 * k + 2) * each] for k in range(pieces)]
-        mine = jnp.concatenate(mine, axis=1).astype(jnp.float32)
-        return mine + partner(jnp.concatenate(theirs, axis=1)).astype(jnp.float32)
-
-    shrink_grad = settle(shrink_part, 1, hidden_width).T
-    expand_grad = settle(expand_part, 2, hidden_width).reshape(-1, 2, hidden_width)
-    mixer_grad = settle(mixer_part, 1, chan_width).T
-    branch_grad = settle(branch_part, 2, chan_width).reshape(-1, 2, chan_width)
-    gate_grad = gate_part[:, :block_count].astype(jnp.float32) + partner(
-        gate_part[:, block_count:]
-    ).astype(jnp.float32)
+    channel_grad = sum_by_steps(
+        channel_pair[:, :chan_width] + partner(channel_pair[:, chan_width:]), ("seq",)
+    )
+    shrink_grad = total(shrink_pair).T
+    expand_grad = lax.optimization_barrier(
+        total(expand_pair).reshape(-1, 2, hidden_width)
+    )
+    mixer_grad = total(mixer_pair).T
+    branch_grad = total(settle(branch_sum, 2, chan_width)).reshape(-1, 2, chan_width)
+    gate_grad = gate_part[:, :block_count] + gate_theirs.astype(jnp.float32)
     grad_shards = (branch_grad, gate_grad, mixer_grad, expand_grad, shrink_grad)
     own_squares = sum((jnp.sum(shard_grad * shard_grad) for shard_grad in grad_shards))
     own_squares = own_squares + jnp.where(
         seq_place == 0, jnp.sum(channel_grad * channel_grad), 0.0
     )
-    total_squares = lax.psum(own_squares, ("seq", "chan"))
+    total_squares = sum_over_all(own_squares.reshape(1))[0]
     grad_norm = jnp.sqrt(total_squares + jnp.sum(gains_grad * gains_grad))
     clip_limit = clip_rms * math.sqrt(PARAMS)
     factor = jnp.minimum(1.0, clip_limit / (grad_norm + 1e-06))
-    branch_new, branch_master = adam(branch_state, branch_grad, factor, rate_matrix, weight_decay)
-    gate_new, gate_master = adam(gate_state, gate_grad, factor, rate_gate, weight_decay)
-    mixer_new, mixer_master = adam(mixer_state, mixer_grad, factor, rate_matrix, weight_decay)
-    expand_new, expand_master = adam(expand_state, expand_grad, factor, rate_matrix, weight_decay)
-    shrink_new, shrink_master = adam(shrink_state, shrink_grad, factor, rate_matrix, weight_decay)
+    part_rows = width // seq_count
+
+    def rows_of_branch(values):
+        return jnp.moveaxis(values, -3, -1).reshape(values.shape[:-3] + (2 * chan_width, part_rows))
+
+    def branch_of_rows(values):
+        return jnp.moveaxis(values.reshape(values.shape[:-2] + (2, chan_width, part_rows)), -1, -3)
+
+    branch_new, branch_copy = map(
+        branch_of_rows,
+        adam_matrix(
+            rows_of_branch(branch_state), rows_of_branch(branch_grad), factor, rate_matrix,
+            weight_decay,
+        ),
+    )
+    gate_rows_state = gate_state.reshape(4, -1, block_size)
+    gate_new, gate_copy = adam_matrix(
+        gate_rows_state, gate_grad.reshape(-1, block_size), factor, rate_gate, weight_decay
+    )
+    gate_new, gate_copy = gate_new.reshape(gate_state.shape), gate_copy.reshape(gate_grad.shape)
+    mixer_new, mixer_copy = adam_matrix(mixer_state, mixer_grad, factor, rate_matrix, weight_decay)
+    expand_new, expand_copy = adam_matrix(
+        expand_state, expand_grad, factor, rate_matrix, weight_decay
+    )
+    shrink_new, shrink_copy = adam_matrix(
+        shrink_state, shrink_grad, factor, rate_matrix, weight_decay
+    )
     channel_all, _ = adam(channel_state, channel_grad, factor, rate_channel, 0.0)
     gains_new, _ = adam(gains_state, gains_grad, factor, rate_gains, 0.0)
     channel_new = jnp.stack([channel_all[0], channel_all[3]])
@@ -697,11 +908,11 @@
         channel_new,
         channel_moments,
         gains_new,
-        branch_master.astype(jnp.bfloat16),
-        gate_master.astype(jnp.bfloat16),
-        mixer_master.astype(jnp.bfloat16),
-        expand_master.astype(jnp.bfloat16),
-        shrink_master.astype(jnp.bfloat16),
+        branch_copy,
+        gate_copy,
+        mixer_copy,
+        expand_copy,
+        shrink_copy,
     )
 
 

time: 1330 us -> 985 us (0.74)
  waiting for transfers between devices: 591 us -> 261 us
  Pallas kernels: 87.2 us -> 156 us
  blocking collectives: 54.9 us -> 0 us
  matrix products: 267 us -> 226 us
  starting transfers between devices: 28.7 us -> 60.5 us
  other arithmetic: 110 us -> 91.1 us
    ppermute x36 -> x53, waiting for transfers between devices: 453 us -> 258 us  [swap(): lax.ppermute(values, axis, [(i, i ^ bit) for i in range(lax.axis_size(axi...]
    reduce_scatter x4, waiting for transfers between devices: 138 us -> 0.02 us  [reduce_seq(): lax.psum_scatter(matrix.astype(jnp.bfloat16), 'seq', scatter_dimension=0,...]
    dynamic_update_slice x0 -> x17, local copies, waits for them, and re-layouts: none -> 58.8 us  [lay_more(): whole = lax.dynamic_update_slice_in_dim(whole, block, start, axis=0)]
    psum x2 -> x0, blocking collectives: 54.9 us -> none  [the longest x1 39.2 us: local(): gains_grad = lax.psum(jnp.stack([gain_one, gain_two]), ('seq', 'chan'))]
    unnamed x193 -> x154, local copies, waits for them, and re-layouts: 85.4 us -> 31 us
    dot_general x5 -> x3, matrix products: 113 us -> 70 us  [contract_cols(): lax.dot_general(left_mat, right_mat, (((1,), (1,)), ((), ())), preferred_...]
    pallas_call x0 -> x5, Pallas kernels: none -> 36.3 us  [adam_matrix(): pl.pallas_call(lambda *refs: adam_kernel(step_rate, decay_use, *refs), gr...]
    ppermute x36 -> x53, starting transfers between devices: 28.1 us -> 59.8 us  [swap(): lax.ppermute(values, axis, [(i, i ^ bit) for i in range(lax.axis_size(axi...]
  transfers between devices with their start and end apart: 45 -> 60, of which waited for: 19 -> 25; matrix products, arithmetic and copies ran while one was open for 22% -> 39% of each run, Pallas kernels for 3% -> 12%
where the time goes in v2:
time: 985 us; the launch traced here: 976 us
  waiting for transfers between devices  261 us (26%)
  matrix products  226 us (23%)
  local copies, waits for them, and re-layouts  156 us (16%)
  Pallas kernels  156 us (16%)
  other arithmetic  91.1 us (9%)
  starting transfers between devices  60.5 us (6%)
  between operations  25.6 us (3%)
    ppermute x53, waiting for transfers between devices, swap(): lax.ppermute(values, axis, [(i, i ^ bit) for i in range(lax.axis_size(axi...  258 us
    dot_general x7, matrix products, contract(): return jnp.dot(left_mat, right_mat, preferred_element_type=jnp.float32)  83.2 us
    dot_general x4, matrix products, contract_rows(): lax.dot_general(left_mat, right_mat, (((0,), (0,)), ((), ())), preferred_...  73.3 us
    dot_general x3, matrix products, contract_cols(): lax.dot_general(left_mat, right_mat, (((1,), (1,)), ((), ())), preferred_...  70 us
    pallas_call x1, Pallas kernels, lru_backward(): pl.pallas_call(lru_backward_kernel, grid_spec=pltpu.PrefetchScalarGridSpe...  65.3 us
    ppermute x53, starting transfers between devices, swap(): lax.ppermute(values, axis, [(i, i ^ bit) for i in range(lax.axis_size(axi...  59.8 us
    dynamic_update_slice x17, local copies, waits for them, and re-layouts, lay_more(): whole = lax.dynamic_update_slice_in_dim(whole, block, start, axis=0)  58.8 us
    pallas_call x1, Pallas kernels, lru_forward(): pl.pallas_call(lru_forward_kernel, grid_spec=pltpu.PrefetchScalarGridSpec...  54 us
  transfers between devices with their start and end apart: 60, of which 25 were waited for; matrix products, arithmetic and copies ran while one was open for 39% of the time, Pallas kernels for 12%

profile of v2, /device:TPU:0, one launch (start us, length us, event | category | flops | bytes accessed | tf_op | source)
XLA Modules:
  0.0 975.9 jit_solution(14272590177659616717)
XLA Ops:
  26.8 42.6 %collective-permute-done.2 = bf16[240,2048]{1,0:T(8,128)(2,1)S(1)} collective-permute-done((bf16[240,2048]{1,0:T(8,128)(2,1)S(1)}, bf16[240,2048]{1,0:T(8,128)(2,1)S(1)}, u32[]{:S(2)}, u32[]{:S(2)}) %collective-permute-start.2) | collective-permute-done | bytes 983072 | tf_op jit(solution)/shard_map/ppermute | solution.py:508
  78.0 24.8 %collective-permute-done.3 = bf16[256,2048]{1,0:T(8,128)(2,1)S(1)} collective-permute-done((bf16[256,2048]{1,0:T(8,128)(2,1)S(1)}, bf16[256,2048]{1,0:T(8,128)(2,1)S(1)}, u32[]{:S(2)}, u32[]{:S(2)}) %collective-permute-start.3) | collective-permute-done | bytes 1048608 | tf_op jit(solution)/shard_map/ppermute | solution.py:508
  139.2 54.0 %lru_forward.1 = (bf16[2048,640]{1,0:T(8,128)(2,1)S(1)}, f32[2048,640]{1,0:T(8,128)}, f32[2048,640]{1,0:T(8,128)}, f32[2048,640]{1,0:T(8,128)}, bf16[2048,640]{1...) custom-call(s32[1]{0:T(128)} %bitcast.place_ref, ...), custom_call_target="tpu_custom_call" | custom-call | flops 14092861440 | bytes 42467328 | tf_op jit(solution)/shard_map/lru_forward/pallas_call | solution.py:347
  194.6 9.6 collective-permute-done.7
  229.2 51.5 %collective-permute-done.12 = bf16[192,2048]{1,0:T(8,128)(2,1)S(1)} collective-permute-done((bf16[192,2048]{1,0:T(8,128)(2,1)S(1)}, bf16[192,2048]{1,0:T(8,128)(2,1)S(1)}, u32[]{:S(2)}, u32[]{:S(2)}) %collective-permute-start.12) | collective-permute-done | bytes 786464 | tf_op jit(solution)/shard_map/ppermute | solution.py:508
  324.6 24.5 %collective-permute-done.13 = bf16[512,2048]{1,0:T(8,128)(2,1)} collective-permute-done((bf16[512,2048]{1,0:T(8,128)(2,1)}, bf16[512,2048]{1,0:T(8,128)(2,1)}, u32[]{:S(2)}, u32[]{:S(2)}) %collective-permute-start.13) | collective-permute-done | bytes 2097184 | tf_op jit(solution)/shard_map/ppermute | solution.py:508
  357.7 34.3 %fusion.96 = f32[2048,3072]{0,1:T(8,128)} fusion(bf16[2048,2048]{1,0:T(8,128)(2,1)} %constant_dynamic-update-slice_fusion.9, bf16[2048,3072]{1,0:T(8,128)(2,1)} %pad_maximum_fusion), kind=kOutput, calls=%fused_computation.220 | convolution fusion | flops 25769803776 | bytes 46137344 | tf_op jit(solution)/shard_map/dot_general | solution.py:48
  398.5 31.8 %multiply_convert_fusion.2 = (bf16[2048,1536]{0,1:T(8,128)(2,1)}, bf16[2048,1536]{0,1:T(8,128)(2,1)}, bf16[2048,1536]{0,1:T(8,128)(2,1)}) fusion(f32[2048,3072]{0,1:T(8,128)} %fusion.96, bf16[2048,2048]{1,0:T(8,128)(2,1)} %copy-done.25, bf16[1536,2048]{1,0:T(8,128)(2,1)} %constant_dynamic-update-slice_fusion.2), kind=kOutput, calls=%fused_computation.7 | convolution fusion | flops 12960399360 | bytes 58720256 | tf_op jit(solution)/shard_map/dot_general | solution.py:42
  436.1 18.8 %fusion.32 = bf16[1024,2048]{1,0:T(8,128)(2,1)} fusion(bf16[2048,3072]{1,0:T(8,128)(2,1)} %pad_maximum_fusion, bf16[1024,1536]{0,1:T(8,128)(2,1)} %slice.404, bf16[1024,1536]{0,1:T(8,128)(2,1)S(1)} %slice.403), kind=kOutput, calls=%fused_computation.65 | convolution fusion | flops 12899581952 | bytes 23068672 | tf_op jit(solution)/shard_map/dot_general | solution.py:42
  464.6 35.4 %fusion.5 = bf16[2048,3072]{1,0:T(8,128)(2,1)} fusion(bf16[2048,2048]{1,0:T(8,128)(2,1)} %constant_dynamic-update-slice_fusion.9, bf16[2048,1536]{0,1:T(8,128)(2,1)} %get-tuple-element.113, bf16[2048,1536]{0,1:T(8,128)(2,1)} %get-tuple-element.114), kind=kOutput, calls=%fused_computation.11 | convolution fusion | flops 25801261056 | bytes 33554432 | tf_op jit(solution)/shard_map/dot_general | solution.py:36
  500.0 11.1 %collective-permute-done.19 = bf16[512,2048]{1,0:T(8,128)(2,1)} collective-permute-done((bf16[512,2048]{1,0:T(8,128)(2,1)}, bf16[512,2048]{1,0:T(8,128)(2,1)}, u32[]{:S(2)}, u32[]{:S(2)}) %collective-permute-start.19) | collective-permute-done | bytes 2097184 | tf_op jit(solution)/shard_map/ppermute | solution.py:508
  517.2 19.4 %fusion.29 = bf16[1024,2048]{1,0:T(8,128)(2,1)} fusion(bf16[2048,3072]{1,0:T(8,128)(2,1)} %pad_maximum_fusion, bf16[1024,1536]{0,1:T(8,128)(2,1)S(1)} %slice.332, bf16[1024,1536]{0,1:T(8,128)(2,1)} %slice.331), kind=kOutput, calls=%fused_computation.64 | convolution fusion | flops 12899581952 | bytes 23068672 | tf_op jit(solution)/shard_map/dot_general | solution.py:42
  560.8 15.2 %convolution_convert_fusion = bf16[2048,1536]{0,1:T(8,128)(2,1)} fusion(bf16[2048,1536]{0,1:T(8,128)(2,1)S(1)} %bitcast.236, bf16[2048,2048]{1,0:T(8,128)(2,1)S(1)} %bitcast.199), kind=kOutput, calls=%fused_computation.17 | convolution fusion | flops 12888047616 | bytes 20971520 | tf_op jit(solution)/shard_map/dot_general | solution.py:36
  576.1 11.6 %convolution_convert_fusion.3 = bf16[1024,2048]{1,0:T(8,128)(2,1)} fusion(bf16[1536,2048]{1,0:T(8,128)(2,1)} %constant_dynamic-update-slice_fusion.2, bf16[2048,1536]{0,1:T(8,128)(2,1)} %get-tuple-element.119), kind=kOutput, calls=%fused_computation.63 | convolution fusion | flops 6444548096 | bytes 13631488 | tf_op jit(solution)/shard_map/dot_general | solution.py:48
  587.7 11.7 %convolution_convert_fusion.2 = bf16[1024,2048]{1,0:T(8,128)(2,1)} fusion(bf16[1536,2048]{1,0:T(8,128)(2,1)} %constant_dynamic-update-slice_fusion.2, bf16[2048,1536]{0,1:T(8,128)(2,1)} %get-tuple-element.119), kind=kOutput, calls=%fused_computation.62 | convolution fusion | flops 6444548096 | bytes 13631488 | tf_op jit(solution)/shard_map/dot_general | solution.py:48
  624.2 9.3 convolution_convert_fusion.8
  642.2 65.3 %lru_backward.1 = (bf16[2048,640]{1,0:T(8,128)(2,1)}, bf16[2048,640]{1,0:T(8,128)(2,1)}, f32[640,640]{1,0:T(8,128)S(1)}, f32[640,640]{1,0:T(8,128)S(1)}, f32[8,8,640]{2,1,0:T(8,128)S(1)}) custom-call(s32[1]{0:T(128)} %bitcast.place_ref, bf16[2048,2048]{1,0:T(8,128)(2,1)} %constant_dynamic-update-slice_fusion.6.back_ref, ...), custom_call_target="tpu_custom_call" | custom-call | flops 12079595520 | bytes 47710208 | tf_op jit(solution)/shard_map/lru_backward/pallas_call | solution.py:405
  714.3 13.4 %convolution_convert_fusion.1 = bf16[2048,1280]{1,0:T(8,128)(2,1)} fusion(bf16[2048,2048]{1,0:T(8,128)(2,1)S(1)} %bitcast.197, bf16[2048,1280]{1,0:T(8,128)(2,1)S(1)} %constant_dynamic-update-slice_fusion.4), kind=kOutput, calls=%fused_computation.18 | convolution fusion | flops 10740039680 | bytes 18874368 | tf_op jit(solution)/shard_map/dot_general | solution.py:36
  769.7 10.3 %convolution_convert_fusion.4 = bf16[1024,2048]{1,0:T(8,128)(2,1)} fusion(bf16[1280,2048]{1,0:T(8,128)(2,1)} %bitcast.202, bf16[2048,1280]{1,0:T(8,128)(2,1)} %copy-done.43), kind=kOutput, calls=%fused_computation.66 | convolution fusion | flops 5370806272 | bytes 12058624 | tf_op jit(solution)/shard_map/dot_general | solution.py:48
  789.7 24.2 %collective-permute-done.33 = bf16[2,2,40,160]{3,2,1,0:T(8,128)(2,1)S(1)} collective-permute-done((bf16[2,2,40,160]{3,2,1,0:T(8,128)(2,1)S(1)}, bf16[2,2,40,160]{3,2,1,0:T(8,128)(2,1)S(1)}, u32[]{:S(2)}, u32[]{:S(2)}) %collective-permute-start.33) | collective-permute-done | bytes 51232 | tf_op jit(solution)/shard_map/ppermute | solution.py:508
  819.7 13.8 %collective-permute-done.29 = bf16[512,2048]{1,0:T(8,128)(2,1)S(1)} collective-permute-done((bf16[512,2048]{1,0:T(8,128)(2,1)}, bf16[512,2048]{1,0:T(8,128)(2,1)S(1)}, u32[]{:S(2)}, u32[]{:S(2)}) %collective-permute-start.29) | collective-permute-done | bytes 2097184 | tf_op jit(solution)/shard_map/ppermute | solution.py:508
  874.1 13.0 %collective-permute-done.37 = bf16[512,640]{1,0:T(8,128)(2,1)S(1)} collective-permute-done((bf16[512,640]{1,0:T(8,128)(2,1)S(1)}, bf16[512,640]{1,0:T(8,128)(2,1)S(1)}, u32[]{:S(2)}, u32[]{:S(2)}) %collective-permute-start.37) | collective-permute-done | bytes 655392 | tf_op jit(solution)/shard_map/ppermute | solution.py:508
  930.7 17.5 %adam.8 = (f32[4,512,2,768]{3,2,1,0:T(2,128)}, bf16[512,2,768]{2,1,0:T(2,128)(2,1)}) custom-call(f32[1,1]{1,0:T(1,128)} %bitcast.49.refs_0_, f32[4,512,2,768]{3,2,1,0:T(2,128)} %refs_1_.4, f32[512,2,768]{2,1,0:T(2,128)S(1)} %reshape.242.refs_2_), custom_call_target="tpu_custom_call" | custom-call | flops 15728640 | bytes 29884416 | tf_op jit(solution)/shard_map/adam/pallas_call | solution.py:488
  948.3 8.2 adam.9
  (395 shorter events, 378.8 us)
Async XLA Ops:
  7.2 126.5 %all-gather.4.cloned.1.call-start = ((), (), s32[]{:S(2)}) async-start(), calls=%async_computation.4 | async-start | bytes 4915200 | tf_op jit(solution)/shard_map/all_gather | solution.py:654
  16.1 53.3 %collective-permute-start.1 = (bf16[256,2048]{1,0:T(8,128)(2,1)}, bf16[256,2048]{1,0:T(8,128)(2,1)}, u32[]{:S(2)}, u32[]{:S(2)}) collective-permute-start(bf16[256,2048]{1,0:T(8,128)(2,1)} %slice.380), channel_id=1, source_target_pairs={{0,2},{1,3},{2,0},{3,1},{4,6},{5,7},{6,4},{7,5},{8,10},{9,11},{10,... | collective-permute-start | bytes 3145736 | tf_op jit(solution)/shard_map/ppermute | solution.py:508
  70.4 243.8 %all-gather.6.cloned.1.call-start = ((), (), s32[]{:S(2)}) async-start(), calls=%async_computation.5 | async-start | bytes 7864320 | tf_op jit(solution)/shard_map/all_gather | solution.py:654
  71.8 52.4 %collective-permute-start = (bf16[512,2048]{1,0:T(8,128)(2,1)}, bf16[512,2048]{1,0:T(8,128)(2,1)}, u32[]{:S(2)}, u32[]{:S(2)}) collective-permute-start(bf16[512,2048]{1,0:T(8,128)(2,1)} %fusion.18), channel_id=1, source_target_pairs={{0,1},{1,0},{2,3},{3,2},{4,5},{5,4},{6,7},{7,6},{8,9},{9,8},{10,11... | collective-permute-start | bytes 6291464 | tf_op jit(solution)/shard_map/ppermute | solution.py:508
  121.2 73.5 %collective-permute-start.8 = (bf16[512,1536]{1,0:T(8,128)(2,1)}, bf16[512,1536]{1,0:T(8,128)(2,1)}, u32[]{:S(2)}, u32[]{:S(2)}) collective-permute-start(bf16[512,1536]{1,0:T(8,128)(2,1)} %constant_dynamic-slice_fusion.1), channel_id=1, source_target_pairs={{0,4},{1,5},{2,6},{3,7},{4,0},{5,1},{6,2},{7,3},{8,12},{9,13},{10,... | collective-permute-start | bytes 4718600 | tf_op jit(solution)/shard_map/ppermute | solution.py:508
  121.7 82.5 %collective-permute-start.7 = (bf16[512,2048]{1,0:T(8,128)(2,1)}, bf16[512,2048]{1,0:T(8,128)(2,1)}, u32[]{:S(2)}, u32[]{:S(2)}) collective-permute-start(bf16[512,2048]{1,0:T(8,128)(2,1)} %param.16), channel_id=1, source_target_pairs={{0,2},{1,3},{2,0},{3,1},{4,6},{5,7},{6,4},{7,5},{8,10},{9,11},{10,... | collective-permute-start | bytes 6291464 | tf_op jit(solution)/shard_map/ppermute | solution.py:508
  204.2 190.2 %all-gather.8.cloned.1.call-start = ((), (), s32[]{:S(2)}) async-start(), calls=%async_computation.6 | async-start | bytes 3932160 | tf_op jit(solution)/shard_map/all_gather | solution.py:654
  218.1 64.8 %collective-permute-start.11 = (bf16[512,2048]{1,0:T(8,128)(2,1)}, bf16[512,2048]{1,0:T(8,128)(2,1)}, u32[]{:S(2)}, u32[]{:S(2)}) collective-permute-start(bf16[512,2048]{1,0:T(8,128)(2,1)} %add_convert_fusion.7), channel_id=1, source_target_pairs={{0,2},{1,3},{2,0},{3,1},{4,6},{5,7},{6,4},{7,5},{8,10},{9,11},{10,... | collective-permute-start | bytes 6291464 | tf_op jit(solution)/shard_map/ppermute | solution.py:508
  225.4 57.6 %collective-permute-start.10 = (bf16[512,2048]{1,0:T(8,128)(2,1)}, bf16[512,2048]{1,0:T(8,128)(2,1)}, u32[]{:S(2)}, u32[]{:S(2)}) collective-permute-start(bf16[512,2048]{1,0:T(8,128)(2,1)} %slice.395), channel_id=1, source_target_pairs={{0,1},{1,0},{2,3},{3,2},{4,5},{5,4},{6,7},{7,6},{8,9},{9,8},{10,11... | collective-permute-start | bytes 6291464 | tf_op jit(solution)/shard_map/ppermute | solution.py:508
  226.7 54.0 %collective-permute-start.12 = (bf16[192,2048]{1,0:T(8,128)(2,1)S(1)}, bf16[192,2048]{1,0:T(8,128)(2,1)S(1)}, u32[]{:S(2)}, u32[]{:S(2)}) collective-permute-start(bf16[192,2048]{1,0:T(8,128)(2,1)S(1)} %constant_dynamic-slice_fusion), channel_id=1, source_target_pairs={{0,4},{1,5},{2,6},{3,7},{4,0},{5,1},{6,2},{7,3},{8,12},{9,13},{10,... | collective-permute-start | bytes 2359304 | tf_op jit(solution)/shard_map/ppermute | solution.py:508
  228.7 68.9 %collective-permute-start.15 = (bf16[512,2048]{1,0:T(8,128)(2,1)}, bf16[512,2048]{1,0:T(8,128)(2,1)}, u32[]{:S(2)}, u32[]{:S(2)}) collective-permute-start(bf16[512,2048]{1,0:T(8,128)(2,1)} %param.16), channel_id=1, source_target_pairs={{0,1},{1,0},{2,3},{3,2},{4,5},{5,4},{6,7},{7,6},{8,9},{9,8},{10,11... | collective-permute-start | bytes 6291464 | tf_op jit(solution)/shard_map/ppermute | solution.py:508
  228.9 72.7 %collective-permute-start.16 = (bf16[512,2048]{1,0:T(8,128)(2,1)}, bf16[512,2048]{1,0:T(8,128)(2,1)}, u32[]{:S(2)}, u32[]{:S(2)}) collective-permute-start(bf16[512,2048]{1,0:T(8,128)(2,1)} %collective-permute-done.7), channel_id=1, source_target_pairs={{0,1},{1,0},{2,3},{3,2},{4,5},{5,4},{6,7},{7,6},{8,9},{9,8},{10,11... | collective-permute-start | bytes 6291464 | tf_op jit(solution)/shard_map/ppermute | solution.py:508
  301.0 48.1 %collective-permute-start.13 = (bf16[512,2048]{1,0:T(8,128)(2,1)}, bf16[512,2048]{1,0:T(8,128)(2,1)}, u32[]{:S(2)}, u32[]{:S(2)}) collective-permute-start(bf16[512,2048]{1,0:T(8,128)(2,1)} %multiply_convert_fusion.3), channel_id=1, source_target_pairs={{0,2},{1,3},{2,0},{3,1},{4,6},{5,7},{6,4},{7,5},{8,10},{9,11},{10,... | collective-permute-start | bytes 6291464 | tf_op jit(solution)/shard_map/ppermute | solution.py:508
  351.1 282.4 %reduce-scatter.5.cloned.1.call-start = ((), (), s32[]{:S(2)}) async-start(), calls=%async_computation.7 | async-start | bytes 15728640 | tf_op jit(solution)/shard_map/reduce_scatter | solution.py:739
  463.1 48.0 %collective-permute-start.19 = (bf16[512,2048]{1,0:T(8,128)(2,1)}, bf16[512,2048]{1,0:T(8,128)(2,1)}, u32[]{:S(2)}, u32[]{:S(2)}) collective-permute-start(bf16[512,2048]{1,0:T(8,128)(2,1)} %add_convert_fusion.6), channel_id=1, source_target_pairs={{0,2},{1,3},{2,0},{3,1},{4,6},{5,7},{6,4},{7,5},{8,10},{9,11},{10,... | collective-permute-start | bytes 6291464 | tf_op jit(solution)/shard_map/ppermute | solution.py:508
  511.1 234.2 %reduce-scatter.9.cloned.1.call-start = ((), (), s32[]{:S(2)}) async-start(), calls=%async_computation.9 | async-start | bytes 7864320 | tf_op jit(solution)/shard_map/reduce_scatter | solution.py:739
  559.0 48.3 %collective-permute-start.21 = (bf16[512,2048]{1,0:T(8,128)(2,1)}, bf16[512,2048]{1,0:T(8,128)(2,1)}, u32[]{:S(2)}, u32[]{:S(2)}) collective-permute-start(bf16[512,2048]{1,0:T(8,128)(2,1)} %get-tuple-element.206), channel_id=1, source_target_pairs={{0,2},{1,3},{2,0},{3,1},{4,6},{5,7},{6,4},{7,5},{8,10},{9,11},{10,... | collective-permute-start | bytes 6291464 | tf_op jit(solution)/shard_map/ppermute | solution.py:508
  607.3 172.7 %reduce-scatter.11.cloned.1.call-start = ((), (), s32[]{:S(2)}) async-start(), calls=%async_computation.10 | async-start | bytes 3276800 | tf_op jit(solution)/shard_map/reduce_scatter | solution.py:739
  617.8 89.7 %collective-permute-start.26 = (bf16[512,2048]{1,0:T(8,128)(2,1)}, bf16[512,2048]{1,0:T(8,128)(2,1)}, u32[]{:S(2)}, u32[]{:S(2)}) collective-permute-start(bf16[512,2048]{1,0:T(8,128)(2,1)} %add_convert_fusion.3), channel_id=1, source_target_pairs={{0,2},{1,3},{2,0},{3,1},{4,6},{5,7},{6,4},{7,5},{8,10},{9,11},{10,... | collective-permute-start | bytes 6291464 | tf_op jit(solution)/shard_map/ppermute | solution.py:508
  633.4 200.1 %reduce-scatter.7.cloned.1.call-start = ((), (), s32[]{:S(2)}) async-start(), calls=%async_computation.8 | async-start | bytes 6553600 | tf_op jit(solution)/shard_map/reduce_scatter | solution.py:739
  638.1 71.1 %collective-permute-start.27 = (bf16[512,1536]{1,0:T(8,128)(2,1)}, bf16[512,1536]{1,0:T(8,128)(2,1)}, u32[]{:S(2)}, u32[]{:S(2)}) collective-permute-start(bf16[512,1536]{1,0:T(8,128)(2,1)} %pad_maximum_fusion.4), channel_id=1, source_target_pairs={{0,4},{1,5},{2,6},{3,7},{4,0},{5,1},{6,2},{7,3},{8,12},{9,13},{10,... | collective-permute-start | bytes 4718600 | tf_op jit(solution)/shard_map/ppermute | solution.py:508
  747.4 66.5 %collective-permute-start.34 = (bf16[512,768]{0,1:T(8,128)(2,1)}, bf16[512,768]{0,1:T(8,128)(2,1)}, u32[]{:S(2)}, u32[]{:S(2)}) collective-permute-start(bf16[512,768]{0,1:T(8,128)(2,1)} %slice.356), channel_id=1, source_target_pairs={{0,4},{1,5},{2,6},{3,7},{4,0},{5,1},{6,2},{7,3},{8,12},{9,13},{10,... | collective-permute-start | bytes 2359304 | tf_op jit(solution)/shard_map/ppermute | solution.py:508
  760.4 77.1 %collective-permute-start.38 = (f32[8,320]{1,0:T(8,128)S(1)}, f32[8,320]{1,0:T(8,128)S(1)}, u32[]{:S(2)}, u32[]{:S(2)}) collective-permute-start(f32[8,320]{1,0:T(8,128)S(1)} %pad_maximum_fusion.11), channel_id=1, source_target_pairs={{0,4},{1,5},{2,6},{3,7},{4,0},{5,1},{6,2},{7,3},{8,12},{9,13},{10,... | collective-permute-start | bytes 30728 | tf_op jit(solution)/shard_map/ppermute | solution.py:508
  764.4 69.1 %collective-permute-start.29 = (bf16[512,2048]{1,0:T(8,128)(2,1)}, bf16[512,2048]{1,0:T(8,128)(2,1)S(1)}, u32[]{:S(2)}, u32[]{:S(2)}) collective-permute-start(bf16[512,2048]{1,0:T(8,128)(2,1)} %add_convert_fusion.1), channel_id=1, source_target_pairs={{0,2},{1,3},{2,0},{3,1},{4,6},{5,7},{6,4},{7,5},{8,10},{9,11},{10,... | collective-permute-start | bytes 6291464 | tf_op jit(solution)/shard_map/ppermute | solution.py:508
  (111 other events, 2020.3 us)
Sparse Core Ops, SparseCore 0:
  70.5 50.6 all-gather.3
  204.4 69.2 all-gather.5
  351.2 43.2 all-gather.7
  511.2 120.7 reduce-scatter.4
  634.8 70.1 reduce-scatter.8
  707.9 39.5 reduce-scatter.10
  751.0 63.8 reduce-scatter.6

commit v3 on v2

--- a/solution.py
+++ b/solution.py
@@ -27,7 +27,8 @@
 rate_channel = 1.0
 rate_gains = 0.5
 SUB = 8
-TILE = 16
+TILE = 64
+PARTS = TILE // SUB
 GELU_SCALE = math.sqrt(2.0 / math.pi)
 GELU_CUBE = 0.044715
 
@@ -131,7 +132,7 @@
     def convolve(step, before):
         base = pl.multiple_of(step * TILE, TILE)
         halves = []
-        for half in range(2):
+        for half in range(PARTS):
             rows = pl.ds(base + half * SUB, SUB)
             now = recur_ref[rows, :]
             masks = mask_ref[rows, :]
@@ -157,7 +158,7 @@
         base = pl.multiple_of(step * TILE, TILE)
         conv = conv_ref[pl.ds(base, TILE), :].astype(jnp.float32)
         halves = []
-        for half in range(2):
+        for half in range(PARTS):
             rows = pl.ds(base + half * SUB, SUB)
             rate = jax.nn.sigmoid(rate_pre[rows, :] + par_ref[CONV + 1 : CONV + 2, :])
             admit = jax.nn.sigmoid(input_pre[rows, :] + par_ref[CONV + 2 : CONV + 3, :])
@@ -228,11 +229,10 @@
         index = steps - 1 - step
         base = pl.multiple_of(index * TILE, TILE)
         conv_tile = conv_ref[pl.ds(base, TILE), :].astype(jnp.float32)
-        halves = [None, None, None]
-        lows = [[None, None] for _ in range(3)]
+        lows = [[None] * PARTS for _ in range(3)]
         edge = pl.multiple_of(jnp.maximum(base - SUB, 0), SUB)
         earlier = jnp.where(index == 0, before_ref[...], hidden_ref[pl.ds(edge, SUB), :])
-        for half in (1, 0):
+        for half in reversed(range(PARTS)):
             rows = pl.ds(base + half * SUB, SUB)
             conv = conv_tile[half * SUB : (half + 1) * SUB, :]
             rate = rate_ref[rows, :]
@@ -254,8 +254,8 @@
             carried = carried + chain * carried_next
             carried_next = jnp.broadcast_to(carried[0:1, :], carried.shape)
             coeff_next = jnp.broadcast_to(coeff[0:1, :], coeff.shape)
-            if half == 1:
-                last = hidden_ref[pl.ds(base, SUB), :]
+            if half:
+                last = hidden_ref[pl.ds(base + (half - 1) * SUB, SUB), :]
             else:
                 last = earlier
             previous = jnp.where(row == 0, roll_down(last, 1), roll_down(hidden, 1))
@@ -293,9 +293,9 @@
 
     def unconvolve(step, carry):
         base = pl.multiple_of((steps - 1 - step) * TILE, TILE)
-        halves = [None, None]
+        halves = [None] * PARTS
         nexts = list(carry)
-        for half in (1, 0):
+        for half in reversed(range(PARTS)):
             rows = pl.ds(base + half * SUB, SUB)
             grad = conv_back[rows, :]
             now = recur_ref[rows, :]
@@ -479,7 +479,7 @@
 
 def adam_matrix(state, gradient, factor, step_rate, decay_use):
     rows, rest = gradient.shape[0], gradient.shape[1:]
-    goal = max(16, 2**16 // math.prod(rest))
+    goal = max(16, 2**17 // math.prod(rest))
     fits = [b for b in range(16, rows + 1, 16) if rows % b == 0 and (b <= goal or b == 16)]
     block = max(fits, default=rows)
     zeros = (0,) * len(rest)
@@ -524,19 +524,9 @@
     return terms[0]
 
 
-def sum_over_all(values):
-    values = values + swap(values, "chan", 1)
-    for axis, step in (("chan", 2), ("seq", 1)):
-        others = range(step, lax.axis_size(axis), step)
-        values = tree_sum([values] + [swap(values, axis, other) for other in others])
-    return values
-
-
-def sum_by_steps(values, axes):
-    for axis in axes:
-        for bit in bits_of(lax.axis_size(axis)):
-            values = values + swap(values, axis, bit)
-    return values
+def sum_over(values, axis, step=1):
+    others = range(step, lax.axis_size(axis), step)
+    return tree_sum([values] + [swap(values, axis, other) for other in others])
 
 
 def both(*values):
@@ -589,10 +579,14 @@
     return [part[: part.shape[0] // 2] for part in parts]
 
 
-def scatter_start(product, parts, size, piece):
+def scatter_start(product, parts, size, piece, first=0):
     far = product(*rows_far(parts)).astype(jnp.bfloat16)
     total, came = scatter_near(far, piece)
-    return swap(total, "chan", size // 2), came, far
+    if first:
+        sent = [swap(rows, "chan", size // 2) for rows in (total[:first], total[first:])]
+    else:
+        sent = swap(total, "chan", size // 2)
+    return sent, came, far
 
 
 def scatter_end(arrived, near, piece):
@@ -668,16 +662,19 @@
         )
     )
     half = piece // 2
-    normed_top, first_part = both(swap(normed_one[:half], "chan", side), first_part)
+    own_expand = expand_weights.reshape(width, 2 * hidden_width)
+    normed_near = lay_rows(gather_blocks(normed_one, side), 2)
+    normed_top, first_part, own_expand, normed_near = both(
+        swap(normed_one[:half], "chan", side), first_part, own_expand, normed_near
+    )
     others = share(first_part)
     other_branch = others[: 2 * chan_width].reshape(own_branch.shape)
     other_mixer = others[2 * chan_width :]
     branch_full = jnp.concatenate([own_branch, other_branch], axis=1)
     normed_end = swap(later(normed_one, normed_top)[half:], "chan", side)
     normed_far = gather_blocks(jnp.concatenate([normed_top, normed_end], axis=0), side)
-    normed_all = lay_rows(gather_blocks(normed_one, side) + normed_far)
+    normed_all = lay_more(normed_near, normed_far)
     back_far = swap(later(cotangent, normed_end), "chan", side)
-    own_expand = expand_weights.reshape(width, 2 * hidden_width)
     expand_part = fetch_part(later(own_expand, normed_end))
     shrink_part = fetch_part(later(shrink_weights, normed_end))
     pair_width = 2 * hidden_width
@@ -766,8 +763,8 @@
     product_low = later(product_low, shrink_local)
     out_arrived, _, out_far = scatter_start(through_shrink, [product_low], group, piece)
     out_near = through_shrink(*rows_near([later(product_low, out_far)])).astype(jnp.bfloat16)
-    middle_far, shrink_local, middle_near, out_near = both(
-        swap(middle_low, "chan", side), shrink_local, middle_near, out_near
+    middle_far, shrink_local, middle_near, out_near, mixer_full = both(
+        swap(middle_low, "chan", side), shrink_local, middle_near, out_near, mixer_full
     )
     shrink_sum = reduce_seq(shrink_local)
     branch_back = lay_more(middle_near, gather_blocks(middle_far, side))
@@ -791,46 +788,34 @@
     gate_back, out_arrived, expand_theirs = both(gate_back, out_arrived, expand_pair[1])
     expand_pair = (expand_pair[0], expand_theirs)
     branch_back_low = jnp.concatenate([gate_back, recur_back], axis=1)
+    through_branch = lambda left: contract(left, branch_full.reshape(4 * chan_width, width))
     branch_local = contract_rows(normed_all, branch_back_low).astype(jnp.bfloat16)
-    branch_sum = reduce_seq(branch_local)
-    through_branch = lambda left: contract(left, branch_full.reshape(4 * chan_width, width))
     branch_back_low = later(branch_back_low, branch_local)
-    arrived, came, far = scatter_start(through_branch, [branch_back_low], group, piece)
-    branch_back_low, *_ = both(branch_back_low, *came)
-    shrink_pair = settle(later(shrink_sum, far), 1, hidden_width)
-    near = through_branch(*rows_near([branch_back_low])).astype(jnp.bfloat16)
-    mixer_pair = settle(later(mixer_sum, near), 1, chan_width)
-    rate_w_grad, input_w_grad, sums = (
-        later(rate_w_grad, far), later(input_w_grad, far), later(sums, far)
-    )
+    arrived, _, far = scatter_start(through_branch, [branch_back_low], group, piece, TILE)
+    branch_back_low, arrived[0] = both(branch_back_low, arrived[0])
+    arrived = jnp.concatenate(arrived, axis=0)
     block_size = gate_blocks.shape[2]
+    part_rows = width // seq_count
     gate_pair = jnp.stack(
         [
             diagonal_blocks(rate_w_grad, 2 * block_count),
             diagonal_blocks(input_w_grad, 2 * block_count),
         ]
-    )
-    gate_pair = gate_pair.reshape(
-        2, 2 * block_count, seq_count, block_size // seq_count, block_size
-    )
-
-    def gate_rows(other):
-        rows = lax.dynamic_index_in_dim(gate_pair, seq_place ^ other, axis=2, keepdims=False)
-        return swap(rows.astype(jnp.bfloat16), "seq", other).astype(jnp.float32) if other else rows
-
-    gate_part = sum(gate_rows(other) for other in range(seq_count))
-    gate_theirs = partner(gate_part[:, block_count:].astype(jnp.bfloat16))
-    branch_sum, near, arrived, gate_theirs, shrink_theirs, mixer_theirs = both(
-        branch_sum, near, arrived, gate_theirs, shrink_pair[1], mixer_pair[1]
-    )
-    mixer_pair = (mixer_pair[0], mixer_theirs)
-    shrink_pair = (shrink_pair[0], shrink_theirs)
-    output = (middle + scatter_end(out_arrived, out_near, piece)).astype(jnp.bfloat16)
-    normed_one_grad = scatter_end(arrived, near, piece)
-    gain_one = jnp.sum(normed_one_grad * rows_float * scale_one, axis=0)
-    residual_grad = middle_grad + norm_back(rows_float, scale_one, gain_first, normed_one_grad)
-    gains_grad = sum_by_steps(jnp.stack([gain_one, gain_two]), ("seq", "chan"))
-
+    ).astype(jnp.bfloat16)
+    gate_parts = (2, 2, block_count, seq_count, block_size // seq_count, block_size)
+    gate_pair = gate_pair.reshape(gate_parts).transpose(3, 1, 0, 2, 4, 5)
+    gate_shape = gate_pair.shape[1:]
+    gate_count = math.prod(gate_shape[:-1])
+    gate_rows = jnp.pad(
+        gate_pair.reshape(seq_count, gate_count, block_size),
+        ((0, 0), (0, part_rows - gate_count), (0, 0)),
+    ).reshape(width, block_size)
+    branch_sum = reduce_seq(jnp.concatenate([branch_local, gate_rows], axis=1))
+    shrink_pair = settle(later(shrink_sum, branch_local), 1, hidden_width)
+    near = through_branch(*rows_near([branch_back_low])).astype(jnp.bfloat16)
+    mixer_pair = settle(later(mixer_sum, near), 1, chan_width)
+    sums = later(sums, branch_local)
+    expand_grad = total(expand_pair).reshape(-1, 2, hidden_width)
     channel_pair = jnp.sum(sums, axis=1)
     channel_pair = jnp.concatenate(
         [
@@ -839,26 +824,54 @@
         ],
         axis=0,
     )
-    channel_grad = sum_by_steps(
-        channel_pair[:, :chan_width] + partner(channel_pair[:, chan_width:]), ("seq",)
-    )
+    channel_own = channel_pair[:, :chan_width] + partner(channel_pair[:, chan_width:])
+    output = (middle + scatter_end(out_arrived, out_near, piece)).astype(jnp.bfloat16)
+    normed_one_grad = scatter_end(arrived, near, piece)
+    gain_one = jnp.sum(normed_one_grad * rows_float * scale_one, axis=0)
+    residual_grad = middle_grad + norm_back(rows_float, scale_one, gain_first, normed_one_grad)
+    (
+        branch_sum, residual_grad, gain_one, gain_two, output, channel_own, shrink_theirs,
+        mixer_theirs, expand_grad,
+    ) = both(
+        branch_sum, residual_grad, gain_one, gain_two, output, channel_own, shrink_pair[1],
+        mixer_pair[1], expand_grad,
+    )
+    mixer_pair = (mixer_pair[0], mixer_theirs)
+    shrink_pair = (shrink_pair[0], shrink_theirs)
+    gate_part = branch_sum[:gate_count, 4 * chan_width :].reshape(gate_shape)
+    gate_pair = (gate_part[0], partner(gate_part[1]))
+    branch_pair = settle(branch_sum[:, : 4 * chan_width], 2, chan_width)
     shrink_grad = total(shrink_pair).T
-    expand_grad = lax.optimization_barrier(
-        total(expand_pair).reshape(-1, 2, hidden_width)
-    )
     mixer_grad = total(mixer_pair).T
-    branch_grad = total(settle(branch_sum, 2, chan_width)).reshape(-1, 2, chan_width)
-    gate_grad = gate_part[:, :block_count] + gate_theirs.astype(jnp.float32)
+    branch_grad = total(branch_pair).reshape(-1, 2, chan_width)
+    gate_grad = total(gate_pair)
     grad_shards = (branch_grad, gate_grad, mixer_grad, expand_grad, shrink_grad)
     own_squares = sum((jnp.sum(shard_grad * shard_grad) for shard_grad in grad_shards))
-    own_squares = own_squares + jnp.where(
-        seq_place == 0, jnp.sum(channel_grad * channel_grad), 0.0
-    )
-    total_squares = sum_over_all(own_squares.reshape(1))[0]
-    grad_norm = jnp.sqrt(total_squares + jnp.sum(gains_grad * gains_grad))
+    lanes = 128
+    packed = sum_over(
+        jnp.concatenate(
+            [
+                gain_one,
+                gain_two,
+                jnp.full((lanes,), own_squares),
+                channel_own.reshape(-1),
+            ]
+        ),
+        "seq",
+    )
+    channel_grad = packed[2 * width + lanes :].reshape(channel_own.shape)
+    packed = jnp.concatenate(
+        [
+            packed[: 2 * width],
+            packed[2 * width : 2 * width + lanes] + jnp.sum(channel_grad * channel_grad),
+        ]
+    )
+    packed = packed + swap(packed, "chan", 1)
+    packed = sum_over(packed, "chan", 2)
+    gains_grad = packed[: 2 * width].reshape(2, width)
+    grad_norm = jnp.sqrt(packed[2 * width] + jnp.sum(gains_grad * gains_grad))
     clip_limit = clip_rms * math.sqrt(PARAMS)
     factor = jnp.minimum(1.0, clip_limit / (grad_norm + 1e-06))
-    part_rows = width // seq_count
 
     def rows_of_branch(values):
         return jnp.moveaxis(values, -3, -1).reshape(values.shape[:-3] + (2 * chan_width, part_rows))

time: 985 us -> 956 us (0.971)
  Pallas kernels: 156 us -> 134 us
  starting transfers between devices: 60.5 us -> 41.9 us
  waiting for transfers between devices: 261 us -> 272 us
  other arithmetic: 91.1 us -> 101 us
    ppermute x53 -> x44, starting transfers between devices: 59.8 us -> 41.1 us  [swap(): lax.ppermute(values, axis, [(i, i ^ bit) for i in range(lax.axis_size(axi...]
    ppermute x53 -> x44, waiting for transfers between devices: 258 us -> 266 us  [swap(): lax.ppermute(values, axis, [(i, i ^ bit) for i in range(lax.axis_size(axi...]
    unnamed x154 -> x140, local copies, waits for them, and re-layouts: 31 us -> 27.8 us
  transfers between devices with their start and end apart: 60 -> 51, of which waited for: 25 -> 28; matrix products, arithmetic and copies ran while one was open for 39% -> 39% of each run, Pallas kernels for 12% -> 11%
where the time goes in v3:
time: 956 us; the launch traced here: 946 us
  waiting for transfers between devices  272 us (28%)
  matrix products  225 us (24%)
  local copies, waits for them, and re-layouts  152 us (16%)
  Pallas kernels  134 us (14%)
  other arithmetic  101 us (11%)
  starting transfers between devices  41.9 us (4%)
  between operations  21.1 us (2%)
    ppermute x44, waiting for transfers between devices, swap(): lax.ppermute(values, axis, [(i, i ^ bit) for i in range(lax.axis_size(axi...  266 us
    dot_general x7, matrix products, contract(): return jnp.dot(left_mat, right_mat, preferred_element_type=jnp.float32)  80.5 us
    dot_general x4, matrix products, contract_rows(): lax.dot_general(left_mat, right_mat, (((0,), (0,)), ((), ())), preferred_...  74.1 us
    dot_general x3, matrix products, contract_cols(): lax.dot_general(left_mat, right_mat, (((1,), (1,)), ((), ())), preferred_...  70.7 us
    dynamic_update_slice x17, local copies, waits for them, and re-layouts, lay_more(): whole = lax.dynamic_update_slice_in_dim(whole, block, start, axis=0)  59.1 us
    pallas_call x1, Pallas kernels, lru_backward(): pl.pallas_call(lru_backward_kernel, grid_spec=pltpu.PrefetchScalarGridSpe...  56.9 us
    pallas_call x1, Pallas kernels, lru_forward(): pl.pallas_call(lru_forward_kernel, grid_spec=pltpu.PrefetchScalarGridSpec...  45.6 us
    ppermute x44, starting transfers between devices, swap(): lax.ppermute(values, axis, [(i, i ^ bit) for i in range(lax.axis_size(axi...  41.1 us
  transfers between devices with their start and end apart: 51, of which 28 were waited for; matrix products, arithmetic and copies ran while one was open for 39% of the time, Pallas kernels for 11%

profile of v3, /device:TPU:0, one launch (start us, length us, event | category | flops | bytes accessed | tf_op | source)
XLA Modules:
  0.0 946.4 jit_solution(457783145199814440)
XLA Ops:
  40.3 29.9 %collective-permute-done.1 = bf16[240,2048]{1,0:T(8,128)(2,1)S(1)} collective-permute-done((bf16[240,2048]{1,0:T(8,128)(2,1)S(1)}, bf16[240,2048]{1,0:T(8,128)(2,1)S(1)}, u32[]{:S(2)}, u32[]{:S(2)}) %collective-permute-start.1) | collective-permute-done | bytes 983072 | tf_op jit(solution)/shard_map/ppermute | solution.py:508
  78.7 25.6 %collective-permute-done.3 = bf16[256,2048]{1,0:T(8,128)(2,1)S(1)} collective-permute-done((bf16[256,2048]{1,0:T(8,128)(2,1)S(1)}, bf16[256,2048]{1,0:T(8,128)(2,1)S(1)}, u32[]{:S(2)}, u32[]{:S(2)}) %collective-permute-start.3) | collective-permute-done | bytes 1048608 | tf_op jit(solution)/shard_map/ppermute | solution.py:508
  127.4 45.6 %lru_forward.1 = (bf16[2048,640]{1,0:T(8,128)(2,1)S(1)}, f32[2048,640]{1,0:T(8,128)}, f32[2048,640]{1,0:T(8,128)}, f32[2048,640]{1,0:T(8,128)}, bf16[2048,640]{1...) custom-call(s32[1]{0:T(128)} %bitcast.3.place_ref, ...), custom_call_target="tpu_custom_call" | custom-call | flops 14092861440 | bytes 42467328 | tf_op jit(solution)/shard_map/lru_forward/pallas_call | solution.py:347
  181.4 11.4 %collective-permute-done.7 = bf16[512,2048]{1,0:T(8,128)(2,1)} collective-permute-done((bf16[512,2048]{1,0:T(8,128)(2,1)}, bf16[512,2048]{1,0:T(8,128)(2,1)}, u32[]{:S(2)}, u32[]{:S(2)}) %collective-permute-start.7) | collective-permute-done | bytes 2097184 | tf_op jit(solution)/shard_map/ppermute | solution.py:508
  217.8 51.5 %collective-permute-done.12 = bf16[192,2048]{1,0:T(8,128)(2,1)S(1)} collective-permute-done((bf16[192,2048]{1,0:T(8,128)(2,1)S(1)}, bf16[192,2048]{1,0:T(8,128)(2,1)S(1)}, u32[]{:S(2)}, u32[]{:S(2)}) %collective-permute-start.12) | collective-permute-done | bytes 786464 | tf_op jit(solution)/shard_map/ppermute | solution.py:508
  313.2 24.6 %collective-permute-done.13 = bf16[512,2048]{1,0:T(8,128)(2,1)} collective-permute-done((bf16[512,2048]{1,0:T(8,128)(2,1)}, bf16[512,2048]{1,0:T(8,128)(2,1)}, u32[]{:S(2)}, u32[]{:S(2)}) %collective-permute-start.13) | collective-permute-done | bytes 2097184 | tf_op jit(solution)/shard_map/ppermute | solution.py:508
  346.3 34.4 %fusion.85 = f32[2048,3072]{0,1:T(8,128)} fusion(bf16[2048,2048]{1,0:T(8,128)(2,1)} %constant_dynamic-update-slice_fusion.9, bf16[2048,3072]{1,0:T(8,128)(2,1)} %pad_maximum_fusion), kind=kOutput, calls=%fused_computation.220 | convolution fusion | flops 25769803776 | bytes 46137344 | tf_op jit(solution)/shard_map/dot_general | solution.py:49
  387.1 31.9 %multiply_convert_fusion.2 = (bf16[2048,1536]{0,1:T(8,128)(2,1)}, bf16[2048,1536]{0,1:T(8,128)(2,1)}, bf16[2048,1536]{0,1:T(8,128)(2,1)}) fusion(f32[2048,3072]{0,1:T(8,128)} %fusion.85, bf16[2048,2048]{1,0:T(8,128)(2,1)} %copy-done.24, bf16[1536,2048]{1,0:T(8,128)(2,1)} %constant_dynamic-update-slice_fusion.2), kind=kOutput, calls=%fused_computation.7 | convolution fusion | flops 12960399360 | bytes 58720256 | tf_op jit(solution)/shard_map/dot_general | solution.py:43
  424.8 18.8 %fusion.32 = bf16[1024,2048]{1,0:T(8,128)(2,1)} fusion(bf16[2048,3072]{1,0:T(8,128)(2,1)} %pad_maximum_fusion, bf16[1024,1536]{0,1:T(8,128)(2,1)} %slice.447, bf16[1024,1536]{0,1:T(8,128)(2,1)S(1)} %slice.446), kind=kOutput, calls=%fused_computation.66 | convolution fusion | flops 12899581952 | bytes 23068672 | tf_op jit(solution)/shard_map/dot_general | solution.py:43
  453.3 35.6 %fusion.5 = bf16[2048,3072]{1,0:T(8,128)(2,1)} fusion(bf16[2048,2048]{1,0:T(8,128)(2,1)} %constant_dynamic-update-slice_fusion.9, bf16[2048,1536]{0,1:T(8,128)(2,1)} %get-tuple-element.120, bf16[2048,1536]{0,1:T(8,128)(2,1)} %get-tuple-element.121), kind=kOutput, calls=%fused_computation.11 | convolution fusion | flops 25801261056 | bytes 33554432 | tf_op jit(solution)/shard_map/dot_general | solution.py:37
  488.9 10.9 %collective-permute-done.19 = bf16[512,2048]{1,0:T(8,128)(2,1)} collective-permute-done((bf16[512,2048]{1,0:T(8,128)(2,1)}, bf16[512,2048]{1,0:T(8,128)(2,1)}, u32[]{:S(2)}, u32[]{:S(2)}) %collective-permute-start.19) | collective-permute-done | bytes 2097184 | tf_op jit(solution)/shard_map/ppermute | solution.py:508
  507.7 20.1 %fusion.29 = bf16[1024,2048]{1,0:T(8,128)(2,1)} fusion(bf16[2048,3072]{1,0:T(8,128)(2,1)} %pad_maximum_fusion, bf16[1024,1536]{0,1:T(8,128)(2,1)} %slice.370, bf16[1024,1536]{0,1:T(8,128)(2,1)} %slice.369), kind=kOutput, calls=%fused_computation.65 | convolution fusion | flops 12899581952 | bytes 23068672 | tf_op jit(solution)/shard_map/dot_general | solution.py:43
  552.5 15.2 %convolution_convert_fusion = bf16[2048,1536]{0,1:T(8,128)(2,1)} fusion(bf16[2048,1536]{0,1:T(8,128)(2,1)S(1)} %bitcast.150, bf16[2048,2048]{1,0:T(8,128)(2,1)S(1)} %bitcast.118), kind=kOutput, calls=%fused_computation.17 | convolution fusion | flops 12888047616 | bytes 20971520 | tf_op jit(solution)/shard_map/dot_general | solution.py:37
  567.8 11.7 %convolution_convert_fusion.3 = bf16[1024,2048]{1,0:T(8,128)(2,1)} fusion(bf16[1536,2048]{1,0:T(8,128)(2,1)} %constant_dynamic-update-slice_fusion.2, bf16[2048,1536]{0,1:T(8,128)(2,1)} %get-tuple-element.126), kind=kOutput, calls=%fused_computation.64 | convolution fusion | flops 6444548096 | bytes 13631488 | tf_op jit(solution)/shard_map/dot_general | solution.py:49
  579.4 11.6 %convolution_convert_fusion.2 = bf16[1024,2048]{1,0:T(8,128)(2,1)} fusion(bf16[1536,2048]{1,0:T(8,128)(2,1)} %constant_dynamic-update-slice_fusion.2, bf16[2048,1536]{0,1:T(8,128)(2,1)} %get-tuple-element.126), kind=kOutput, calls=%fused_computation.63 | convolution fusion | flops 6444548096 | bytes 13631488 | tf_op jit(solution)/shard_map/dot_general | solution.py:49
  615.9 9.4 convolution_convert_fusion.8
  632.2 56.9 %lru_backward.1 = (bf16[2048,640]{1,0:T(8,128)(2,1)}, bf16[2048,640]{1,0:T(8,128)(2,1)}, f32[640,640]{1,0:T(8,128)S(1)}, f32[640,640]{1,0:T(8,128)S(1)}, f32[8,8,640]{2,1,0:T(8,128)S(1)}) custom-call(s32[1]{0:T(128)} %bitcast.3.place_ref, bf16[2048,2048]{1,0:T(8,128)(2,1)} %constant_dynamic-update-slice_fusion.6.back_ref, ...), custom_call_target="tpu_custom_call" | custom-call | flops 12079595520 | bytes 47710208 | tf_op jit(solution)/shard_map/lru_backward/pallas_call | solution.py:405
  690.6 10.4 %collective-permute-done.26 = bf16[512,1536]{1,0:T(8,128)(2,1)} collective-permute-done((bf16[512,1536]{1,0:T(8,128)(2,1)}, bf16[512,1536]{1,0:T(8,128)(2,1)}, u32[]{:S(2)}, u32[]{:S(2)}) %collective-permute-start.26) | collective-permute-done | bytes 1572896 | tf_op jit(solution)/shard_map/ppermute | solution.py:508
  705.7 13.9 %convolution_convert_fusion.1 = bf16[2048,1280]{0,1:T(8,128)(2,1)S(1)} fusion(bf16[2048,2048]{1,0:T(8,128)(2,1)} %constant_dynamic-update-slice_fusion.15.normed_ref, bf16[2048,1280]{1,0:T(8,128)(2,1)S(1)} %constant_dynamic-update-slice_fusion.4), kind=kOutput, calls=%fused_computation.18 | convolution fusion | flops 10740039680 | bytes 18874368 | tf_op jit(solution)/shard_map/dot_general | solution.py:37
  740.3 8.3 collective-permute-done.28
  780.4 20.2 %collective-permute-done.32 = f32[8,320]{1,0:T(8,128)S(1)} collective-permute-done((f32[8,320]{1,0:T(8,128)S(1)}, f32[8,320]{1,0:T(8,128)S(1)}, u32[]{:S(2)}, u32[]{:S(2)}) %collective-permute-start.32) | collective-permute-done | bytes 10272 | tf_op jit(solution)/shard_map/ppermute | solution.py:508
  805.7 13.8 %collective-permute-done.30 = bf16[448,2048]{1,0:T(8,128)(2,1)} collective-permute-done((bf16[448,2048]{1,0:T(8,128)(2,1)}, bf16[448,2048]{1,0:T(8,128)(2,1)}, u32[]{:S(2)}, u32[]{:S(2)}) %collective-permute-start.30) | collective-permute-done | bytes 1835040 | tf_op jit(solution)/shard_map/ppermute | solution.py:508
  855.3 17.6 %collective-permute-done.35 = bf16[512,640]{0,1:T(8,128)(2,1)} collective-permute-done((bf16[512,640]{0,1:T(8,128)(2,1)}, bf16[512,640]{0,1:T(8,128)(2,1)}, u32[]{:S(2)}, u32[]{:S(2)}) %collective-permute-start.35) | collective-permute-done | bytes 655392 | tf_op jit(solution)/shard_map/ppermute | solution.py:508
  906.5 14.1 %adam.8 = (f32[4,512,2,768]{3,2,1,0:T(2,128)}, bf16[512,2,768]{2,1,0:T(2,128)(2,1)}) custom-call(f32[1,1]{1,0:T(1,128)} %bitcast.41.refs_0_, f32[4,512,2,768]{3,2,1,0:T(2,128)} %refs_1_.4, f32[512,2,768]{2,1,0:T(2,128)S(1)} %reshape.287.refs_2_), custom_call_target="tpu_custom_call" | custom-call | flops 15728640 | bytes 29884416 | tf_op jit(solution)/shard_map/adam/pallas_call | solution.py:488
  (383 shorter events, 382.1 us)
Async XLA Ops:
  7.2 114.8 %all-gather.4.cloned.1.call-start = ((), (), s32[]{:S(2)}) async-start(), calls=%async_computation.4 | async-start | bytes 4915200 | tf_op jit(solution)/shard_map/all_gather | solution.py:648
  16.6 53.7 %collective-permute-start = (bf16[256,2048]{1,0:T(8,128)(2,1)}, bf16[256,2048]{1,0:T(8,128)(2,1)}, u32[]{:S(2)}, u32[]{:S(2)}) collective-permute-start(bf16[256,2048]{1,0:T(8,128)(2,1)} %slice.425), channel_id=1, source_target_pairs={{0,2},{1,3},{2,0},{3,1},{4,6},{5,7},{6,4},{7,5},{8,10},{9,11},{10,... | collective-permute-start | bytes 3145736 | tf_op jit(solution)/shard_map/ppermute | solution.py:508
  24.2 46.0 %collective-permute-start.1 = (bf16[240,2048]{1,0:T(8,128)(2,1)S(1)}, bf16[240,2048]{1,0:T(8,128)(2,1)S(1)}, u32[]{:S(2)}, u32[]{:S(2)}) collective-permute-start(bf16[240,2048]{1,0:T(8,128)(2,1)S(1)} %constant_dynamic-slice_fusion.2), channel_id=1, source_target_pairs={{0,4},{1,5},{2,6},{3,7},{4,0},{5,1},{6,2},{7,3},{8,12},{9,13},{10,... | collective-permute-start | bytes 2949128 | tf_op jit(solution)/shard_map/ppermute | solution.py:508
  71.2 231.6 %all-gather.6.cloned.1.call-start = ((), (), s32[]{:S(2)}) async-start(), calls=%async_computation.5 | async-start | bytes 7864320 | tf_op jit(solution)/shard_map/all_gather | solution.py:648
  109.8 71.7 %collective-permute-start.8 = (bf16[512,1536]{1,0:T(8,128)(2,1)}, bf16[512,1536]{1,0:T(8,128)(2,1)}, u32[]{:S(2)}, u32[]{:S(2)}) collective-permute-start(bf16[512,1536]{1,0:T(8,128)(2,1)} %constant_dynamic-slice_fusion.1), channel_id=1, source_target_pairs={{0,4},{1,5},{2,6},{3,7},{4,0},{5,1},{6,2},{7,3},{8,12},{9,13},{10,... | collective-permute-start | bytes 4718600 | tf_op jit(solution)/shard_map/ppermute | solution.py:508
  110.3 82.5 %collective-permute-start.7 = (bf16[512,2048]{1,0:T(8,128)(2,1)}, bf16[512,2048]{1,0:T(8,128)(2,1)}, u32[]{:S(2)}, u32[]{:S(2)}) collective-permute-start(bf16[512,2048]{1,0:T(8,128)(2,1)} %param.16), channel_id=1, source_target_pairs={{0,2},{1,3},{2,0},{3,1},{4,6},{5,7},{6,4},{7,5},{8,10},{9,11},{10,... | collective-permute-start | bytes 6291464 | tf_op jit(solution)/shard_map/ppermute | solution.py:508
  192.8 190.2 %all-gather.8.cloned.1.call-start = ((), (), s32[]{:S(2)}) async-start(), calls=%async_computation.6 | async-start | bytes 3932160 | tf_op jit(solution)/shard_map/all_gather | solution.py:648
  206.7 64.8 %collective-permute-start.11 = (bf16[512,2048]{1,0:T(8,128)(2,1)}, bf16[512,2048]{1,0:T(8,128)(2,1)}, u32[]{:S(2)}, u32[]{:S(2)}) collective-permute-start(bf16[512,2048]{1,0:T(8,128)(2,1)} %add_convert_fusion.7), channel_id=1, source_target_pairs={{0,2},{1,3},{2,0},{3,1},{4,6},{5,7},{6,4},{7,5},{8,10},{9,11},{10,... | collective-permute-start | bytes 6291464 | tf_op jit(solution)/shard_map/ppermute | solution.py:508
  214.0 57.6 %collective-permute-start.10 = (bf16[512,2048]{1,0:T(8,128)(2,1)}, bf16[512,2048]{1,0:T(8,128)(2,1)}, u32[]{:S(2)}, u32[]{:S(2)}) collective-permute-start(bf16[512,2048]{1,0:T(8,128)(2,1)} %slice.440), channel_id=1, source_target_pairs={{0,1},{1,0},{2,3},{3,2},{4,5},{5,4},{6,7},{7,6},{8,9},{9,8},{10,11... | collective-permute-start | bytes 6291464 | tf_op jit(solution)/shard_map/ppermute | solution.py:508
  215.3 54.0 %collective-permute-start.12 = (bf16[192,2048]{1,0:T(8,128)(2,1)S(1)}, bf16[192,2048]{1,0:T(8,128)(2,1)S(1)}, u32[]{:S(2)}, u32[]{:S(2)}) collective-permute-start(bf16[192,2048]{1,0:T(8,128)(2,1)S(1)} %constant_dynamic-slice_fusion), channel_id=1, source_target_pairs={{0,4},{1,5},{2,6},{3,7},{4,0},{5,1},{6,2},{7,3},{8,12},{9,13},{10,... | collective-permute-start | bytes 2359304 | tf_op jit(solution)/shard_map/ppermute | solution.py:508
  217.3 65.8 %collective-permute-start.15 = (bf16[512,2048]{1,0:T(8,128)(2,1)}, bf16[512,2048]{1,0:T(8,128)(2,1)}, u32[]{:S(2)}, u32[]{:S(2)}) collective-permute-start(bf16[512,2048]{1,0:T(8,128)(2,1)} %param.16), channel_id=1, source_target_pairs={{0,1},{1,0},{2,3},{3,2},{4,5},{5,4},{6,7},{7,6},{8,9},{9,8},{10,11... | collective-permute-start | bytes 6291464 | tf_op jit(solution)/shard_map/ppermute | solution.py:508
  217.5 72.7 %collective-permute-start.16 = (bf16[512,2048]{1,0:T(8,128)(2,1)}, bf16[512,2048]{1,0:T(8,128)(2,1)}, u32[]{:S(2)}, u32[]{:S(2)}) collective-permute-start(bf16[512,2048]{1,0:T(8,128)(2,1)} %collective-permute-done.7), channel_id=1, source_target_pairs={{0,1},{1,0},{2,3},{3,2},{4,5},{5,4},{6,7},{7,6},{8,9},{9,8},{10,11... | collective-permute-start | bytes 6291464 | tf_op jit(solution)/shard_map/ppermute | solution.py:508
  289.6 48.1 %collective-permute-start.13 = (bf16[512,2048]{1,0:T(8,128)(2,1)}, bf16[512,2048]{1,0:T(8,128)(2,1)}, u32[]{:S(2)}, u32[]{:S(2)}) collective-permute-start(bf16[512,2048]{1,0:T(8,128)(2,1)} %multiply_convert_fusion.3), channel_id=1, source_target_pairs={{0,2},{1,3},{2,0},{3,1},{4,6},{5,7},{6,4},{7,5},{8,10},{9,11},{10,... | collective-permute-start | bytes 6291464 | tf_op jit(solution)/shard_map/ppermute | solution.py:508
  339.7 285.7 %reduce-scatter.5.cloned.1.call-start = ((), (), s32[]{:S(2)}) async-start(), calls=%async_computation.7 | async-start | bytes 15728640 | tf_op jit(solution)/shard_map/reduce_scatter | solution.py:736
  451.8 48.0 %collective-permute-start.19 = (bf16[512,2048]{1,0:T(8,128)(2,1)}, bf16[512,2048]{1,0:T(8,128)(2,1)}, u32[]{:S(2)}, u32[]{:S(2)}) collective-permute-start(bf16[512,2048]{1,0:T(8,128)(2,1)} %add_convert_fusion.6), channel_id=1, source_target_pairs={{0,2},{1,3},{2,0},{3,1},{4,6},{5,7},{6,4},{7,5},{8,10},{9,11},{10,... | collective-permute-start | bytes 6291464 | tf_op jit(solution)/shard_map/ppermute | solution.py:508
  499.8 277.2 %reduce-scatter.9.cloned.1.call-start = ((), (), s32[]{:S(2)}) async-start(), calls=%async_computation.9 | async-start | bytes 7864320 | tf_op jit(solution)/shard_map/reduce_scatter | solution.py:736
  550.6 48.1 %collective-permute-start.21 = (bf16[512,2048]{1,0:T(8,128)(2,1)}, bf16[512,2048]{1,0:T(8,128)(2,1)}, u32[]{:S(2)}, u32[]{:S(2)}) collective-permute-start(bf16[512,2048]{1,0:T(8,128)(2,1)} %get-tuple-element.191), channel_id=1, source_target_pairs={{0,2},{1,3},{2,0},{3,1},{4,6},{5,7},{6,4},{7,5},{8,10},{9,11},{10,... | collective-permute-start | bytes 6291464 | tf_op jit(solution)/shard_map/ppermute | solution.py:508
  598.7 202.5 %reduce-scatter.11.cloned.1.call-start = ((), (), s32[]{:S(2)}) async-start(), calls=%async_computation.10 | async-start | bytes 3276800 | tf_op jit(solution)/shard_map/reduce_scatter | solution.py:736
  609.6 81.0 %collective-permute-start.25 = (bf16[512,2048]{1,0:T(8,128)(2,1)}, bf16[512,2048]{1,0:T(8,128)(2,1)}, u32[]{:S(2)}, u32[]{:S(2)}) collective-permute-start(bf16[512,2048]{1,0:T(8,128)(2,1)} %add_convert_fusion.4), channel_id=1, source_target_pairs={{0,2},{1,3},{2,0},{3,1},{4,6},{5,7},{6,4},{7,5},{8,10},{9,11},{10,... | collective-permute-start | bytes 6291464 | tf_op jit(solution)/shard_map/ppermute | solution.py:508
  625.3 208.5 %reduce-scatter.7.cloned.1.call-start = ((), (), s32[]{:S(2)}) async-start(), calls=%async_computation.8 | async-start | bytes 7372800 | tf_op jit(solution)/shard_map/reduce_scatter | solution.py:736
  629.8 71.1 %collective-permute-start.26 = (bf16[512,1536]{1,0:T(8,128)(2,1)}, bf16[512,1536]{1,0:T(8,128)(2,1)}, u32[]{:S(2)}, u32[]{:S(2)}) collective-permute-start(bf16[512,1536]{1,0:T(8,128)(2,1)} %pad_maximum_fusion.6), channel_id=1, source_target_pairs={{0,4},{1,5},{2,6},{3,7},{4,0},{5,1},{6,2},{7,3},{8,12},{9,13},{10,... | collective-permute-start | bytes 4718600 | tf_op jit(solution)/shard_map/ppermute | solution.py:508
  758.1 61.4 %collective-permute-start.29 = (bf16[512,2048]{1,0:T(8,128)(2,1)}, bf16[512,2048]{1,0:T(8,128)(2,1)}, u32[]{:S(2)}, u32[]{:S(2)}) collective-permute-start(bf16[512,2048]{1,0:T(8,128)(2,1)} %slice.468), channel_id=1, source_target_pairs={{0,1},{1,0},{2,3},{3,2},{4,5},{5,4},{6,7},{7,6},{8,9},{9,8},{10,11... | collective-permute-start | bytes 6291464 | tf_op jit(solution)/shard_map/ppermute | solution.py:508
  759.5 60.0 %collective-permute-start.30 = (bf16[448,2048]{1,0:T(8,128)(2,1)}, bf16[448,2048]{1,0:T(8,128)(2,1)}, u32[]{:S(2)}, u32[]{:S(2)}) collective-permute-start(bf16[448,2048]{1,0:T(8,128)(2,1)} %slice.469), channel_id=1, source_target_pairs={{0,2},{1,3},{2,0},{3,1},{4,6},{5,7},{6,4},{7,5},{8,10},{9,11},{10,... | collective-permute-start | bytes 5505032 | tf_op jit(solution)/shard_map/ppermute | solution.py:508
  779.7 51.6 %collective-permute-start.33 = (bf16[512,768]{0,1:T(8,128)(2,1)}, bf16[512,768]{0,1:T(8,128)(2,1)}, u32[]{:S(2)}, u32[]{:S(2)}) collective-permute-start(bf16[512,768]{0,1:T(8,128)(2,1)} %slice.401), channel_id=1, source_target_pairs={{0,4},{1,5},{2,6},{3,7},{4,0},{5,1},{6,2},{7,3},{8,12},{9,13},{10,... | collective-permute-start | bytes 2359304 | tf_op jit(solution)/shard_map/ppermute | solution.py:508
  (95 other events, 1710.3 us)
Sparse Core Ops, SparseCore 0:
  71.3 50.6 all-gather.3
  193.0 69.2 all-gather.5
  339.8 43.2 all-gather.7
  499.9 120.7 reduce-scatter.4
  623.5 70.1 reduce-scatter.8
  696.6 39.5 reduce-scatter.10
  739.7 66.8 reduce-scatter.6

commit v4 on v3

--- a/solution.py
+++ b/solution.py
@@ -580,7 +580,7 @@
 
 
 def scatter_start(product, parts, size, piece, first=0):
-    far = product(*rows_far(parts)).astype(jnp.bfloat16)
+    far = product(*parts).astype(jnp.bfloat16)
     total, came = scatter_near(far, piece)
     if first:
         sent = [swap(rows, "chan", size // 2) for rows in (total[:first], total[first:])]
@@ -701,7 +701,7 @@
     )
     mixed, back_far, expand_part = both(mixed, back_far, expand_part)
     mixer_full = jnp.concatenate([mixer_weights, other_mixer], axis=0)
-    back_all = lay_rows(gather_blocks(cotangent, side) + gather_blocks(back_far, side))
+    back_halves = [lay_rows(gather_blocks(half_of, side)) for half_of in (cotangent, back_far)]
     other_expand = share(expand_part)
     expand_full = jnp.concatenate(
         [
@@ -713,25 +713,32 @@
         axis=1,
     )
     through_mixer = lambda left: contract(left, mixer_full)
-    arrived, came, _ = scatter_start(through_mixer, [mixed], group, piece)
+    arrived, came, _ = scatter_start(through_mixer, rows_far([mixed]), group, piece)
     near = through_mixer(*rows_near([later(mixed, *came)])).astype(jnp.bfloat16)
     arrived, shrink_part = both(arrived, shrink_part)
     middle = rows_float + scatter_end(arrived, near, piece)
     scale_two = lax.rsqrt(jnp.mean(middle * middle, axis=-1, keepdims=True) + norm_eps)
     normed_two = (middle * scale_two * gain_second).astype(jnp.bfloat16)
     shrink_full = lay_rows([shrink_weights, share(later(shrink_part, other_expand))])
-    mlp_near = lay_rows(gather_blocks(normed_two, side), 2)
-    mlp_far, mlp_near, back_all, expand_full = both(
-        swap(normed_two, "chan", side), mlp_near, back_all, expand_full
-    )
-    normed_mlp = lay_more(mlp_near, gather_blocks(mlp_far, side))
-    expanded = contract(normed_mlp, expand_full)
-    product_grad = contract_cols(back_all, shrink_full)
-    up_part = expanded[:, pair_width:]
-    act_part, slope_part = gelu_parts(expanded[:, :pair_width])
-    product_low = (act_part * up_part).astype(jnp.bfloat16)
-    gate_grad_low = (product_grad * up_part * slope_part).astype(jnp.bfloat16)
-    up_grad_low = (product_grad * act_part).astype(jnp.bfloat16)
+    mlp_near = lay_rows(gather_blocks(normed_two, side))
+    mlp_far = swap(normed_two, "chan", side)
+
+    def mlp(rows, backs):
+        expanded = contract(rows, expand_full)
+        up_part = expanded[:, pair_width:]
+        act_part, slope_part = gelu_parts(expanded[:, :pair_width])
+        product_grad = contract_cols(backs, shrink_full)
+        return (
+            (act_part * up_part).astype(jnp.bfloat16),
+            (product_grad * up_part * slope_part).astype(jnp.bfloat16),
+            (product_grad * act_part).astype(jnp.bfloat16),
+        )
+
+    product_near, gate_near, up_near = mlp(mlp_near, back_halves[0])
+    mlp_far, product_near, gate_near, up_near = both(mlp_far, product_near, gate_near, up_near)
+    mlp_far = lay_rows(gather_blocks(mlp_far, side))
+    product_far, gate_far, up_far = mlp(mlp_far, back_halves[1])
+
     def reduce_seq(matrix):
         return lax.psum_scatter(
             matrix.astype(jnp.bfloat16), "seq", scatter_dimension=0, tiled=True
@@ -743,26 +750,32 @@
     def through_shrink(left):
         return contract(left, shrink_full)
 
-    arrived, came, _ = scatter_start(through_expand, [gate_grad_low, up_grad_low], group, piece)
-    gate_grad_low, up_grad_low, product_low, *_ = both(
-        gate_grad_low, up_grad_low, product_low, *came
-    )
-    expand_local = contract_rows(
-        normed_mlp, jnp.concatenate([gate_grad_low, up_grad_low], axis=1)
-    ).astype(jnp.bfloat16)
-    arrived, expand_local, gate_grad_low = both(arrived, expand_local, gate_grad_low)
-    near = through_expand(*rows_near([gate_grad_low, up_grad_low])).astype(jnp.bfloat16)
+    arrived, came, _ = scatter_start(through_expand, [gate_far, up_far], group, piece)
+    gate_far, up_far, product_far, *_ = both(gate_far, up_far, product_far, *came)
+    expand_back = jnp.concatenate(
+        [
+            jnp.concatenate([gate_near, up_near], axis=1),
+            jnp.concatenate([gate_far, up_far], axis=1),
+        ],
+        axis=0,
+    )
+    normed_mlp = lay_rows([mlp_near, mlp_far])
+    expand_local = contract_rows(normed_mlp, expand_back).astype(jnp.bfloat16)
+    arrived, expand_local, gate_near, up_near = both(arrived, expand_local, gate_near, up_near)
+    near = through_expand(gate_near, up_near).astype(jnp.bfloat16)
     expand_sum = reduce_seq(expand_local)
     normed_two_grad = scatter_end(arrived, near, piece)
     back_float = cotangent.astype(jnp.float32)
     middle_grad = back_float + norm_back(middle, scale_two, gain_second, normed_two_grad)
     middle_low = middle_grad.astype(jnp.bfloat16)
-    product_low = later(product_low, middle_low)
+    product_near, product_far = later(product_near, middle_low), later(product_far, middle_low)
+    back_all = lay_rows(back_halves)
+    product_low = lay_rows([product_near, product_far])
     shrink_local = contract_rows(back_all, product_low).astype(jnp.bfloat16)
     middle_near = lay_rows(gather_blocks(middle_low, side), 2)
-    product_low = later(product_low, shrink_local)
-    out_arrived, _, out_far = scatter_start(through_shrink, [product_low], group, piece)
-    out_near = through_shrink(*rows_near([later(product_low, out_far)])).astype(jnp.bfloat16)
+    product_far = later(product_far, shrink_local)
+    out_arrived, _, out_far = scatter_start(through_shrink, [product_far], group, piece)
+    out_near = through_shrink(later(product_near, out_far)).astype(jnp.bfloat16)
     middle_far, shrink_local, middle_near, out_near, mixer_full = both(
         swap(middle_low, "chan", side), shrink_local, middle_near, out_near, mixer_full
     )
@@ -791,7 +804,9 @@
     through_branch = lambda left: contract(left, branch_full.reshape(4 * chan_width, width))
     branch_local = contract_rows(normed_all, branch_back_low).astype(jnp.bfloat16)
     branch_back_low = later(branch_back_low, branch_local)
-    arrived, _, far = scatter_start(through_branch, [branch_back_low], group, piece, TILE)
+    arrived, _, far = scatter_start(
+        through_branch, rows_far([branch_back_low]), group, piece, TILE
+    )
     branch_back_low, arrived[0] = both(branch_back_low, arrived[0])
     arrived = jnp.concatenate(arrived, axis=0)
     block_size = gate_blocks.shape[2]

time: 956 us -> 904 us (0.946)
  local copies, waits for them, and re-layouts: 152 us -> 109 us
  waiting for transfers between devices: 272 us -> 255 us
    ppermute x44, waiting for transfers between devices: 266 us -> 234 us  [swap(): lax.ppermute(values, axis, [(i, i ^ bit) for i in range(lax.axis_size(axi...]
    dynamic_update_slice x17 -> x9, local copies, waits for them, and re-layouts: 59.1 us -> 32.7 us  [lay_more(): whole = lax.dynamic_update_slice_in_dim(whole, block, start, axis=0)]
    slice x4 -> x0, local copies, waits for them, and re-layouts: 12.3 us -> none  [the longest x2 7.88 us: rows_near(): return [part[:part.shape[0] // 2] for part in parts]]
    dot_general x7 -> x8, matrix products: 80.5 us -> 84.5 us  [contract(): return jnp.dot(left_mat, right_mat, preferred_element_type=jnp.float32)]
    dot_general x3 -> x4, matrix products: 70.7 us -> 70.6 us  [contract_cols(): lax.dot_general(left_mat, right_mat, (((1,), (1,)), ((), ())), preferred_...]
    unnamed x140 -> x112, local copies, waits for them, and re-layouts: 27.8 us -> 27.9 us
  transfers between devices with their start and end apart: 51 -> 51, of which waited for: 28 -> 28; matrix products, arithmetic and copies ran while one was open for 39% -> 41% of each run, Pallas kernels for 11% -> 11%
where the time goes in v4:
time: 904 us; the launch traced here: 895 us
  waiting for transfers between devices  255 us (28%)
  matrix products  234 us (26%)
  Pallas kernels  134 us (15%)
  local copies, waits for them, and re-layouts  109 us (12%)
  other arithmetic  98.2 us (11%)
  starting transfers between devices  43.2 us (5%)
  between operations  21 us (2%)
    ppermute x44, waiting for transfers between devices, swap(): lax.ppermute(values, axis, [(i, i ^ bit) for i in range(lax.axis_size(axi...  234 us
    dot_general x8, matrix products, contract(): return jnp.dot(left_mat, right_mat, preferred_element_type=jnp.float32)  84.5 us
    dot_general x4, matrix products, contract_rows(): lax.dot_general(left_mat, right_mat, (((0,), (0,)), ((), ())), preferred_...  78.9 us
    dot_general x4, matrix products, contract_cols(): lax.dot_general(left_mat, right_mat, (((1,), (1,)), ((), ())), preferred_...  70.6 us
    pallas_call x1, Pallas kernels, lru_backward(): pl.pallas_call(lru_backward_kernel, grid_spec=pltpu.PrefetchScalarGridSpe...  57 us
    pallas_call x1, Pallas kernels, lru_forward(): pl.pallas_call(lru_forward_kernel, grid_spec=pltpu.PrefetchScalarGridSpec...  45.6 us
    ppermute x44, starting transfers between devices, swap(): lax.ppermute(values, axis, [(i, i ^ bit) for i in range(lax.axis_size(axi...  41.9 us
    dynamic_update_slice x9, local copies, waits for them, and re-layouts, lay_more(): whole = lax.dynamic_update_slice_in_dim(whole, block, start, axis=0)  32.7 us
  transfers between devices with their start and end apart: 51, of which 28 were waited for; matrix products, arithmetic and copies ran while one was open for 41% of the time, Pallas kernels for 11%

profile of v4, /device:TPU:0, one launch (start us, length us, event | category | flops | bytes accessed | tf_op | source)
XLA Modules:
  0.0 894.9 jit_solution(8917531275519687562)
XLA Ops:
  37.5 28.9 %collective-permute-done.1 = bf16[240,2048]{1,0:T(8,128)(2,1)} collective-permute-done((bf16[240,2048]{1,0:T(8,128)(2,1)S(1)}, bf16[240,2048]{1,0:T(8,128)(2,1)}, u32[]{:S(2)}, u32[]{:S(2)}) %collective-permute-start.1) | collective-permute-done | bytes 983072 | tf_op jit(solution)/shard_map/ppermute | solution.py:508
  72.4 27.1 %collective-permute-done.3 = bf16[256,2048]{1,0:T(8,128)(2,1)S(1)} collective-permute-done((bf16[256,2048]{1,0:T(8,128)(2,1)}, bf16[256,2048]{1,0:T(8,128)(2,1)S(1)}, u32[]{:S(2)}, u32[]{:S(2)}) %collective-permute-start.3) | collective-permute-done | bytes 1048608 | tf_op jit(solution)/shard_map/ppermute | solution.py:508
  122.7 45.6 %lru_forward.1 = (bf16[2048,640]{1,0:T(8,128)(2,1)S(1)}, f32[2048,640]{1,0:T(8,128)}, f32[2048,640]{1,0:T(8,128)}, f32[2048,640]{1,0:T(8,128)}, bf16[2048,640]{1...) custom-call(s32[1]{0:T(128)} %bitcast.3.place_ref, ...), custom_call_target="tpu_custom_call" | custom-call | flops 14092861440 | bytes 42467328 | tf_op jit(solution)/shard_map/lru_forward/pallas_call | solution.py:347
  169.8 12.3 %collective-permute-done.8 = bf16[512,1536]{1,0:T(8,128)(2,1)} collective-permute-done((bf16[512,1536]{1,0:T(8,128)(2,1)}, bf16[512,1536]{1,0:T(8,128)(2,1)}, u32[]{:S(2)}, u32[]{:S(2)}) %collective-permute-start.8) | collective-permute-done | bytes 1572896 | tf_op jit(solution)/shard_map/ppermute | solution.py:508
  209.8 52.0 %collective-permute-done.12 = bf16[192,2048]{1,0:T(8,128)(2,1)S(1)} collective-permute-done((bf16[192,2048]{1,0:T(8,128)(2,1)S(1)}, bf16[192,2048]{1,0:T(8,128)(2,1)S(1)}, u32[]{:S(2)}, u32[]{:S(2)}) %collective-permute-start.12) | collective-permute-done | bytes 786464 | tf_op jit(solution)/shard_map/ppermute | solution.py:508
  287.5 19.7 %fusion.57 = f32[1024,3072]{1,0:T(8,128)} fusion(bf16[512,2048]{1,0:T(8,128)(2,1)} %collective-permute-done.15, bf16[512,2048]{1,0:T(8,128)(2,1)} %multiply_convert_fusion.6, bf16[2048,768]{1,0:T(8,128)(2,1)} %get-tuple-element.214, bf16[2048,768]{1,0:T(8,128)(2,1)} %get-tuple-element.212, bf16[2048,768]{1,0:T(8,128)(2,1)} %get-tuple-element.213, ...), kind=kOutput, calls=%fused_computation.76 | convolution fusion | flops 12943622144 | bytes 29360128 | tf_op jit(solution)/shard_map/dot_general | solution.py:49
  320.4 17.6 %multiply_convert_fusion.3 = (bf16[1024,1536]{1,0:T(8,128)(2,1)}, bf16[1024,1536]{1,0:T(8,128)(2,1)}, bf16[1024,1536]{1,0:T(8,128)(2,1)}) fusion(f32[1024,3072]{1,0:T(8,128)} %fusion.57, bf16[1536,2048]{1,0:T(8,128)(2,1)} %constant_dynamic-update-slice_fusion.2, bf16[512,2048]{1,0:T(8,128)(2,1)} %collective-permute-done.16, bf16[512,2048]{1,0:T(8,128)(2,1)} %param.16), kind=kOutput, calls=%fused_computation.54 | convolution fusion | flops 6488588288 | bytes 32505856 | tf_op jit(solution)/shard_map/dot_general | solution.py:43
  342.5 19.8 %fusion.65 = f32[1024,3072]{1,0:T(8,128)} fusion(bf16[512,2048]{1,0:T(8,128)(2,1)} %collective-permute-done.17, bf16[512,2048]{1,0:T(8,128)(2,1)} %collective-permute-done.14, bf16[2048,768]{1,0:T(8,128)(2,1)} %get-tuple-element.214, bf16[2048,768]{1,0:T(8,128)(2,1)} %get-tuple-element.212, bf16[2048,768]{1,0:T(8,128)(2,1)} %get-tuple-element.213, ...), kind=kOutput, calls=%fused_computation.84 | convolution fusion | flops 12943622144 | bytes 29360128 | tf_op jit(solution)/shard_map/dot_general | solution.py:49
  362.3 17.7 %multiply_convert_fusion.2 = (bf16[1024,1536]{1,0:T(8,128)(2,1)}, bf16[1024,1536]{1,0:T(8,128)(2,1)}, bf16[1024,1536]{1,0:T(8,128)(2,1)}) fusion(f32[1024,3072]{1,0:T(8,128)} %fusion.65, bf16[1536,2048]{1,0:T(8,128)(2,1)} %constant_dynamic-update-slice_fusion.2, bf16[512,2048]{1,0:T(8,128)(2,1)} %collective-permute-done.13, ...), kind=kOutput, calls=%fused_computation.50 | convolution fusion | flops 6488588288 | bytes 32505856 | tf_op jit(solution)/shard_map/dot_general | solution.py:43
  380.1 17.5 %fusion.74 = bf16[1024,2048]{1,0:T(8,128)(2,1)S(1)} fusion(bf16[1024,1536]{1,0:T(8,128)(2,1)} %get-tuple-element.121, bf16[1024,1536]{1,0:T(8,128)(2,1)} %get-tuple-element.120, bf16[2048,768]{1,0:T(8,128)(2,1)} %get-tuple-element.214, bf16[2048,768]{1,0:T(8,128)(2,1)} %get-tuple-element.212, bf16[2048,768]{1,0:T(8,128)(2,1)} %get-tuple-element.213, ...), kind=kOutput, calls=%fused_computation.110 | convolution fusion | flops 12949913600 | bytes 23068672 | tf_op jit(solution)/shard_map/dot_general | solution.py:43
  409.1 35.6 %fusion.8 = bf16[2048,3072]{1,0:T(8,128)(2,1)} fusion(bf16[1024,1536]{1,0:T(8,128)(2,1)} %get-tuple-element.121, bf16[1024,1536]{1,0:T(8,128)(2,1)} %get-tuple-element.120, bf16[1024,1536]{1,0:T(8,128)(2,1)} %get-tuple-element.123, bf16[1024,1536]{1,0:T(8,128)(2,1)} %get-tuple-element.122, bf16[2048,2048]{1,0:T(8,128)(2,1)} %fusion.148), kind=kOutput, calls=%fused_computation.9 | convolution fusion | flops 25826426880 | bytes 33554432 | tf_op jit(solution)/shard_map/dot_general | solution.py:37
  444.7 11.1 %collective-permute-done.19 = bf16[512,2048]{1,0:T(8,128)(2,1)} collective-permute-done((bf16[512,2048]{1,0:T(8,128)(2,1)}, bf16[512,2048]{1,0:T(8,128)(2,1)}, u32[]{:S(2)}, u32[]{:S(2)}) %collective-permute-start.19) | collective-permute-done | bytes 2097184 | tf_op jit(solution)/shard_map/ppermute | solution.py:508
  455.9 17.8 %fusion.71 = bf16[1024,2048]{1,0:T(8,128)(2,1)S(1)} fusion(bf16[1024,1536]{1,0:T(8,128)(2,1)} %get-tuple-element.123, bf16[1024,1536]{1,0:T(8,128)(2,1)} %get-tuple-element.122, bf16[2048,768]{1,0:T(8,128)(2,1)} %get-tuple-element.214, bf16[2048,768]{1,0:T(8,128)(2,1)} %get-tuple-element.212, bf16[2048,768]{1,0:T(8,128)(2,1)} %get-tuple-element.213, ...), kind=kOutput, calls=%fused_computation.109 | convolution fusion | flops 12949913600 | bytes 23068672 | tf_op jit(solution)/shard_map/dot_general | solution.py:43
  490.3 19.8 %fusion.26 = bf16[2048,1536]{0,1:T(8,128)(2,1)} fusion(bf16[512,2048]{1,0:T(8,128)(2,1)} %collective-permute-done.13, bf16[512,2048]{1,0:T(8,128)(2,1)} %collective-permute-done.7, bf16[512,2048]{1,0:T(8,128)(2,1)} %collective-permute-done.16, bf16[512,2048]{1,0:T(8,128)(2,1)} %param.16, bf16[1024,1536]{1,0:T(8,128)(2,1)} %get-tuple-element.129, ...), kind=kOutput, calls=%fused_computation.30 | convolution fusion | flops 12934184960 | bytes 20971520 | tf_op jit(solution)/shard_map/dot_general | solution.py:37
  510.1 11.1 %convolution_convert_fusion.2 = bf16[1024,2048]{1,0:T(8,128)(2,1)} fusion(bf16[1024,1536]{1,0:T(8,128)(2,1)} %get-tuple-element.129, bf16[1536,2048]{1,0:T(8,128)(2,1)} %constant_dynamic-update-slice_fusion.2), kind=kOutput, calls=%fused_computation.108 | convolution fusion | flops 6444548096 | bytes 13631488 | tf_op jit(solution)/shard_map/dot_general | solution.py:49
  527.4 11.0 %convolution_convert_fusion.1 = bf16[1024,2048]{1,0:T(8,128)(2,1)} fusion(bf16[1024,1536]{1,0:T(8,128)(2,1)S(1)} %copy-done.49, bf16[1536,2048]{1,0:T(8,128)(2,1)} %constant_dynamic-update-slice_fusion.2), kind=kOutput, calls=%fused_computation.107 | convolution fusion | flops 6444548096 | bytes 13631488 | tf_op jit(solution)/shard_map/dot_general | solution.py:49
  558.2 9.6 %convolution_convert_fusion.7 = bf16[2048,640]{0,1:T(8,128)(2,1)} fusion(bf16[2048,2048]{1,0:T(8,128)(2,1)} %constant_dynamic-update-slice_fusion.6.back_ref, bf16[2048,640]{1,0:T(8,128)(2,1)S(1)} %copy-done.11), kind=kOutput, calls=%fused_computation.115 | convolution fusion | flops 5370019840 | bytes 13631488 | tf_op jit(solution)/shard_map/dot_general | solution.py:37
  583.6 57.0 %lru_backward.1 = (bf16[2048,640]{1,0:T(8,128)(2,1)}, bf16[2048,640]{1,0:T(8,128)(2,1)}, f32[640,640]{1,0:T(8,128)S(1)}, f32[640,640]{1,0:T(8,128)S(1)}, f32[8,8,640]{2,1,0:T(8,128)S(1)}) custom-call(s32[1]{0:T(128)} %bitcast.3.place_ref, bf16[2048,2048]{1,0:T(8,128)(2,1)} %constant_dynamic-update-slice_fusion.6.back_ref, ...), custom_call_target="tpu_custom_call" | custom-call | flops 12079595520 | bytes 47710208 | tf_op jit(solution)/shard_map/lru_backward/pallas_call | solution.py:405
  642.1 10.2 %collective-permute-done.26 = bf16[512,1536]{1,0:T(8,128)(2,1)} collective-permute-done((bf16[512,1536]{1,0:T(8,128)(2,1)}, bf16[512,1536]{1,0:T(8,128)(2,1)}, u32[]{:S(2)}, u32[]{:S(2)}) %collective-permute-start.26) | collective-permute-done | bytes 1572896 | tf_op jit(solution)/shard_map/ppermute | solution.py:508
  657.1 13.9 %convolution_convert_fusion = bf16[2048,1280]{0,1:T(8,128)(2,1)S(1)} fusion(bf16[2048,2048]{1,0:T(8,128)(2,1)} %constant_dynamic-update-slice_fusion.9.normed_ref, bf16[2048,1280]{1,0:T(8,128)(2,1)S(1)} %constant_dynamic-update-slice_fusion.4), kind=kOutput, calls=%fused_computation.31 | convolution fusion | flops 10740039680 | bytes 18874368 | tf_op jit(solution)/shard_map/dot_general | solution.py:37
  731.7 20.2 %collective-permute-done.32 = f32[8,320]{1,0:T(8,128)S(1)} collective-permute-done((f32[8,320]{1,0:T(8,128)S(1)}, f32[8,320]{1,0:T(8,128)S(1)}, u32[]{:S(2)}, u32[]{:S(2)}) %collective-permute-start.32) | collective-permute-done | bytes 10272 | tf_op jit(solution)/shard_map/ppermute | solution.py:508
  757.0 13.5 %collective-permute-done.30 = bf16[448,2048]{1,0:T(8,128)(2,1)} collective-permute-done((bf16[448,2048]{1,0:T(8,128)(2,1)}, bf16[448,2048]{1,0:T(8,128)(2,1)}, u32[]{:S(2)}, u32[]{:S(2)}) %collective-permute-start.30) | collective-permute-done | bytes 1835040 | tf_op jit(solution)/shard_map/ppermute | solution.py:508
  804.7 19.1 %collective-permute-done.36 = bf16[2,2,40,160]{3,2,1,0:T(8,128)(2,1)} collective-permute-done((bf16[2,2,40,160]{3,2,1,0:T(8,128)(2,1)}, bf16[2,2,40,160]{3,2,1,0:T(8,128)(2,1)}, u32[]{:S(2)}, u32[]{:S(2)}) %collective-permute-start.36) | collective-permute-done | bytes 51232 | tf_op jit(solution)/shard_map/ppermute | solution.py:508
  853.7 14.1 %adam.8 = (f32[4,512,2,768]{3,2,1,0:T(2,128)}, bf16[512,2,768]{2,1,0:T(2,128)(2,1)}) custom-call(f32[1,1]{1,0:T(1,128)} %bitcast.41.refs_0_, f32[4,512,2,768]{3,2,1,0:T(2,128)} %refs_1_.4, f32[512,2,768]{2,1,0:T(2,128)S(1)} %reshape.287.refs_2_), custom_call_target="tpu_custom_call" | custom-call | flops 15728640 | bytes 29884416 | tf_op jit(solution)/shard_map/adam/pallas_call | solution.py:488
  (342 shorter events, 351.4 us)
Async XLA Ops:
  7.2 110.1 %all-gather.4.cloned.1.call-start = ((), (), s32[]{:S(2)}) async-start(), calls=%async_computation.4 | async-start | bytes 4915200 | tf_op jit(solution)/shard_map/all_gather | solution.py:648
  14.1 52.4 %collective-permute-start = (bf16[256,2048]{1,0:T(8,128)(2,1)}, bf16[256,2048]{1,0:T(8,128)(2,1)S(1)}, u32[]{:S(2)}, u32[]{:S(2)}) collective-permute-start(bf16[256,2048]{1,0:T(8,128)(2,1)} %slice.409), channel_id=1, source_target_pairs={{0,2},{1,3},{2,0},{3,1},{4,6},{5,7},{6,4},{7,5},{8,10},{9,11},{10,... | collective-permute-start | bytes 3145736 | tf_op jit(solution)/shard_map/ppermute | solution.py:508
  20.4 46.0 %collective-permute-start.1 = (bf16[240,2048]{1,0:T(8,128)(2,1)S(1)}, bf16[240,2048]{1,0:T(8,128)(2,1)}, u32[]{:S(2)}, u32[]{:S(2)}) collective-permute-start(bf16[240,2048]{1,0:T(8,128)(2,1)S(1)} %constant_dynamic-slice_fusion.2), channel_id=1, source_target_pairs={{0,4},{1,5},{2,6},{3,7},{4,0},{5,1},{6,2},{7,3},{8,12},{9,13},{10,... | collective-permute-start | bytes 2949128 | tf_op jit(solution)/shard_map/ppermute | solution.py:508
  66.5 205.7 %all-gather.6.cloned.1.call-start = ((), (), s32[]{:S(2)}) async-start(), calls=%async_computation.5 | async-start | bytes 7864320 | tf_op jit(solution)/shard_map/all_gather | solution.py:648
  102.2 82.1 %collective-permute-start.7 = (bf16[512,2048]{1,0:T(8,128)(2,1)}, bf16[512,2048]{1,0:T(8,128)(2,1)}, u32[]{:S(2)}, u32[]{:S(2)}) collective-permute-start(bf16[512,2048]{1,0:T(8,128)(2,1)} %param.16), channel_id=1, source_target_pairs={{0,2},{1,3},{2,0},{3,1},{4,6},{5,7},{6,4},{7,5},{8,10},{9,11},{10,... | collective-permute-start | bytes 6291464 | tf_op jit(solution)/shard_map/ppermute | solution.py:508
  105.0 77.2 %collective-permute-start.8 = (bf16[512,1536]{1,0:T(8,128)(2,1)}, bf16[512,1536]{1,0:T(8,128)(2,1)}, u32[]{:S(2)}, u32[]{:S(2)}) collective-permute-start(bf16[512,1536]{1,0:T(8,128)(2,1)} %constant_dynamic-slice_fusion.1), channel_id=1, source_target_pairs={{0,4},{1,5},{2,6},{3,7},{4,0},{5,1},{6,2},{7,3},{8,12},{9,13},{10,... | collective-permute-start | bytes 4718600 | tf_op jit(solution)/shard_map/ppermute | solution.py:508
  184.4 132.0 %all-gather.8.cloned.1.call-start = ((), (), s32[]{:S(2)}) async-start(), calls=%async_computation.6 | async-start | bytes 3932160 | tf_op jit(solution)/shard_map/all_gather | solution.py:648
  198.3 64.8 %collective-permute-start.11 = (bf16[512,2048]{1,0:T(8,128)(2,1)}, bf16[512,2048]{1,0:T(8,128)(2,1)}, u32[]{:S(2)}, u32[]{:S(2)}) collective-permute-start(bf16[512,2048]{1,0:T(8,128)(2,1)} %add_convert_fusion.7), channel_id=1, source_target_pairs={{0,2},{1,3},{2,0},{3,1},{4,6},{5,7},{6,4},{7,5},{8,10},{9,11},{10,... | collective-permute-start | bytes 6291464 | tf_op jit(solution)/shard_map/ppermute | solution.py:508
  206.8 56.3 %collective-permute-start.10 = (bf16[512,2048]{1,0:T(8,128)(2,1)}, bf16[512,2048]{1,0:T(8,128)(2,1)}, u32[]{:S(2)}, u32[]{:S(2)}) collective-permute-start(bf16[512,2048]{1,0:T(8,128)(2,1)} %slice.424), channel_id=1, source_target_pairs={{0,1},{1,0},{2,3},{3,2},{4,5},{5,4},{6,7},{7,6},{8,9},{9,8},{10,11... | collective-permute-start | bytes 6291464 | tf_op jit(solution)/shard_map/ppermute | solution.py:508
  208.0 53.8 %collective-permute-start.12 = (bf16[192,2048]{1,0:T(8,128)(2,1)S(1)}, bf16[192,2048]{1,0:T(8,128)(2,1)S(1)}, u32[]{:S(2)}, u32[]{:S(2)}) collective-permute-start(bf16[192,2048]{1,0:T(8,128)(2,1)S(1)} %constant_dynamic-slice_fusion), channel_id=1, source_target_pairs={{0,4},{1,5},{2,6},{3,7},{4,0},{5,1},{6,2},{7,3},{8,12},{9,13},{10,... | collective-permute-start | bytes 2359304 | tf_op jit(solution)/shard_map/ppermute | solution.py:508
  271.6 48.7 %collective-permute-start.16 = (bf16[512,2048]{1,0:T(8,128)(2,1)}, bf16[512,2048]{1,0:T(8,128)(2,1)}, u32[]{:S(2)}, u32[]{:S(2)}) collective-permute-start(bf16[512,2048]{1,0:T(8,128)(2,1)} %param.16), channel_id=1, source_target_pairs={{0,1},{1,0},{2,3},{3,2},{4,5},{5,4},{6,7},{7,6},{8,9},{9,8},{10,11... | collective-permute-start | bytes 6291464 | tf_op jit(solution)/shard_map/ppermute | solution.py:508
  272.2 304.6 %reduce-scatter.5.cloned.1.call-start = ((), (), s32[]{:S(2)}) async-start(), calls=%async_computation.7 | async-start | bytes 15728640 | tf_op jit(solution)/shard_map/reduce_scatter | solution.py:743
  283.0 54.9 %collective-permute-start.14 = (bf16[512,2048]{1,0:T(8,128)(2,1)}, bf16[512,2048]{1,0:T(8,128)(2,1)}, u32[]{:S(2)}, u32[]{:S(2)}) collective-permute-start(bf16[512,2048]{1,0:T(8,128)(2,1)} %multiply_convert_fusion.6), channel_id=1, source_target_pairs={{0,2},{1,3},{2,0},{3,1},{4,6},{5,7},{6,4},{7,5},{8,10},{9,11},{10,... | collective-permute-start | bytes 6291464 | tf_op jit(solution)/shard_map/ppermute | solution.py:508
  407.6 48.2 %collective-permute-start.19 = (bf16[512,2048]{1,0:T(8,128)(2,1)}, bf16[512,2048]{1,0:T(8,128)(2,1)}, u32[]{:S(2)}, u32[]{:S(2)}) collective-permute-start(bf16[512,2048]{1,0:T(8,128)(2,1)} %add_convert_fusion.6), channel_id=1, source_target_pairs={{0,2},{1,3},{2,0},{3,1},{4,6},{5,7},{6,4},{7,5},{8,10},{9,11},{10,... | collective-permute-start | bytes 6291464 | tf_op jit(solution)/shard_map/ppermute | solution.py:508
  455.9 258.8 %reduce-scatter.9.cloned.1.call-start = ((), (), s32[]{:S(2)}) async-start(), calls=%async_computation.9 | async-start | bytes 7864320 | tf_op jit(solution)/shard_map/reduce_scatter | solution.py:743
  488.8 53.5 %collective-permute-start.21 = (bf16[512,2048]{1,0:T(8,128)(2,1)}, bf16[512,2048]{1,0:T(8,128)(2,1)}, u32[]{:S(2)}, u32[]{:S(2)}) collective-permute-start(bf16[512,2048]{1,0:T(8,128)(2,1)} %get-tuple-element.195), channel_id=1, source_target_pairs={{0,2},{1,3},{2,0},{3,1},{4,6},{5,7},{6,4},{7,5},{8,10},{9,11},{10,... | collective-permute-start | bytes 6291464 | tf_op jit(solution)/shard_map/ppermute | solution.py:508
  490.3 48.2 %collective-permute-start.22 = (bf16[512,2048]{1,0:T(8,128)(2,1)}, bf16[512,2048]{1,0:T(8,128)(2,1)}, u32[]{:S(2)}, u32[]{:S(2)}) collective-permute-start(bf16[512,2048]{1,0:T(8,128)(2,1)} %get-tuple-element.195), channel_id=1, source_target_pairs={{0,1},{1,0},{2,3},{3,2},{4,5},{5,4},{6,7},{7,6},{8,9},{9,8},{10,11... | collective-permute-start | bytes 6291464 | tf_op jit(solution)/shard_map/ppermute | solution.py:508
  542.3 210.3 %reduce-scatter.11.cloned.1.call-start = ((), (), s32[]{:S(2)}) async-start(), calls=%async_computation.10 | async-start | bytes 3276800 | tf_op jit(solution)/shard_map/reduce_scatter | solution.py:743
  553.4 88.7 %collective-permute-start.25 = (bf16[512,2048]{1,0:T(8,128)(2,1)}, bf16[512,2048]{1,0:T(8,128)(2,1)}, u32[]{:S(2)}, u32[]{:S(2)}) collective-permute-start(bf16[512,2048]{1,0:T(8,128)(2,1)} %add_convert_fusion.4), channel_id=1, source_target_pairs={{0,2},{1,3},{2,0},{3,1},{4,6},{5,7},{6,4},{7,5},{8,10},{9,11},{10,... | collective-permute-start | bytes 6291464 | tf_op jit(solution)/shard_map/ppermute | solution.py:508
  567.9 218.2 %reduce-scatter.7.cloned.1.call-start = ((), (), s32[]{:S(2)}) async-start(), calls=%async_computation.8 | async-start | bytes 7372800 | tf_op jit(solution)/shard_map/reduce_scatter | solution.py:743
  581.2 71.1 %collective-permute-start.26 = (bf16[512,1536]{1,0:T(8,128)(2,1)}, bf16[512,1536]{1,0:T(8,128)(2,1)}, u32[]{:S(2)}, u32[]{:S(2)}) collective-permute-start(bf16[512,1536]{1,0:T(8,128)(2,1)} %pad_maximum_fusion.6), channel_id=1, source_target_pairs={{0,4},{1,5},{2,6},{3,7},{4,0},{5,1},{6,2},{7,3},{8,12},{9,13},{10,... | collective-permute-start | bytes 4718600 | tf_op jit(solution)/shard_map/ppermute | solution.py:508
  709.1 61.4 %collective-permute-start.29 = (bf16[512,2048]{1,0:T(8,128)(2,1)}, bf16[512,2048]{1,0:T(8,128)(2,1)}, u32[]{:S(2)}, u32[]{:S(2)}) collective-permute-start(bf16[512,2048]{1,0:T(8,128)(2,1)} %slice.452), channel_id=1, source_target_pairs={{0,1},{1,0},{2,3},{3,2},{4,5},{5,4},{6,7},{7,6},{8,9},{9,8},{10,11... | collective-permute-start | bytes 6291464 | tf_op jit(solution)/shard_map/ppermute | solution.py:508
  710.6 60.0 %collective-permute-start.30 = (bf16[448,2048]{1,0:T(8,128)(2,1)}, bf16[448,2048]{1,0:T(8,128)(2,1)}, u32[]{:S(2)}, u32[]{:S(2)}) collective-permute-start(bf16[448,2048]{1,0:T(8,128)(2,1)} %slice.453), channel_id=1, source_target_pairs={{0,2},{1,3},{2,0},{3,1},{4,6},{5,7},{6,4},{7,5},{8,10},{9,11},{10,... | collective-permute-start | bytes 5505032 | tf_op jit(solution)/shard_map/ppermute | solution.py:508
  716.8 65.7 %collective-permute-start.33 = (bf16[512,768]{0,1:T(8,128)(2,1)}, bf16[512,768]{0,1:T(8,128)(2,1)}, u32[]{:S(2)}, u32[]{:S(2)}) collective-permute-start(bf16[512,768]{0,1:T(8,128)(2,1)} %slice.385), channel_id=1, source_target_pairs={{0,4},{1,5},{2,6},{3,7},{4,0},{5,1},{6,2},{7,3},{8,12},{9,13},{10,... | collective-permute-start | bytes 2359304 | tf_op jit(solution)/shard_map/ppermute | solution.py:508
  (81 other events, 1475.2 us)
Sparse Core Ops, SparseCore 0:
  66.6 50.6 all-gather.3
  184.5 70.2 all-gather.5
  272.3 44.0 all-gather.7
  456.0 120.7 reduce-scatter.4
  580.1 70.1 reduce-scatter.8
  653.2 39.5 reduce-scatter.10
  696.4 66.8 reduce-scatter.6

commit v5 on v4

--- a/solution.py
+++ b/solution.py
@@ -779,7 +779,6 @@
     middle_far, shrink_local, middle_near, out_near, mixer_full = both(
         swap(middle_low, "chan", side), shrink_local, middle_near, out_near, mixer_full
     )
-    shrink_sum = reduce_seq(shrink_local)
     branch_back = lay_more(middle_near, gather_blocks(middle_far, side))
     gain_two = jnp.sum(normed_two_grad * middle * scale_two, axis=0)
 
@@ -792,7 +791,7 @@
         return pair[0].astype(jnp.float32) + pair[1].astype(jnp.float32)
 
     mixer_local = contract_rows(branch_back, mixed).astype(jnp.bfloat16)
-    mixer_sum = reduce_seq(mixer_local)
+    units_sum = reduce_seq(jnp.concatenate([shrink_local, mixer_local], axis=1))
     expand_pair = settle(expand_sum, 2, hidden_width)
     gate_back, recur_back, rate_w_grad, input_w_grad, sums = lru_backward(
         place, later(branch_back, mixer_local), mixer_full, gate_branch, recur_input, hidden,
@@ -826,9 +825,10 @@
         ((0, 0), (0, part_rows - gate_count), (0, 0)),
     ).reshape(width, block_size)
     branch_sum = reduce_seq(jnp.concatenate([branch_local, gate_rows], axis=1))
-    shrink_pair = settle(later(shrink_sum, branch_local), 1, hidden_width)
+    units_sum = later(units_sum, branch_local)
+    shrink_pair = settle(units_sum[:, :pair_width], 1, hidden_width)
     near = through_branch(*rows_near([branch_back_low])).astype(jnp.bfloat16)
-    mixer_pair = settle(later(mixer_sum, near), 1, chan_width)
+    mixer_pair = settle(units_sum[:, pair_width:], 1, chan_width)
     sums = later(sums, branch_local)
     expand_grad = total(expand_pair).reshape(-1, 2, hidden_width)
     channel_pair = jnp.sum(sums, axis=1)

time: 904 us -> 912 us (level)
  waiting for transfers between devices: 255 us -> 269 us
    unnamed x112 -> x116, local copies, waits for them, and re-layouts: 27.9 us -> 28.1 us
  transfers between devices with their start and end apart: 51 -> 50, of which waited for: 28 -> 28; matrix products, arithmetic and copies ran while one was open for 41% -> 40% of each run, Pallas kernels for 11% -> 11%
where the time goes in v5:
time: 912 us; the launch traced here: 904 us
  waiting for transfers between devices  269 us (29%)
  matrix products  231 us (25%)
  Pallas kernels  134 us (15%)
  other arithmetic  103 us (11%)
  local copies, waits for them, and re-layouts  102 us (11%)
  starting transfers between devices  43 us (5%)
  between operations  21.1 us (2%)
    ppermute x44, waiting for transfers between devices, swap(): lax.ppermute(values, axis, [(i, i ^ bit) for i in range(lax.axis_size(axi...  242 us
    dot_general x8, matrix products, contract(): return jnp.dot(left_mat, right_mat, preferred_element_type=jnp.float32)  85 us
    dot_general x4, matrix products, contract_rows(): lax.dot_general(left_mat, right_mat, (((0,), (0,)), ((), ())), preferred_...  75.6 us
    dot_general x4, matrix products, contract_cols(): lax.dot_general(left_mat, right_mat, (((1,), (1,)), ((), ())), preferred_...  70.6 us
    pallas_call x1, Pallas kernels, lru_backward(): pl.pallas_call(lru_backward_kernel, grid_spec=pltpu.PrefetchScalarGridSpe...  57.2 us
    pallas_call x1, Pallas kernels, lru_forward(): pl.pallas_call(lru_forward_kernel, grid_spec=pltpu.PrefetchScalarGridSpec...  45.6 us
    ppermute x44, starting transfers between devices, swap(): lax.ppermute(values, axis, [(i, i ^ bit) for i in range(lax.axis_size(axi...  41.9 us
    pallas_call x5, Pallas kernels, adam_matrix(): pl.pallas_call(lambda *refs: adam_kernel(step_rate, decay_use, *refs), gr...  31.1 us
  transfers between devices with their start and end apart: 50, of which 28 were waited for; matrix products, arithmetic and copies ran while one was open for 40% of the time, Pallas kernels for 11%

profile of v5, /device:TPU:0, one launch (start us, length us, event | category | flops | bytes accessed | tf_op | source)
XLA Modules:
  0.0 903.7 jit_solution(8947355466468468459)
XLA Ops:
  37.5 28.9 %collective-permute-done.1 = bf16[240,2048]{1,0:T(8,128)(2,1)} collective-permute-done((bf16[240,2048]{1,0:T(8,128)(2,1)S(1)}, bf16[240,2048]{1,0:T(8,128)(2,1)}, u32[]{:S(2)}, u32[]{:S(2)}) %collective-permute-start.1) | collective-permute-done | bytes 983072 | tf_op jit(solution)/shard_map/ppermute | solution.py:508
  72.4 27.1 %collective-permute-done.3 = bf16[256,2048]{1,0:T(8,128)(2,1)S(1)} collective-permute-done((bf16[256,2048]{1,0:T(8,128)(2,1)}, bf16[256,2048]{1,0:T(8,128)(2,1)S(1)}, u32[]{:S(2)}, u32[]{:S(2)}) %collective-permute-start.3) | collective-permute-done | bytes 1048608 | tf_op jit(solution)/shard_map/ppermute | solution.py:508
  122.7 45.6 %lru_forward.1 = (bf16[2048,640]{1,0:T(8,128)(2,1)S(1)}, f32[2048,640]{1,0:T(8,128)}, f32[2048,640]{1,0:T(8,128)}, f32[2048,640]{1,0:T(8,128)}, bf16[2048,640]{1...) custom-call(s32[1]{0:T(128)} %bitcast.3.place_ref, ...), custom_call_target="tpu_custom_call" | custom-call | flops 14092861440 | bytes 42467328 | tf_op jit(solution)/shard_map/lru_forward/pallas_call | solution.py:347
  169.8 12.4 %collective-permute-done.8 = bf16[512,1536]{1,0:T(8,128)(2,1)} collective-permute-done((bf16[512,1536]{1,0:T(8,128)(2,1)}, bf16[512,1536]{1,0:T(8,128)(2,1)}, u32[]{:S(2)}, u32[]{:S(2)}) %collective-permute-start.8) | collective-permute-done | bytes 1572896 | tf_op jit(solution)/shard_map/ppermute | solution.py:508
  209.9 52.0 %collective-permute-done.12 = bf16[192,2048]{1,0:T(8,128)(2,1)S(1)} collective-permute-done((bf16[192,2048]{1,0:T(8,128)(2,1)S(1)}, bf16[192,2048]{1,0:T(8,128)(2,1)S(1)}, u32[]{:S(2)}, u32[]{:S(2)}) %collective-permute-start.12) | collective-permute-done | bytes 786464 | tf_op jit(solution)/shard_map/ppermute | solution.py:508
  287.9 19.7 %fusion.57 = f32[1024,3072]{1,0:T(8,128)} fusion(bf16[512,2048]{1,0:T(8,128)(2,1)} %collective-permute-done.15, bf16[512,2048]{1,0:T(8,128)(2,1)} %multiply_convert_fusion.6, bf16[2048,768]{1,0:T(8,128)(2,1)} %get-tuple-element.212, bf16[2048,768]{1,0:T(8,128)(2,1)} %get-tuple-element.210, bf16[2048,768]{1,0:T(8,128)(2,1)} %get-tuple-element.211, ...), kind=kOutput, calls=%fused_computation.77 | convolution fusion | flops 12943622144 | bytes 29360128 | tf_op jit(solution)/shard_map/dot_general | solution.py:49
  320.5 17.6 %multiply_convert_fusion.3 = (bf16[1024,1536]{1,0:T(8,128)(2,1)}, bf16[1024,1536]{1,0:T(8,128)(2,1)}, bf16[1024,1536]{1,0:T(8,128)(2,1)}) fusion(f32[1024,3072]{1,0:T(8,128)} %fusion.57, bf16[1536,2048]{1,0:T(8,128)(2,1)} %constant_dynamic-update-slice_fusion.2, bf16[512,2048]{1,0:T(8,128)(2,1)} %collective-permute-done.16, bf16[512,2048]{1,0:T(8,128)(2,1)} %param.16), kind=kOutput, calls=%fused_computation.55 | convolution fusion | flops 6488588288 | bytes 32505856 | tf_op jit(solution)/shard_map/dot_general | solution.py:43
  342.6 19.8 %fusion.65 = f32[1024,3072]{1,0:T(8,128)} fusion(bf16[512,2048]{1,0:T(8,128)(2,1)} %collective-permute-done.17, bf16[512,2048]{1,0:T(8,128)(2,1)} %collective-permute-done.14, bf16[2048,768]{1,0:T(8,128)(2,1)} %get-tuple-element.212, bf16[2048,768]{1,0:T(8,128)(2,1)} %get-tuple-element.210, bf16[2048,768]{1,0:T(8,128)(2,1)} %get-tuple-element.211, ...), kind=kOutput, calls=%fused_computation.85 | convolution fusion | flops 12943622144 | bytes 29360128 | tf_op jit(solution)/shard_map/dot_general | solution.py:49
  362.5 17.7 %multiply_convert_fusion.2 = (bf16[1024,1536]{1,0:T(8,128)(2,1)}, bf16[1024,1536]{1,0:T(8,128)(2,1)}, bf16[1024,1536]{1,0:T(8,128)(2,1)}) fusion(f32[1024,3072]{1,0:T(8,128)} %fusion.65, bf16[1536,2048]{1,0:T(8,128)(2,1)} %constant_dynamic-update-slice_fusion.2, bf16[512,2048]{1,0:T(8,128)(2,1)} %collective-permute-done.13, ...), kind=kOutput, calls=%fused_computation.51 | convolution fusion | flops 6488588288 | bytes 32505856 | tf_op jit(solution)/shard_map/dot_general | solution.py:43
  380.2 17.5 %fusion.74 = bf16[1024,2048]{1,0:T(8,128)(2,1)S(1)} fusion(bf16[1024,1536]{1,0:T(8,128)(2,1)} %get-tuple-element.120, bf16[1024,1536]{1,0:T(8,128)(2,1)} %get-tuple-element.119, bf16[2048,768]{1,0:T(8,128)(2,1)} %get-tuple-element.212, bf16[2048,768]{1,0:T(8,128)(2,1)} %get-tuple-element.210, bf16[2048,768]{1,0:T(8,128)(2,1)} %get-tuple-element.211, ...), kind=kOutput, calls=%fused_computation.111 | convolution fusion | flops 12949913600 | bytes 23068672 | tf_op jit(solution)/shard_map/dot_general | solution.py:43
  409.2 35.6 %fusion.8 = bf16[2048,3072]{1,0:T(8,128)(2,1)} fusion(bf16[1024,1536]{1,0:T(8,128)(2,1)} %get-tuple-element.120, bf16[1024,1536]{1,0:T(8,128)(2,1)} %get-tuple-element.119, bf16[1024,1536]{1,0:T(8,128)(2,1)} %get-tuple-element.122, bf16[1024,1536]{1,0:T(8,128)(2,1)} %get-tuple-element.121, bf16[2048,2048]{1,0:T(8,128)(2,1)} %fusion.148), kind=kOutput, calls=%fused_computation.9 | convolution fusion | flops 25826426880 | bytes 33554432 | tf_op jit(solution)/shard_map/dot_general | solution.py:37
  444.8 11.2 %collective-permute-done.19 = bf16[512,2048]{1,0:T(8,128)(2,1)} collective-permute-done((bf16[512,2048]{1,0:T(8,128)(2,1)}, bf16[512,2048]{1,0:T(8,128)(2,1)}, u32[]{:S(2)}, u32[]{:S(2)}) %collective-permute-start.19) | collective-permute-done | bytes 2097184 | tf_op jit(solution)/shard_map/ppermute | solution.py:508
  456.1 17.8 %fusion.71 = bf16[1024,2048]{1,0:T(8,128)(2,1)S(1)} fusion(bf16[1024,1536]{1,0:T(8,128)(2,1)} %get-tuple-element.122, bf16[1024,1536]{1,0:T(8,128)(2,1)} %get-tuple-element.121, bf16[2048,768]{1,0:T(8,128)(2,1)} %get-tuple-element.212, bf16[2048,768]{1,0:T(8,128)(2,1)} %get-tuple-element.210, bf16[2048,768]{1,0:T(8,128)(2,1)} %get-tuple-element.211, ...), kind=kOutput, calls=%fused_computation.110 | convolution fusion | flops 12949913600 | bytes 23068672 | tf_op jit(solution)/shard_map/dot_general | solution.py:43
  490.5 19.8 %fusion.26 = bf16[2048,1536]{0,1:T(8,128)(2,1)} fusion(bf16[512,2048]{1,0:T(8,128)(2,1)} %collective-permute-done.13, bf16[512,2048]{1,0:T(8,128)(2,1)} %collective-permute-done.7, bf16[512,2048]{1,0:T(8,128)(2,1)} %collective-permute-done.16, bf16[512,2048]{1,0:T(8,128)(2,1)} %param.16, bf16[1024,1536]{1,0:T(8,128)(2,1)} %get-tuple-element.128, ...), kind=kOutput, calls=%fused_computation.31 | convolution fusion | flops 12934184960 | bytes 20971520 | tf_op jit(solution)/shard_map/dot_general | solution.py:37
  510.3 11.1 %convolution_convert_fusion.2 = bf16[1024,2048]{1,0:T(8,128)(2,1)} fusion(bf16[1024,1536]{1,0:T(8,128)(2,1)} %get-tuple-element.128, bf16[1536,2048]{1,0:T(8,128)(2,1)} %constant_dynamic-update-slice_fusion.2), kind=kOutput, calls=%fused_computation.109 | convolution fusion | flops 6444548096 | bytes 13631488 | tf_op jit(solution)/shard_map/dot_general | solution.py:49
  524.2 11.5 %convolution_convert_fusion.1 = bf16[1024,2048]{1,0:T(8,128)(2,1)} fusion(bf16[1024,1536]{1,0:T(8,128)(2,1)S(1)} %copy-done.49, bf16[1536,2048]{1,0:T(8,128)(2,1)} %constant_dynamic-update-slice_fusion.2), kind=kOutput, calls=%fused_computation.108 | convolution fusion | flops 6444548096 | bytes 13631488 | tf_op jit(solution)/shard_map/dot_general | solution.py:49
  561.7 15.2 %reduce-scatter.4.cloned.1.call-done = bf16[512,3072]{1,0:T(8,128)(2,1)} async-done(((bf16[2048,3072]{1,0:T(8,128)(2,1)}), bf16[512,3072]{1,0:T(8,128)(2,1)}) %reduce-scatter.4.cloned.1.call-update) | async-done | bytes 3145744 | tf_op jit(solution)/shard_map/reduce_scatter | solution.py:743
  583.8 57.2 %lru_backward.1 = (bf16[2048,640]{1,0:T(8,128)(2,1)}, bf16[2048,640]{1,0:T(8,128)(2,1)}, f32[640,640]{1,0:T(8,128)S(1)}, f32[640,640]{1,0:T(8,128)S(1)}, f32[8,8,640]{2,1,0:T(8,128)S(1)}) custom-call(s32[1]{0:T(128)} %bitcast.3.place_ref, bf16[2048,2048]{1,0:T(8,128)(2,1)} %copy-done.15, bf16[640,2048]{1,0:T(8,128)(2,1)} %pad_maximum_fusion.5.mixer_ref, ...), custom_call_target="tpu_custom_call" | custom-call | flops 12079595520 | bytes 47710208 | tf_op jit(solution)/shard_map/lru_backward/pallas_call | solution.py:405
  642.5 10.0 %collective-permute-done.26 = bf16[512,1536]{1,0:T(8,128)(2,1)} collective-permute-done((bf16[512,1536]{1,0:T(8,128)(2,1)}, bf16[512,1536]{1,0:T(8,128)(2,1)}, u32[]{:S(2)}, u32[]{:S(2)}) %collective-permute-start.26) | collective-permute-done | bytes 1572896 | tf_op jit(solution)/shard_map/ppermute | solution.py:508
  657.4 14.1 %convolution_convert_fusion = bf16[2048,1280]{0,1:T(8,128)(2,1)S(1)} fusion(bf16[2048,2048]{1,0:T(8,128)(2,1)} %constant_dynamic-update-slice_fusion.9.normed_ref, bf16[2048,1280]{1,0:T(8,128)(2,1)S(1)} %constant_dynamic-update-slice_fusion.4), kind=kOutput, calls=%fused_computation.32 | convolution fusion | flops 10740039680 | bytes 18874368 | tf_op jit(solution)/shard_map/dot_general | solution.py:37
  736.9 19.2 %collective-permute-done.32 = f32[8,320]{1,0:T(8,128)S(1)} collective-permute-done((f32[8,320]{1,0:T(8,128)S(1)}, f32[8,320]{1,0:T(8,128)S(1)}, u32[]{:S(2)}, u32[]{:S(2)}) %collective-permute-start.32) | collective-permute-done | bytes 10272 | tf_op jit(solution)/shard_map/ppermute | solution.py:508
  756.6 25.1 %collective-permute-done.30 = bf16[448,2048]{1,0:T(8,128)(2,1)} collective-permute-done((bf16[448,2048]{1,0:T(8,128)(2,1)}, bf16[448,2048]{1,0:T(8,128)(2,1)}, u32[]{:S(2)}, u32[]{:S(2)}) %collective-permute-start.30) | collective-permute-done | bytes 1835040 | tf_op jit(solution)/shard_map/ppermute | solution.py:508
  812.3 20.7 %collective-permute-done.36 = bf16[2,2,40,160]{3,2,1,0:T(8,128)(2,1)} collective-permute-done((bf16[2,2,40,160]{3,2,1,0:T(8,128)(2,1)}, bf16[2,2,40,160]{3,2,1,0:T(8,128)(2,1)}, u32[]{:S(2)}, u32[]{:S(2)}) %collective-permute-start.36) | collective-permute-done | bytes 51232 | tf_op jit(solution)/shard_map/ppermute | solution.py:508
  862.5 14.1 %adam.8 = (f32[4,512,2,768]{3,2,1,0:T(2,128)}, bf16[512,2,768]{2,1,0:T(2,128)(2,1)}) custom-call(f32[1,1]{1,0:T(1,128)} %bitcast.41.refs_0_, f32[4,512,2,768]{3,2,1,0:T(2,128)} %refs_1_.4, f32[512,2,768]{2,1,0:T(2,128)S(1)} %reshape.287.refs_2_), custom_call_target="tpu_custom_call" | custom-call | flops 15728640 | bytes 29884416 | tf_op jit(solution)/shard_map/adam/pallas_call | solution.py:488
  (345 shorter events, 341.6 us)
Async XLA Ops:
  7.2 110.1 %all-gather.4.cloned.1.call-start = ((), (), s32[]{:S(2)}) async-start(), calls=%async_computation.3 | async-start | bytes 4915200 | tf_op jit(solution)/shard_map/all_gather | solution.py:648
  14.1 52.4 %collective-permute-start = (bf16[256,2048]{1,0:T(8,128)(2,1)}, bf16[256,2048]{1,0:T(8,128)(2,1)S(1)}, u32[]{:S(2)}, u32[]{:S(2)}) collective-permute-start(bf16[256,2048]{1,0:T(8,128)(2,1)} %slice.415), channel_id=1, source_target_pairs={{0,2},{1,3},{2,0},{3,1},{4,6},{5,7},{6,4},{7,5},{8,10},{9,11},{10,... | collective-permute-start | bytes 3145736 | tf_op jit(solution)/shard_map/ppermute | solution.py:508
  20.4 46.0 %collective-permute-start.1 = (bf16[240,2048]{1,0:T(8,128)(2,1)S(1)}, bf16[240,2048]{1,0:T(8,128)(2,1)}, u32[]{:S(2)}, u32[]{:S(2)}) collective-permute-start(bf16[240,2048]{1,0:T(8,128)(2,1)S(1)} %constant_dynamic-slice_fusion.2), channel_id=1, source_target_pairs={{0,4},{1,5},{2,6},{3,7},{4,0},{5,1},{6,2},{7,3},{8,12},{9,13},{10,... | collective-permute-start | bytes 2949128 | tf_op jit(solution)/shard_map/ppermute | solution.py:508
  66.5 205.8 %all-gather.6.cloned.1.call-start = ((), (), s32[]{:S(2)}) async-start(), calls=%async_computation.4 | async-start | bytes 7864320 | tf_op jit(solution)/shard_map/all_gather | solution.py:648
  102.2 82.1 %collective-permute-start.7 = (bf16[512,2048]{1,0:T(8,128)(2,1)}, bf16[512,2048]{1,0:T(8,128)(2,1)}, u32[]{:S(2)}, u32[]{:S(2)}) collective-permute-start(bf16[512,2048]{1,0:T(8,128)(2,1)} %param.16), channel_id=1, source_target_pairs={{0,2},{1,3},{2,0},{3,1},{4,6},{5,7},{6,4},{7,5},{8,10},{9,11},{10,... | collective-permute-start | bytes 6291464 | tf_op jit(solution)/shard_map/ppermute | solution.py:508
  105.0 77.2 %collective-permute-start.8 = (bf16[512,1536]{1,0:T(8,128)(2,1)}, bf16[512,1536]{1,0:T(8,128)(2,1)}, u32[]{:S(2)}, u32[]{:S(2)}) collective-permute-start(bf16[512,1536]{1,0:T(8,128)(2,1)} %constant_dynamic-slice_fusion.1), channel_id=1, source_target_pairs={{0,4},{1,5},{2,6},{3,7},{4,0},{5,1},{6,2},{7,3},{8,12},{9,13},{10,... | collective-permute-start | bytes 4718600 | tf_op jit(solution)/shard_map/ppermute | solution.py:508
  184.4 132.1 %all-gather.8.cloned.1.call-start = ((), (), s32[]{:S(2)}) async-start(), calls=%async_computation.5 | async-start | bytes 3932160 | tf_op jit(solution)/shard_map/all_gather | solution.py:648
  198.3 64.8 %collective-permute-start.11 = (bf16[512,2048]{1,0:T(8,128)(2,1)}, bf16[512,2048]{1,0:T(8,128)(2,1)}, u32[]{:S(2)}, u32[]{:S(2)}) collective-permute-start(bf16[512,2048]{1,0:T(8,128)(2,1)} %add_convert_fusion.7), channel_id=1, source_target_pairs={{0,2},{1,3},{2,0},{3,1},{4,6},{5,7},{6,4},{7,5},{8,10},{9,11},{10,... | collective-permute-start | bytes 6291464 | tf_op jit(solution)/shard_map/ppermute | solution.py:508
  206.9 56.3 %collective-permute-start.10 = (bf16[512,2048]{1,0:T(8,128)(2,1)}, bf16[512,2048]{1,0:T(8,128)(2,1)}, u32[]{:S(2)}, u32[]{:S(2)}) collective-permute-start(bf16[512,2048]{1,0:T(8,128)(2,1)} %slice.430), channel_id=1, source_target_pairs={{0,1},{1,0},{2,3},{3,2},{4,5},{5,4},{6,7},{7,6},{8,9},{9,8},{10,11... | collective-permute-start | bytes 6291464 | tf_op jit(solution)/shard_map/ppermute | solution.py:508
  208.1 53.8 %collective-permute-start.12 = (bf16[192,2048]{1,0:T(8,128)(2,1)S(1)}, bf16[192,2048]{1,0:T(8,128)(2,1)S(1)}, u32[]{:S(2)}, u32[]{:S(2)}) collective-permute-start(bf16[192,2048]{1,0:T(8,128)(2,1)S(1)} %constant_dynamic-slice_fusion), channel_id=1, source_target_pairs={{0,4},{1,5},{2,6},{3,7},{4,0},{5,1},{6,2},{7,3},{8,12},{9,13},{10,... | collective-permute-start | bytes 2359304 | tf_op jit(solution)/shard_map/ppermute | solution.py:508
  271.7 48.7 %collective-permute-start.16 = (bf16[512,2048]{1,0:T(8,128)(2,1)}, bf16[512,2048]{1,0:T(8,128)(2,1)}, u32[]{:S(2)}, u32[]{:S(2)}) collective-permute-start(bf16[512,2048]{1,0:T(8,128)(2,1)} %param.16), channel_id=1, source_target_pairs={{0,1},{1,0},{2,3},{3,2},{4,5},{5,4},{6,7},{7,6},{8,9},{9,8},{10,11... | collective-permute-start | bytes 6291464 | tf_op jit(solution)/shard_map/ppermute | solution.py:508
  272.2 304.7 %reduce-scatter.4.cloned.1.call-start = ((), (), s32[]{:S(2)}) async-start(), calls=%async_computation.6 | async-start | bytes 15728640 | tf_op jit(solution)/shard_map/reduce_scatter | solution.py:743
  283.4 54.7 %collective-permute-start.14 = (bf16[512,2048]{1,0:T(8,128)(2,1)}, bf16[512,2048]{1,0:T(8,128)(2,1)}, u32[]{:S(2)}, u32[]{:S(2)}) collective-permute-start(bf16[512,2048]{1,0:T(8,128)(2,1)} %multiply_convert_fusion.6), channel_id=1, source_target_pairs={{0,2},{1,3},{2,0},{3,1},{4,6},{5,7},{6,4},{7,5},{8,10},{9,11},{10,... | collective-permute-start | bytes 6291464 | tf_op jit(solution)/shard_map/ppermute | solution.py:508
  407.7 48.3 %collective-permute-start.19 = (bf16[512,2048]{1,0:T(8,128)(2,1)}, bf16[512,2048]{1,0:T(8,128)(2,1)}, u32[]{:S(2)}, u32[]{:S(2)}) collective-permute-start(bf16[512,2048]{1,0:T(8,128)(2,1)} %add_convert_fusion.6), channel_id=1, source_target_pairs={{0,2},{1,3},{2,0},{3,1},{4,6},{5,7},{6,4},{7,5},{8,10},{9,11},{10,... | collective-permute-start | bytes 6291464 | tf_op jit(solution)/shard_map/ppermute | solution.py:508
  456.0 253.7 %reduce-scatter.8.cloned.1.call-start = ((), (), s32[]{:S(2)}) async-start(), calls=%async_computation.8 | async-start | bytes 11141120 | tf_op jit(solution)/shard_map/reduce_scatter | solution.py:743
  489.0 48.5 %collective-permute-start.21 = (bf16[512,2048]{1,0:T(8,128)(2,1)}, bf16[512,2048]{1,0:T(8,128)(2,1)}, u32[]{:S(2)}, u32[]{:S(2)}) collective-permute-start(bf16[512,2048]{1,0:T(8,128)(2,1)} %get-tuple-element.193), channel_id=1, source_target_pairs={{0,2},{1,3},{2,0},{3,1},{4,6},{5,7},{6,4},{7,5},{8,10},{9,11},{10,... | collective-permute-start | bytes 6291464 | tf_op jit(solution)/shard_map/ppermute | solution.py:508
  490.5 45.2 %collective-permute-start.22 = (bf16[512,2048]{1,0:T(8,128)(2,1)}, bf16[512,2048]{1,0:T(8,128)(2,1)}, u32[]{:S(2)}, u32[]{:S(2)}) collective-permute-start(bf16[512,2048]{1,0:T(8,128)(2,1)} %get-tuple-element.193), channel_id=1, source_target_pairs={{0,1},{1,0},{2,3},{3,2},{4,5},{5,4},{6,7},{7,6},{8,9},{9,8},{10,11... | collective-permute-start | bytes 6291464 | tf_op jit(solution)/shard_map/ppermute | solution.py:508
  552.8 240.8 %reduce-scatter.6.cloned.1.call-start = ((), (), s32[]{:S(2)}) async-start(), calls=%async_computation.7 | async-start | bytes 7372800 | tf_op jit(solution)/shard_map/reduce_scatter | solution.py:743
  561.1 81.3 %collective-permute-start.25 = (bf16[512,2048]{1,0:T(8,128)(2,1)}, bf16[512,2048]{1,0:T(8,128)(2,1)}, u32[]{:S(2)}, u32[]{:S(2)}) collective-permute-start(bf16[512,2048]{1,0:T(8,128)(2,1)} %add_convert_fusion.4), channel_id=1, source_target_pairs={{0,2},{1,3},{2,0},{3,1},{4,6},{5,7},{6,4},{7,5},{8,10},{9,11},{10,... | collective-permute-start | bytes 6291464 | tf_op jit(solution)/shard_map/ppermute | solution.py:508
  581.4 71.1 %collective-permute-start.26 = (bf16[512,1536]{1,0:T(8,128)(2,1)}, bf16[512,1536]{1,0:T(8,128)(2,1)}, u32[]{:S(2)}, u32[]{:S(2)}) collective-permute-start(bf16[512,1536]{1,0:T(8,128)(2,1)} %pad_maximum_fusion.7), channel_id=1, source_target_pairs={{0,4},{1,5},{2,6},{3,7},{4,0},{5,1},{6,2},{7,3},{8,12},{9,13},{10,... | collective-permute-start | bytes 4718600 | tf_op jit(solution)/shard_map/ppermute | solution.py:508
  709.7 72.1 %collective-permute-start.29 = (bf16[512,2048]{1,0:T(8,128)(2,1)}, bf16[512,2048]{1,0:T(8,128)(2,1)}, u32[]{:S(2)}, u32[]{:S(2)}) collective-permute-start(bf16[512,2048]{1,0:T(8,128)(2,1)} %slice.458), channel_id=1, source_target_pairs={{0,1},{1,0},{2,3},{3,2},{4,5},{5,4},{6,7},{7,6},{8,9},{9,8},{10,11... | collective-permute-start | bytes 6291464 | tf_op jit(solution)/shard_map/ppermute | solution.py:508
  714.9 66.9 %collective-permute-start.30 = (bf16[448,2048]{1,0:T(8,128)(2,1)}, bf16[448,2048]{1,0:T(8,128)(2,1)}, u32[]{:S(2)}, u32[]{:S(2)}) collective-permute-start(bf16[448,2048]{1,0:T(8,128)(2,1)} %slice.459), channel_id=1, source_target_pairs={{0,2},{1,3},{2,0},{3,1},{4,6},{5,7},{6,4},{7,5},{8,10},{9,11},{10,... | collective-permute-start | bytes 5505032 | tf_op jit(solution)/shard_map/ppermute | solution.py:508
  718.9 74.7 %collective-permute-start.33 = (bf16[512,768]{0,1:T(8,128)(2,1)}, bf16[512,768]{0,1:T(8,128)(2,1)}, u32[]{:S(2)}, u32[]{:S(2)}) collective-permute-start(bf16[512,768]{0,1:T(8,128)(2,1)} %slice.391), channel_id=1, source_target_pairs={{0,4},{1,5},{2,6},{3,7},{4,0},{5,1},{6,2},{7,3},{8,12},{9,13},{10,... | collective-permute-start | bytes 2359304 | tf_op jit(solution)/shard_map/ppermute | solution.py:508
  719.0 74.6 %collective-permute-start.34 = (bf16[512,320]{0,1:T(8,128)(2,1)}, bf16[512,320]{0,1:T(8,128)(2,1)}, u32[]{:S(2)}, u32[]{:S(2)}) collective-permute-start(bf16[512,320]{0,1:T(8,128)(2,1)} %slice.392), channel_id=1, source_target_pairs={{0,4},{1,5},{2,6},{3,7},{4,0},{5,1},{6,2},{7,3},{8,12},{9,13},{10,... | collective-permute-start | bytes 983048 | tf_op jit(solution)/shard_map/ppermute | solution.py:508
  (82 other events, 1496.1 us)
Sparse Core Ops, SparseCore 0:
  66.6 50.6 all-gather.3
  184.5 70.2 all-gather.5
  272.4 44.0 all-gather.7
  456.2 120.7 reduce-scatter.3
  579.9 90.6 reduce-scatter.7
  674.9 66.8 reduce-scatter.5
